TPU v7x, 512 devices: a whole 4x8x8 slice. The times are simulated.
512 devices in a mesh: elem: 128 (over y, z, core), sub: 4 (over x).
Axes of the slice: x: 4, y: 8, z: 8, core: 2. Of those that a mesh axis runs over, the one named last changes fastest.
Arguments:
- velocity: float32 [2, 8, 512, 128, 128], P(None, None, ('elem', 'sub')), may hold values from -12 to 12
- thickness: float32 [8, 512, 128, 128], P(None, ('elem', 'sub')), may hold values from 0.5 to 1.5
- coriolis: float32 [512, 128, 128], P(('elem', 'sub')), may hold values from 4 to 16
- elem_mass: float32 [512, 32, 32], P(('elem', 'sub')), may hold values from 0.25 to 4
- block_owner: int32 [4, 128], replicated, may hold values from 0 to 511, as said below
Outputs:
- new_velocity: float32 [2, 8, 512, 128, 128], P(None, None, ('elem', 'sub'))
- new_thickness: float32 [8, 512, 128, 128], P(None, ('elem', 'sub'))
Inputs may be any that keep to these rules, and one draw needn't show every extreme that they name: `block_owner`: every block index appears once. Each aligned run of 16 block indices (a square run s) fills a 4 x 4 square of blocks whose first column is a multiple of 4, in an order along which successive indices share an edge; the square of run s + 1 lies directly right of that of run s (columns wrap around). Each aligned run of 4 indices (one index of elem) fills a 2 x 2 square whose first row and column are even.
All inputs are finite; a program needn't handle non-finite values.
Results may differ from a plain program's by a relative error of at most 0.0003.
Values sent between devices are 32-bit elements; how exact they have to be, the bound alone decides.
No kernel may reach another device: no remote copies, remote signals or barrier semaphores. Data moves between devices by JAX's collectives and lax.ppermute only.
A program may use at most 64 MiB of HBM per device.

v0:
```python
import functools
import math

import jax
import jax.numpy as jnp
import numpy as np
from jax import lax
from jax.experimental import pallas as pl
from jax.experimental.pallas import tpu as pltpu
from jax.sharding import PartitionSpec as P

courant = 0.1
hyper_coef = 0.002
axes = ("elem", "sub")
f32 = jnp.float32
HIGH = lax.Precision.HIGHEST
RIGHT, LEFT, UPPER, LOWER = range(4)
steps8 = ((0, 1), (0, -1), (1, 0), (-1, 0), (1, 1), (1, -1), (-1, 1), (-1, -1))


def gll_tables():
    points = [-1.0, -1.0 / math.sqrt(5.0), 1.0 / math.sqrt(5.0), 1.0]
    weights = np.array([1.0 / 6.0, 5.0 / 6.0, 5.0 / 6.0, 1.0 / 6.0])
    spread = [
        math.prod([points[target] - points[others] for others in range(4) if others != target])
        for target in range(4)
    ]
    derivative = np.zeros((4, 4))
    for target in range(4):
        for source in range(4):
            if target == source:
                derivative[target, source] = sum(
                    1.0 / (points[target] - points[others]) for others in range(4) if others != target
                )
            else:
                derivative[target, source] = spread[target] / (
                    spread[source] * (points[target] - points[source])
                )
    return weights, 2.0 * derivative


WEIGHTS, FIRST = gll_tables()
SECOND = FIRST @ FIRST
CENTRE = float(SECOND[0, 0])


def offset_rows(table):
    rows = np.zeros((7, 4))
    for shift in range(-3, 4):
        for target in range(4):
            if 0 <= target + shift < 4:
                rows[shift + 3, target] = table[target, target + shift]
    return rows


def constant_tables():
    along_x = np.stack([np.kron(np.eye(32), FIRST.T), np.kron(np.eye(32), SECOND.T)])
    expand = np.kron(np.eye(32), WEIGHTS[:, None])
    tiles = np.zeros((27, 8, 128))
    for base, table in ((0, FIRST), (7, SECOND)):
        tiles[base : base + 7] = np.tile(offset_rows(table), (1, 2))[:, :, None]
    tiles[14:21] = np.tile(offset_rows(SECOND), (1, 32))[:, None, :]
    arm_low = np.array([0.0, SECOND[0, 1], SECOND[0, 2], SECOND[0, 3]])
    arm_high = np.array([SECOND[3, 0], SECOND[3, 1], SECOND[3, 2], 0.0])
    tiles[21] = np.tile(arm_low, 32)[None]
    tiles[22] = np.tile(arm_high, 32)[None]
    high = np.array([-hyper_coef * WEIGHTS[a] / WEIGHTS[3] * SECOND[a, 3] for a in range(4)])
    low = np.array([-hyper_coef * WEIGHTS[a] / WEIGHTS[0] * SECOND[a, 0] for a in range(4)])
    tiles[23] = np.concatenate([[0.0, 0.0, 0.0, high[0]], high])[:, None]
    tiles[24] = np.concatenate([low, [low[3], 0.0, 0.0, 0.0]])[:, None]
    across = np.zeros(128)
    across[:5] = [*low, low[3]]
    across[123:] = [high[0], *high]
    tiles[25] = across[None]
    ends = np.zeros(128)
    ends[0] = ends[127] = 1.0
    tiles[26] = ends[None]
    return (
        jnp.asarray(along_x, f32),
        jnp.asarray(expand, f32),
        jnp.asarray(expand.T, f32),
        jnp.asarray(tiles, f32),
    )


def lane_index(rows):
    return lax.broadcasted_iota(jnp.int32, (rows, 128), 1)


def turn(values, steps, axis=1):
    steps = steps % values.shape[axis]
    return values if steps == 0 else pltpu.roll(values, steps, axis)


def share_lanes(values):
    lane = lane_index(values.shape[0])
    first = (lane % 4 == 0) & (lane > 0)
    last = (lane % 4 == 3) & (lane < 127)
    return values + jnp.where(first, turn(values, 1), jnp.where(last, turn(values, 127), 0.0))


def share_rows(values):
    row = lax.broadcasted_iota(jnp.int32, values.shape, 0)
    first = (row % 4 == 0) & (row > 0)
    last = (row % 4 == 3) & (row < 127)
    return values + jnp.where(
        first, turn(values, 1, 0), jnp.where(last, turn(values, 127, 0), 0.0)
    )


def share_block(values):
    return share_rows(share_lanes(values))


def along_rows(values, tiles_ref, base):
    grouped = values.reshape(16, 8, 128)
    total = grouped * tiles_ref[base + 3][None]
    for shift in (-3, -2, -1, 1, 2, 3):
        total = total + pltpu.roll(grouped, (-shift) % 8, 1) * tiles_ref[base + 3 + shift][None]
    return total.reshape(128, 128)


def second_lanes(values, tiles_ref):
    total = values * tiles_ref[17, 0:1]
    for shift in (-3, -2, -1, 1, 2, 3):
        total = total + turn(values, -shift) * tiles_ref[17 + shift, 0:1]
    return total


def pack_end(lines, at_high):
    lane = lane_index(8)
    start = 124 if at_high else 0
    packed = jnp.zeros((8, 128), f32)
    for part in range(3):
        moved = turn(lines[8 * part : 8 * part + 8], 4 * part - start)
        packed = jnp.where(lane // 4 == part, moved, packed)
    return packed


def pack_mass(line, at_high):
    lane = lane_index(8)
    start = 124 if at_high else 0
    wide = jnp.broadcast_to(line, (8, 128))
    packed = jnp.zeros((8, 128), f32)
    for part in range(3):
        packed = jnp.where(lane // 4 == 6 + part, turn(wide, 24 + 4 * part - start), packed)
    return packed


def fold_line(line):
    lane = lane_index(8)
    row = lax.broadcasted_iota(jnp.int32, (8, 128), 0)
    wide = jnp.broadcast_to(line, (8, 128))
    folded = jnp.zeros((8, 128), f32)
    for part in range(4):
        folded = jnp.where((row == part) & (lane // 32 == 2), turn(wide, 64 - 32 * part), folded)
    return folded


def unfold_line(tile):
    lane = lane_index(1)
    line = jnp.zeros((1, 128), f32)
    for part in range(4):
        line = jnp.where(lane // 32 == part, turn(tile[part : part + 1], 32 * part - 64), line)
    return line


def find_tables(device, owner_ref, table_ref, cols_b):
    square = device // 16
    squares = cols_b // 4
    place = jnp.zeros((48, 128), f32)
    index = lax.broadcasted_iota(jnp.int32, (48, 1), 0)
    wanted = ((square + index // 16 + squares - 1) % squares) * 16 + index % 16
    lane = lane_index(1)
    own = jnp.zeros((1, 128), f32)
    for row in range(4):
        line = owner_ref[row : row + 1, :]
        code = (128 * row + lane).astype(f32)
        place = place + jnp.where(line == wanted, code, 0.0)
        own = own + jnp.where(line == device, code, 0.0)
    place = jnp.sum(place, axis=1, keepdims=True).astype(jnp.int32)
    own = jnp.sum(own, axis=1, keepdims=True).astype(jnp.int32)
    own_row, own_col = own // 128, own % 128
    rows, cols = place // 128, place % 128
    member = device % 16
    here_rows, here_cols = rows[16:32], cols[16:32]
    down, over = here_rows - own_row, here_cols - own_col
    inside = jnp.full((16, 1), 8, jnp.int32)
    for number, (step_y, step_x) in enumerate(steps8):
        inside = jnp.where((down == step_y) & (over == step_x), number, inside)
    table_ref[0:16, :] = jnp.broadcast_to(inside, (16, 128))
    crossing = jnp.full((16, 1), 6, jnp.int32)
    sixteen = lax.broadcasted_iota(jnp.int32, (16, 1), 0)
    for side, start, step_x in ((0, 32, 1), (1, 0, -1)):
        picked = sixteen == member
        their = jnp.sum(
            jnp.where(picked, place[start : start + 16], 0).astype(f32), axis=0, keepdims=True
        ).astype(jnp.int32)
        their_row, their_col = their // 128, their % 128
        beside = their_col == (here_cols + step_x + cols_b) % cols_b
        for number, step_y in enumerate((0, 1, -1)):
            crossing = jnp.where(
                beside & (here_rows - their_row == step_y), 3 * side + number, crossing
            )
    table_ref[16:32, :] = jnp.broadcast_to(crossing, (16, 128))
    way = lax.broadcasted_iota(jnp.int32, (8, 1), 0)
    step_y = jnp.zeros((8, 1), jnp.int32)
    step_x = jnp.zeros((8, 1), jnp.int32)
    for number, (along_y, along_x) in enumerate(steps8):
        step_y = jnp.where(way == number, along_y, step_y)
        step_x = jnp.where(way == number, along_x, step_x)
    near_row = own_row + step_y
    near_col = (own_col + step_x + cols_b) % cols_b
    found = jnp.zeros((8, 128), f32)
    for row in range(4):
        line = owner_ref[row : row + 1, :].astype(f32)
        found = found + jnp.where((near_row == row) & (near_col == lane), line, 0.0)
    found = jnp.sum(found, axis=1, keepdims=True).astype(jnp.int32)
    there = (near_row >= 0) & (near_row < 4)
    slot = 2 * (found % 16) + jnp.where(found // 16 == square, 0, 1)
    table_ref[32:40, :] = jnp.broadcast_to(slot, (8, 128))
    table_ref[40:48, :] = jnp.broadcast_to(there.astype(jnp.int32), (8, 128))


def first_kernel(
    cols_b, device_ref, owner_ref, velocity_ref, height_ref, coriolis_ref, elem_mass_ref,
    along_x_ref, expand_ref, expand_t_ref, tiles_ref,
    partial_ref, side_ref, upright_ref, mass_ref, table_ref, top_ref,
    node_mass, inner_inverse, columns, turned, upper_lower,
):
    level = pl.program_id(0)
    lane = lane_index(128)

    @pl.when(level == 0)
    def _():
        rows = jnp.dot(
            expand_ref[...], elem_mass_ref[0], precision=HIGH, preferred_element_type=f32
        )
        mass = jnp.dot(rows, expand_t_ref[...], precision=HIGH, preferred_element_type=f32)
        node_mass[...] = mass
        local_mass = share_block(mass)
        mass_ref[...] = local_mass
        row = lax.broadcasted_iota(jnp.int32, (128, 128), 0)
        inner = (row > 0) & (row < 127) & (lane > 0) & (lane < 127)
        inner_inverse[...] = jnp.where(inner, 1.0 / local_mass, 0.0)
        columns[...] = jnp.where(lane // 2 == 48, turn(mass, 97), 0.0)
        find_tables(device_ref[0], owner_ref, table_ref, cols_b)
        top_ref[...] = jnp.zeros_like(top_ref)

    mass = node_mass[...]
    east = velocity_ref[0, 0]
    north = velocity_ref[1, 0]
    height = height_ref[0]
    squared = east * east + north * north
    energy = 0.5 * squared + height
    speed = jnp.max(jnp.sqrt(squared) + jnp.sqrt(height))
    top_ref[...] = jnp.maximum(top_ref[...], speed)
    flux_x, flux_y = height * east, height * north
    first_x = jnp.dot(
        jnp.concatenate([north, energy, flux_x], 0), along_x_ref[0],
        precision=HIGH, preferred_element_type=f32,
    )
    second_x = jnp.dot(
        jnp.concatenate([east, north, height], 0), along_x_ref[1],
        precision=HIGH, preferred_element_type=f32,
    )
    absolute = first_x[:128] - along_rows(east, tiles_ref, 0) + coriolis_ref[0]
    tendencies = (
        absolute * north - first_x[128:256],
        -absolute * east - along_rows(energy, tiles_ref, 0),
        -(first_x[256:] + along_rows(flux_y, tiles_ref, 0)),
    )
    smoothed = []
    for part, values in enumerate((east, north, height)):
        lap = second_x[128 * part : 128 * part + 128] + along_rows(values, tiles_ref, 7)
        local = share_block(lap * mass)
        place = 8 * part + level
        upper_lower[0, pl.ds(place, 1), :] = local[127:128]
        upper_lower[1, pl.ds(place, 1), :] = local[0:1]
        columns[...] = jnp.where(
            lane // 2 == place, pltpu.roll(local, 2 * place + 1, 1), columns[...]
        )
        smoothed.append(local * inner_inverse[...])
    second_x = jnp.dot(
        jnp.concatenate(smoothed, 0), along_x_ref[1], precision=HIGH, preferred_element_type=f32
    )
    for part in range(3):
        lap = second_x[128 * part : 128 * part + 128] + along_rows(smoothed[part], tiles_ref, 7)
        local = share_block((tendencies[part] - hyper_coef * lap) * mass)
        partial_ref[part, 0] = local
        place = 24 + 8 * part + level
        upper_lower[0, pl.ds(place, 1), :] = local[127:128]
        upper_lower[1, pl.ds(place, 1), :] = local[0:1]
        columns[...] = jnp.where(
            lane // 2 == place, pltpu.roll(local, 2 * place + 1, 1), columns[...]
        )

    @pl.when(level == 7)
    def _():
        turned[...] = jnp.transpose(columns[...])
        for place in range(48):
            side_ref[0, place : place + 1, :] = turned[2 * place : 2 * place + 1, :]
            side_ref[1, place : place + 1, :] = turned[2 * place + 1 : 2 * place + 2, :]
        mass_lines = (
            turned[96:97, :], turned[97:98, :], node_mass[127:128, :], node_mass[0:1, :],
        )
        smooth_lines = (
            side_ref[0, 0:24, :], side_ref[1, 0:24, :], upper_lower[0, 0:24, :], upper_lower[1, 0:24, :],
        )
        change_lines = {
            UPPER: upper_lower[0, 24:48, :], LOWER: upper_lower[1, 24:48, :],
        }
        ends = {}
        for side in range(4):
            local_mass = share_lanes(mass_lines[side])
            for high in (False, True):
                ends[side, high] = pack_end(smooth_lines[side], high) + pack_mass(local_mass, high)
        upright_ref[0, 0:48, :] = upper_lower[0, 0:48, :]
        upright_ref[1, 0:48, :] = upper_lower[1, 0:48, :]
        extras = (
            ends[UPPER, True] + turn(ends[LOWER, True], 12),
            ends[UPPER, False] + turn(ends[LOWER, False], 12),
            ends[LEFT, True] + turn(ends[RIGHT, True], 12),
            ends[LEFT, False] + turn(ends[RIGHT, False], 12),
        )
        for side in range(4):
            tile = extras[side] + fold_line(mass_lines[side])
            if side < 2:
                side_ref[side, 48:56, :] = tile
            else:
                upright_ref[side - 2, 48:56, :] = tile
        for across, sideways in ((RIGHT, True), (LEFT, False)):
            for number, (along, upward) in enumerate(((UPPER, True), (LOWER, False))):
                tile = ends[along, sideways] + turn(ends[across, upward], 12)
                tile = tile + turn(pack_end(change_lines[along], sideways), 48)
                side_ref[across, 56 + 8 * number : 64 + 8 * number, :] = tile


def pack_kernel(table_ref, side_ref, upright_ref, ahead_ref, behind_ref, tops_ref, send_ref):
    lane = lane_index(8)
    top = jnp.max(tops_ref[...])
    for place in range(16):
        message = table_ref[place, 0]

        @pl.when(message < 2)
        def _():
            send_ref[2 * place] = side_ref[jnp.minimum(message, 1), 0:56, :]

        @pl.when((message >= 2) & (message < 4))
        def _():
            send_ref[2 * place] = upright_ref[jnp.clip(message - 2, 0, 1)]

        for corner, (side, row) in enumerate(((0, 56), (1, 56), (0, 64), (1, 64))):

            @pl.when(message == 4 + corner)
            def _(side=side, row=row):
                send_ref[2 * place, 48:56, :] = side_ref[side, row : row + 8, :]

        send_ref[2 * place, 48:56, :] = jnp.where(lane >= 96, top, send_ref[2 * place, 48:56, :])
        crossing = table_ref[16 + place, 0]
        for base, ref in ((0, ahead_ref), (3, behind_ref)):

            @pl.when(crossing == base)
            def _(ref=ref):
                send_ref[2 * place + 1] = ref[0:56, :]

            @pl.when(crossing == base + 1)
            def _(ref=ref):
                send_ref[2 * place + 1, 48:56, :] = ref[56:64, :]

            @pl.when(crossing == base + 2)
            def _(ref=ref):
                send_ref[2 * place + 1, 48:56, :] = ref[64:72, :]


def edge_terms(table_ref, side_ref, upright_ref, received_ref, tiles_ref):
    lane = lane_index(1)

    def message(way, start, stop):
        values = received_ref[table_ref[32 + way, 0], start:stop, :]
        return jnp.where(table_ref[40 + way, 0] > 0, values, 0.0)

    own = (
        side_ref[0, 0:24, :], side_ref[1, 0:24, :], upright_ref[0, 0:24, :], upright_ref[1, 0:24, :],
    )
    own_mass = (
        unfold_line(side_ref[0, 48:56, :]), unfold_line(side_ref[1, 48:56, :]),
        unfold_line(upright_ref[0, 48:56, :]), unfold_line(upright_ref[1, 48:56, :]),
    )
    near = [message(side, 0, 24) for side in range(4)]
    change = [message(side, 24, 48) for side in range(4)]
    extra = [message(side, 48, 56) for side in range(4)]
    mass = [unfold_line(extra[side]) for side in range(4)]
    shared_mass = [share_lanes(mass[side]) for side in range(4)]
    total = [own[side] + near[side] for side in range(4)]
    total_mass = [share_lanes(own_mass[side]) + shared_mass[side] for side in range(4)]
    corners = []
    for along in (UPPER, LOWER):
        for across in (RIGHT, LEFT):
            corner = 4 + 2 * (along - UPPER) + across
            at_x = 127 if across == RIGHT else 0
            at_y = 127 if along == UPPER else 0
            tile = message(corner, 48, 56)
            end_x = 0 if across == RIGHT else 3

            def spread_out(packed, start, at_x=at_x):
                return jnp.concatenate(
                    [turn(packed, at_x - start - 4 * part) for part in range(3)], 0
                )

            far = spread_out(tile, end_x)
            far_mass = turn(tile, at_x - 24 - end_x)[0:1]
            corners.append((along, across, at_x, at_y, tile, far_mass, spread_out))
            on_x, on_y = lane == at_x, lane == at_y
            total[along] = total[along] + jnp.where(
                on_x, turn(near[across], at_x - at_y) + far, 0.0
            )
            total_mass[along] = total_mass[along] + jnp.where(
                on_x, turn(mass[across], at_x - at_y) + far_mass, 0.0
            )
            total[across] = total[across] + jnp.where(
                on_y, turn(near[along] + far, at_y - at_x), 0.0
            )
            total_mass[across] = total_mass[across] + jnp.where(
                on_y, turn(mass[along] + far_mass, at_y - at_x), 0.0
            )
    smooth = [total[side] / total_mass[side] for side in range(4)]
    curve = [second_lanes(smooth[side], tiles_ref) for side in range(4)]
    added = [
        change[side]
        - hyper_coef
        * (shared_mass[side] * CENTRE * smooth[side] + share_lanes(mass[side] * curve[side]))
        for side in range(4)
    ]

    def arm(beside, diagonal, coefs):
        both = beside + diagonal
        weight = turn(both, -24)
        value = jnp.where(weight > 0.0, both / jnp.where(weight > 0.0, weight, 1.0), 0.0) * coefs
        value = value + turn(value, -1)
        return value + turn(value, -2)

    for along, across, at_x, at_y, tile, far_mass, spread_out in corners:
        beside = extra[across] if along == UPPER else turn(extra[across], -12)
        arm_x = spread_out(arm(beside, tile, tiles_ref[21 if across == RIGHT else 22]), 0)
        beside = extra[along] if across == LEFT else turn(extra[along], -12)
        arm_y = spread_out(
            arm(beside, turn(tile, -12), tiles_ref[21 if along == UPPER else 22]), 0
        )
        middle = CENTRE * smooth[along]
        arm_x, arm_y = arm_x + middle, arm_y + middle
        own_x = curve[along]
        own_y = turn(curve[across], at_x - at_y)
        mass_x = turn(mass[across], at_x - at_y)
        end_x = 0 if across == RIGHT else 3
        value = (
            turn(change[across], at_x - at_y) + change[along] + spread_out(tile, 48 + end_x)
        ) - hyper_coef * (
            mass_x * (arm_x + own_y) + mass[along] * (own_x + arm_y) + far_mass * (arm_x + arm_y)
        )
        added[along] = jnp.where(lane == at_x, value, added[along])
    ends = (lane == 0) | (lane == 127)
    plain, edge = [], []
    for side in range(4):
        line = smooth[side] if side >= UPPER else jnp.where(ends, 0.0, smooth[side])
        outside = added[side] if side >= UPPER else jnp.where(ends, 0.0, added[side])
        bend = curve[side] if side >= UPPER else second_lanes(line, tiles_ref)
        plain.append(share_lanes(own_mass[side] * line))
        edge.append(outside - hyper_coef * share_lanes(own_mass[side] * bend))
    return plain, edge, total_mass


def last_kernel(
    table_ref, side_ref, upright_ref, received_ref, tiles_ref, mass_ref,
    velocity_ref, height_ref, partial_ref, new_velocity_ref, new_height_ref,
    rows, columns, inverse,
):
    level = pl.program_id(0)
    lane = lane_index(128)

    @pl.when(level == 0)
    def _():
        plain, edge, total_mass = edge_terms(
            table_ref, side_ref, upright_ref, received_ref, tiles_ref
        )
        rows[0] = plain[UPPER]
        rows[1] = plain[LOWER]
        rows[2] = edge[UPPER]
        rows[3] = edge[LOWER]
        stacked = jnp.concatenate(
            [plain[LEFT], plain[RIGHT], edge[LEFT], edge[RIGHT]]
            + [jnp.broadcast_to(total_mass[side], (16, 128)) for side in (LEFT, RIGHT)],
            0,
        )
        columns[...] = jnp.transpose(stacked)
        sides = columns[...]
        mass = mass_ref[...]
        mass = jnp.where(lane == 0, sides[:, 96:97], mass)
        mass = jnp.where(lane == 127, sides[:, 112:113], mass)
        row = lax.broadcasted_iota(jnp.int32, (128, 128), 0)
        mass = jnp.where(row == 127, total_mass[UPPER], mass)
        mass = jnp.where(row == 0, total_mass[LOWER], mass)
        top = jnp.zeros((8, 128), f32)
        for place in range(16):
            top = jnp.maximum(top, received_ref[2 * place, 48:56, :])
        top = jnp.max(jnp.where(lane_index(8) >= 96, top, 0.0))
        inverse[...] = (courant / top) / mass

    moved = pltpu.roll(columns[...], (128 - level) % 128, 1)
    factor = inverse[...]
    left = lane < 64
    across = tiles_ref[25, 0:1]
    ends = tiles_ref[26, 0:1]
    for part in range(3):
        start = 8 * part
        plain = jnp.where(left, moved[:, start : start + 1], moved[:, start + 24 : start + 25])
        edge = jnp.where(left, moved[:, start + 48 : start + 49], moved[:, start + 72 : start + 73])
        value = partial_ref[part, 0] + across * plain + ends * edge
        place = pl.ds(start + level, 1)
        upper = tiles_ref[23] * rows[0, place, :]
        lower = tiles_ref[24] * rows[1, place, :]
        row = lax.broadcasted_iota(jnp.int32, (8, 128), 0)
        upper = upper + jnp.where(row == 7, rows[2, place, :], 0.0)
        lower = lower + jnp.where(row == 0, rows[3, place, :], 0.0)
        value = jnp.concatenate([value[:8] + lower, value[8:120], value[120:] + upper], 0)
        if part < 2:
            new_velocity_ref[part, 0] = velocity_ref[part, 0] + factor * value
        else:
            new_height_ref[0] = height_ref[0] + factor * value


def whole(shape, space=None):
    if space is None:
        return pl.BlockSpec(shape, lambda level: (0,) * len(shape))
    return pl.BlockSpec(memory_space=space)


def per_device(velocity, thickness, coriolis, elem_mass, block_owner):
    cols_b = block_owner.shape[1]
    count = 4 * cols_b
    velocity = velocity[:, :, 0]
    thickness = thickness[:, 0]
    along_x, expand, expand_t, tiles = constant_tables()
    device = (lax.axis_index("elem") * lax.axis_size("sub") + lax.axis_index("sub")).reshape(1)
    if cols_b < 128:
        block_owner = jnp.pad(block_owner, ((0, 0), (0, 128 - cols_b)), constant_values=-1)
    pair = pl.BlockSpec((2, 1, 128, 128), lambda level: (0, level, 0, 0))
    single = pl.BlockSpec((1, 128, 128), lambda level: (level, 0, 0))
    triple = pl.BlockSpec((3, 1, 128, 128), lambda level: (0, level, 0, 0))
    shape = jax.ShapeDtypeStruct
    params = pltpu.CompilerParams(
        dimension_semantics=("arbitrary",), vmem_limit_bytes=32 * 1024 * 1024
    )
    partial, side, upright, local_mass, table, top = pl.pallas_call(
        functools.partial(first_kernel, cols_b),
        grid=(8,),
        in_specs=[
            whole((1,), pltpu.SMEM), whole((4, 128)), pair, single, whole((1, 128, 128)),
            whole((1, 32, 32)), whole((2, 128, 128)), whole((128, 32)), whole((32, 128)),
            whole((27, 8, 128)),
        ],
        out_specs=[
            triple, whole((2, 72, 128)), whole((2, 56, 128)), whole((128, 128)), whole((48, 128)),
            whole((32, 128)),
        ],
        out_shape=[
            shape((3, 8, 128, 128), f32), shape((2, 72, 128), f32), shape((2, 56, 128), f32),
            shape((128, 128), f32), shape((48, 128), jnp.int32), shape((32, 128), f32),
        ],
        scratch_shapes=[
            pltpu.VMEM((128, 128), f32), pltpu.VMEM((128, 128), f32), pltpu.VMEM((128, 128), f32),
            pltpu.VMEM((128, 128), f32), pltpu.VMEM((2, 48, 128), f32),
        ],
        compiler_params=params,
        name="first",
    )(device, block_owner, velocity, thickness, coriolis, elem_mass, along_x, expand, expand_t, tiles)
    squares = count // 16
    same_place = [[16 * s + i for s in range(squares)] for i in range(16)]
    same_square = [[16 * s + i for i in range(16)] for s in range(squares)]
    tops = lax.all_to_all(
        top[:squares], axes, 0, 0, axis_index_groups=same_place, tiled=True
    )
    ahead = lax.ppermute(side[1], axes, [(b, (b - 16) % count) for b in range(count)])
    behind = lax.ppermute(side[0], axes, [(b, (b + 16) % count) for b in range(count)])
    send = pl.pallas_call(
        pack_kernel,
        in_specs=[whole((48, 128), pltpu.SMEM)] + [pl.BlockSpec(memory_space=pltpu.VMEM)] * 5,
        out_specs=pl.BlockSpec(memory_space=pltpu.VMEM),
        out_shape=shape((32, 56, 128), f32),
        compiler_params=pltpu.CompilerParams(vmem_limit_bytes=32 * 1024 * 1024),
        name="pack",
    )(table, side, upright, ahead, behind, tops)
    received = lax.all_to_all(
        send.reshape(16, 112, 128), axes, 0, 0, axis_index_groups=same_square, tiled=True
    ).reshape(32, 56, 128)
    new_velocity, new_thickness = pl.pallas_call(
        last_kernel,
        grid=(8,),
        in_specs=[
            whole((48, 128), pltpu.SMEM), whole((2, 72, 128)), whole((2, 56, 128)),
            whole((32, 56, 128)), whole((27, 8, 128)), whole((128, 128)), pair, single, triple,
        ],
        out_specs=[pair, single],
        out_shape=[shape((2, 8, 128, 128), f32), shape((8, 128, 128), f32)],
        scratch_shapes=[
            pltpu.VMEM((4, 24, 128), f32), pltpu.VMEM((128, 128), f32), pltpu.VMEM((128, 128), f32),
        ],
        compiler_params=params,
        name="last",
    )(table, side, upright, received, tiles, local_mass, velocity, thickness, partial)
    return new_velocity[:, :, None], new_thickness[:, None]


def solution(mesh):
    return jax.shard_map(
        per_device,
        mesh=mesh,
        in_specs=(
            P(None, None, axes, None, None),
            P(None, axes, None, None),
            P(axes, None, None),
            P(axes, None, None),
            P(),
        ),
        out_specs=(
            P(None, None, axes, None, None),
            P(None, axes, None, None),
        ),
        check_vma=False,
    )
```

profile of v0, /device:TPU:1, one launch (start us, length us, event | category | flops | bytes accessed | tf_op | source)
XLA Modules:
  0.0 87.3 jit_solution(12066557341643547035)
XLA Ops:
  0.6 0.0 copy-start
  0.6 1.2 %copy-done = f32[2,8,1,128,128]{4,3,2,1,0:T(8,128)S(1)} copy-done((f32[2,8,1,128,128]{4,3,2,1,0:T(8,128)S(1)}, f32[2,8,1,128,128]{4,3,2,1,0:T(8,128)}, u32[]{:S(2)}) %copy-start) | copy-done | bytes 1048600
  1.9 0.0 copy-start.2
  1.9 1.0 %copy-done.2 = f32[8,1,128,128]{3,2,1,0:T(8,128)S(1)} copy-done((f32[8,1,128,128]{3,2,1,0:T(8,128)S(1)}, f32[8,1,128,128]{3,2,1,0:T(8,128)}, u32[]{:S(2)}) %copy-start.2) | copy-done | bytes 524312
  2.9 0.9 %copy-done.4 = f32[27,8,128]{2,1,0:T(8,128)S(1)} copy-done((f32[27,8,128]{2,1,0:T(8,128)S(1)}, f32[27,8,128]{2,1,0:T(8,128)}, u32[]{:S(2)}) %copy-start.4) | copy-done | bytes 110616
  3.8 0.9 %copy-done.5 = f32[2,128,128]{2,1,0:T(8,128)S(1)} copy-done((f32[2,128,128]{2,1,0:T(8,128)S(1)}, f32[2,128,128]{2,1,0:T(8,128)}, u32[]{:S(2)}) %copy-start.5) | copy-done | bytes 131096
  4.7 0.8 copy-done.6
  5.6 0.8 copy-done.7
  6.4 0.7 copy-done.8
  7.1 0.7 copy-done.9
  7.8 0.7 copy-done.10
  8.5 12.4 %first.1 = (f32[3,8,128,128]{3,2,1,0:T(8,128)S(1)}, f32[2,72,128]{2,1,0:T(8,128)S(1)}, f32[2,56,128]{2,1,0:T(8,128)S(1)}, f32[128,128]{1,0:T(8,128)S(1)}, s32[48,128]{1,0:T(8,128)S(1)}, /*index=5*/f32[32,128]{1,0:T(8,128)S(1)}) custom-call(s32[1]{0:T(128)} %bitcast.device_ref, s32[4,128]{1,0:T(4,128)S(1)} %copy-done.10, f32[2,8,128,128]{3,2,1,0:T(8,128)S(1)} %bitcast.19, ...), custom_call_target="tpu_custom_call" | custom-call | tf_op jit(solution)/shard_map/first/pallas_call | solution.py:554
  20.9 0.0 copy-start.1
  20.9 0.0 copy-start.3
  20.9 6.8 %collective-permute-start.1 = (f32[72,128]{1,0:T(8,128)S(1)}, f32[72,128]{1,0:T(8,128)S(1)}, u32[]{:S(2)}, u32[]{:S(2)}) collective-permute-start(f32[72,128]{1,0:T(8,128)S(1)} %get-tuple-element.22), channel_id=1, source_target_pairs={{0,16},{1,17},{2,18},{3,19},{4,20},{5,21},{6,22},{7,23},{8,24},{9,... | collective-permute-start | bytes 110600 | tf_op jit(solution)/shard_map/ppermute | solution.py:584
  27.7 9.7 %collective-permute-start = (f32[72,128]{1,0:T(8,128)S(1)}, f32[72,128]{1,0:T(8,128)S(1)}, u32[]{:S(2)}, u32[]{:S(2)}) collective-permute-start(f32[72,128]{1,0:T(8,128)S(1)} %get-tuple-element.23), channel_id=1, source_target_pairs={{0,496},{1,497},{2,498},{3,499},{4,500},{5,501},{6,502},{7,503},{8... | collective-permute-start | bytes 110600 | tf_op jit(solution)/shard_map/ppermute | solution.py:583
  37.4 18.3 %all_to_all.16 = f32[32,1,128]{2,1,0:T(1,128)S(1)} all-to-all(f32[32,1,128]{2,1,0:T(1,128)S(1)} %bitcast.26), channel_id=1, replica_groups={{0,16,32,48,64,80,96,112,128,144,160,176,192,208,224,240,256,272,288,30..., dimensions={0} | all-to-all | bytes 32768 | tf_op jit(solution)/shard_map/all_to_all | solution.py:580
  55.7 0.0 collective-permute-done.1.behind_ref
  55.7 0.0 collective-permute-done.ahead_ref
  55.7 2.1 %pack.1 = f32[32,56,128]{2,1,0:T(8,128)S(1)} custom-call(s32[48,128]{1,0:T(8,128)S(1)} %get-tuple-element.10.table_ref, f32[2,72,128]{2,1,0:T(8,128)S(1)} %get-tuple-element.11.side_ref, f32[2,56,128]{2,1,0:T(8,128)S(1)} %get-tuple-element.12.upright_ref, f32[72,128]{1,0:T(8,128)S(1)} %collective-permute-done.ahead_ref, ...), custom_call_target="tpu_custom_call" | custom-call | tf_op jit(solution)/shard_map/pack/pallas_call | solution.py:585
  57.8 22.2 %all_to_all.17 = f32[16,112,128]{2,1,0:T(8,128)S(1)} all-to-all(f32[16,112,128]{2,1,0:T(8,128)S(1)} %bitcast.22), channel_id=1, replica_groups={{0,1,2,3,4,5,6,7,8,9,10,11,12,13,14,15},{16,17,18,19,20,21,22,23,24,25,..., dimensions={0} | all-to-all | bytes 1835008 | tf_op jit(solution)/shard_map/all_to_all | solution.py:593
  80.0 0.0 copy-done.1
  80.0 0.0 copy-done.3
  80.0 7.3 %last.1 = (f32[2,8,128,128]{3,2,1,0:T(8,128)}, f32[8,128,128]{2,1,0:T(8,128)}) custom-call(s32[48,128]{1,0:T(8,128)S(1)} %get-tuple-element.10.table_ref, f32[2,72,128]{2,1,0:T(8,128)S(1)} %get-tuple-element.11.side_ref, f32[2,56,128]{2,1,0:T(8,128)S(1)} %get-tuple-element.12.upright_ref, f32[32,56,128]{2,1,0:T(8,128)S(1)} %bitcast.21, ...), custom_call_target="tpu_custom_call" | custom-call | tf_op jit(solution)/shard_map/last/pallas_call | solution.py:596
  (8 shorter events, 0.0 us)
Async XLA Ops:
  0.6 1.2 %copy-start = (f32[2,8,1,128,128]{4,3,2,1,0:T(8,128)S(1)}, f32[2,8,1,128,128]{4,3,2,1,0:T(8,128)}, u32[]{:S(2)}) copy-start(f32[2,8,1,128,128]{4,3,2,1,0:T(8,128)} %param.9) | copy-start | bytes 3145732
  1.9 1.0 %copy-start.2 = (f32[8,1,128,128]{3,2,1,0:T(8,128)S(1)}, f32[8,1,128,128]{3,2,1,0:T(8,128)}, u32[]{:S(2)}) copy-start(f32[8,1,128,128]{3,2,1,0:T(8,128)} %param.10) | copy-start | bytes 1572868
  2.9 0.9 %copy-start.4 = (f32[27,8,128]{2,1,0:T(8,128)S(1)}, f32[27,8,128]{2,1,0:T(8,128)}, u32[]{:S(2)}) copy-start(f32[27,8,128]{2,1,0:T(8,128)} %constant.22.clone.tiles_ref) | copy-start | bytes 331780
  3.8 0.9 %copy-start.5 = (f32[2,128,128]{2,1,0:T(8,128)S(1)}, f32[2,128,128]{2,1,0:T(8,128)}, u32[]{:S(2)}) copy-start(f32[2,128,128]{2,1,0:T(8,128)} %constant.19.clone.along_x_ref) | copy-start | bytes 393220
  4.7 0.8 copy-start.6
  5.5 0.8 copy-start.7
  6.4 0.7 copy-start.8
  7.1 0.7 copy-start.9
  7.8 0.7 copy-start.10
  20.9 59.1 %copy-start.1 = (f32[2,8,1,128,128]{4,3,2,1,0:T(8,128)S(1)}, f32[2,8,1,128,128]{4,3,2,1,0:T(8,128)}, u32[]{:S(2)}) copy-start(f32[2,8,1,128,128]{4,3,2,1,0:T(8,128)} %param.9) | copy-start | bytes 3145732
  20.9 59.1 %copy-start.3 = (f32[8,1,128,128]{3,2,1,0:T(8,128)S(1)}, f32[8,1,128,128]{3,2,1,0:T(8,128)}, u32[]{:S(2)}) copy-start(f32[8,1,128,128]{3,2,1,0:T(8,128)} %param.10) | copy-start | bytes 1572868
  20.9 34.8 %collective-permute-start.1 = (f32[72,128]{1,0:T(8,128)S(1)}, f32[72,128]{1,0:T(8,128)S(1)}, u32[]{:S(2)}, u32[]{:S(2)}) collective-permute-start(f32[72,128]{1,0:T(8,128)S(1)} %get-tuple-element.22), channel_id=1, source_target_pairs={{0,16},{1,17},{2,18},{3,19},{4,20},{5,21},{6,22},{7,23},{8,24},{9,... | collective-permute-start | bytes 110600 | tf_op jit(solution)/shard_map/ppermute | solution.py:584
  27.7 28.0 %collective-permute-start = (f32[72,128]{1,0:T(8,128)S(1)}, f32[72,128]{1,0:T(8,128)S(1)}, u32[]{:S(2)}, u32[]{:S(2)}) collective-permute-start(f32[72,128]{1,0:T(8,128)S(1)} %get-tuple-element.23), channel_id=1, source_target_pairs={{0,496},{1,497},{2,498},{3,499},{4,500},{5,501},{6,502},{7,503},{8... | collective-permute-start | bytes 110600 | tf_op jit(solution)/shard_map/ppermute | solution.py:583
where the time goes:
time: 87.9 us; the launch traced here: 87.3 us
  blocking collectives  40.5 us (46%)
  Pallas kernels  21.7 us (25%)
  starting transfers between devices  16.4 us (19%)
  local copies, waits for them, and re-layouts  7.87 us (9%)
    all_to_all x1, blocking collectives, per_device(): lax.all_to_all(send.reshape(16, 112, 128), axes, 0, 0, axis_index_groups=...  22.2 us
    all_to_all x1, blocking collectives, per_device(): lax.all_to_all(top[:squares], axes, 0, 0, axis_index_groups=same_place, t...  18.3 us
    pallas_call x1, Pallas kernels, per_device(): pl.pallas_call(functools.partial(first_kernel, cols_b), grid=(8,), in_spe...  12.4 us
    ppermute x1, starting transfers between devices, per_device(): lax.ppermute(side[1], axes, [(b, (b - 16) % count) for b in range(count)])  9.68 us
    unnamed x22, local copies, waits for them, and re-layouts  7.87 us
    pallas_call x1, Pallas kernels, per_device(): pl.pallas_call(last_kernel, grid=(8,), in_specs=[whole((48, 128), pltpu.S...  7.28 us
    ppermute x1, starting transfers between devices, per_device(): lax.ppermute(side[0], axes, [(b, (b + 16) % count) for b in range(count)])  6.77 us
    pallas_call x1, Pallas kernels, per_device(): pl.pallas_call(pack_kernel, in_specs=[whole((48, 128), pltpu.SMEM)] + [pl...  2.08 us
  transfers between devices with their start and end apart: 2, of which 0 were waited for; matrix products, arithmetic and copies ran while one was open for 0% of the time, Pallas kernels for 0%

commit v1 on v0

--- a/solution.py
+++ b/solution.py
@@ -11,6 +11,12 @@
 
 courant = 0.1
 hyper_coef = 0.002
+TOP_ROWS = 256
+MIB = 1024 * 1024
+EDGE_VMEM = 60 * MIB
+PACK_VMEM = 60 * MIB
+BLOCK_VMEM = 60 * MIB
+LAST_VMEM = 60 * MIB
 axes = ("elem", "sub")
 f32 = jnp.float32
 HIGH = lax.Precision.HIGHEST
@@ -222,118 +228,163 @@
     table_ref[40:48, :] = jnp.broadcast_to(there.astype(jnp.int32), (8, 128))
 
 
-def first_kernel(
+def share_band(values):
+    across = share_lanes(values).reshape(16, 8, 128)
+    row = lax.broadcasted_iota(jnp.int32, (1, 8, 128), 1)
+    above = pltpu.roll(across, 1, 1)
+    below = pltpu.roll(across, 7, 1)
+    shared = across + jnp.where(row == 4, above, jnp.where(row == 3, below, 0.0))
+    return shared.reshape(128, 128)
+
+
+def changes(east, north, height, coriolis, mass, inverse, share, along_x_ref, tiles_ref):
+    energy = 0.5 * (east * east + north * north) + height
+    flux_x, flux_y = height * east, height * north
+    first_x = jnp.dot(
+        jnp.concatenate([north, energy, flux_x], 0), along_x_ref[0],
+        precision=HIGH, preferred_element_type=f32,
+    )
+    second_x = jnp.dot(
+        jnp.concatenate([east, north, height], 0), along_x_ref[1],
+        precision=HIGH, preferred_element_type=f32,
+    )
+    absolute = first_x[:128] - along_rows(east, tiles_ref, 0) + coriolis
+    tendencies = (
+        absolute * north - first_x[128:256],
+        -absolute * east - along_rows(energy, tiles_ref, 0),
+        -(first_x[256:] + along_rows(flux_y, tiles_ref, 0)),
+    )
+    locals_, smoothed = [], []
+    for part, values in enumerate((east, north, height)):
+        lap = second_x[128 * part : 128 * part + 128] + along_rows(values, tiles_ref, 7)
+        local = share(lap * mass)
+        locals_.append(local)
+        smoothed.append(local * inverse)
+    second_x = jnp.dot(
+        jnp.concatenate(smoothed, 0), along_x_ref[1], precision=HIGH, preferred_element_type=f32
+    )
+    changed = []
+    for part in range(3):
+        lap = second_x[128 * part : 128 * part + 128] + along_rows(smoothed[part], tiles_ref, 7)
+        changed.append(share((tendencies[part] - hyper_coef * lap) * mass))
+    return locals_, changed
+
+
+def edge_kernel(
     cols_b, device_ref, owner_ref, velocity_ref, height_ref, coriolis_ref, elem_mass_ref,
     along_x_ref, expand_ref, expand_t_ref, tiles_ref,
-    partial_ref, side_ref, upright_ref, mass_ref, table_ref, top_ref,
-    node_mass, inner_inverse, columns, turned, upper_lower,
+    side_ref, upright_ref, mass_ref, table_ref, top_ref,
+    smooth, change,
 ):
-    level = pl.program_id(0)
     lane = lane_index(128)
-
-    @pl.when(level == 0)
+    top = jnp.zeros((128, 128), f32)
+    for level in range(8):
+        east, north = velocity_ref[0, level], velocity_ref[1, level]
+        top = jnp.maximum(
+            top, jnp.sqrt(east * east + north * north) + jnp.sqrt(height_ref[level])
+        )
+    top_ref[...] = jnp.broadcast_to(jnp.max(top), top_ref.shape)
+    rows = jnp.dot(expand_ref[...], elem_mass_ref[0], precision=HIGH, preferred_element_type=f32)
+    mass = jnp.dot(rows, expand_t_ref[...], precision=HIGH, preferred_element_type=f32)
+    mass_ref[...] = mass
+    find_tables(device_ref[0], owner_ref, table_ref, cols_b)
+    mass_t = jnp.transpose(mass)
+    coriolis = coriolis_ref[0]
+
+    def upright_band(ref_value):
+        return jnp.concatenate([ref_value[120:128], ref_value[0:8]], 0)
+
+    def upright_plane(read):
+        return jnp.concatenate(
+            [piece for level in range(8) for piece in (read(level, 120), read(level, 0))], 0
+        )
+
+    def sideways_plane(read):
+        packed = jnp.zeros((128, 128), f32)
+        for level in range(8):
+            packed = jnp.where(lane // 16 == level, turn(read(level), 8 + 16 * level), packed)
+        return jnp.transpose(packed)
+
+    def repeat(band):
+        return jnp.concatenate([band] * 8, 0)
+
+    row = lax.broadcasted_iota(jnp.int32, (128, 128), 0) % 16
+    inner = (row != 7) & (row != 8) & (lane > 0) & (lane < 127)
+    for way in range(2):
+        if way == 0:
+            planes = [
+                upright_plane(lambda level, at, c=c: velocity_ref[c, level, at : at + 8, :])
+                for c in range(2)
+            ] + [upright_plane(lambda level, at: height_ref[level, at : at + 8, :])]
+            turning = repeat(upright_band(coriolis))
+            band_mass = repeat(upright_band(mass))
+        else:
+            planes = [
+                sideways_plane(lambda level, c=c: velocity_ref[c, level]) for c in (1, 0)
+            ] + [sideways_plane(lambda level: height_ref[level])]
+            turning = -sideways_plane(lambda level: coriolis)
+            band_mass = repeat(upright_band(mass_t))
+        inverse = jnp.where(inner, 1.0 / share_band(band_mass), 0.0)
+        locals_, changed = changes(
+            *planes, turning, band_mass, inverse, share_band, along_x_ref, tiles_ref
+        )
+        for part in range(3):
+            target = part if way == 0 or part == 2 else 1 - part
+            smooth[way, target] = locals_[part]
+            change[way, target] = changed[part]
+
+    for way, ref in ((0, upright_ref), (1, side_ref)):
+        for end in range(2):
+            for part in range(3):
+                place = pl.ds(7 + end, 8, stride=16)
+                ref[end, 8 * part : 8 * part + 8, :] = smooth.at[way, part][place, :]
+                ref[end, 24 + 8 * part : 32 + 8 * part, :] = change.at[way, part][place, :]
+    mass_lines = (mass_t[127:128], mass_t[0:1], mass[127:128], mass[0:1])
+    lines = (side_ref[0], side_ref[1], upright_ref[0], upright_ref[1])
+    ends = {}
+    for side in range(4):
+        local_mass = share_lanes(mass_lines[side])
+        for high in (False, True):
+            ends[side, high] = pack_end(lines[side][0:24], high) + pack_mass(local_mass, high)
+    extras = (
+        ends[UPPER, True] + turn(ends[LOWER, True], 12),
+        ends[UPPER, False] + turn(ends[LOWER, False], 12),
+        ends[LEFT, True] + turn(ends[RIGHT, True], 12),
+        ends[LEFT, False] + turn(ends[RIGHT, False], 12),
+    )
+    for side in range(4):
+        tile = extras[side] + fold_line(mass_lines[side])
+        if side < 2:
+            side_ref[side, 48:56, :] = tile
+        else:
+            upright_ref[side - 2, 48:56, :] = tile
+    for across, sideways in ((RIGHT, True), (LEFT, False)):
+        for number, (along, upward) in enumerate(((UPPER, True), (LOWER, False))):
+            tile = ends[along, sideways] + turn(ends[across, upward], 12)
+            tile = tile + turn(pack_end(lines[along][24:48], sideways), 48)
+            side_ref[across, 56 + 8 * number : 64 + 8 * number, :] = tile
+
+
+def block_kernel(
+    velocity_ref, height_ref, coriolis_ref, mass_in_ref, along_x_ref, tiles_ref, after_ref,
+    partial_ref, mass_ref, inner_inverse,
+):
+    lane = lane_index(128)
+
+    @pl.when(pl.program_id(0) == 0)
     def _():
-        rows = jnp.dot(
-            expand_ref[...], elem_mass_ref[0], precision=HIGH, preferred_element_type=f32
-        )
-        mass = jnp.dot(rows, expand_t_ref[...], precision=HIGH, preferred_element_type=f32)
-        node_mass[...] = mass
-        local_mass = share_block(mass)
+        local_mass = share_block(mass_in_ref[...])
         mass_ref[...] = local_mass
         row = lax.broadcasted_iota(jnp.int32, (128, 128), 0)
         inner = (row > 0) & (row < 127) & (lane > 0) & (lane < 127)
         inner_inverse[...] = jnp.where(inner, 1.0 / local_mass, 0.0)
-        columns[...] = jnp.where(lane // 2 == 48, turn(mass, 97), 0.0)
-        find_tables(device_ref[0], owner_ref, table_ref, cols_b)
-        top_ref[...] = jnp.zeros_like(top_ref)
-
-    mass = node_mass[...]
-    east = velocity_ref[0, 0]
-    north = velocity_ref[1, 0]
-    height = height_ref[0]
-    squared = east * east + north * north
-    energy = 0.5 * squared + height
-    speed = jnp.max(jnp.sqrt(squared) + jnp.sqrt(height))
-    top_ref[...] = jnp.maximum(top_ref[...], speed)
-    flux_x, flux_y = height * east, height * north
-    first_x = jnp.dot(
-        jnp.concatenate([north, energy, flux_x], 0), along_x_ref[0],
-        precision=HIGH, preferred_element_type=f32,
-    )
-    second_x = jnp.dot(
-        jnp.concatenate([east, north, height], 0), along_x_ref[1],
-        precision=HIGH, preferred_element_type=f32,
-    )
-    absolute = first_x[:128] - along_rows(east, tiles_ref, 0) + coriolis_ref[0]
-    tendencies = (
-        absolute * north - first_x[128:256],
-        -absolute * east - along_rows(energy, tiles_ref, 0),
-        -(first_x[256:] + along_rows(flux_y, tiles_ref, 0)),
-    )
-    smoothed = []
-    for part, values in enumerate((east, north, height)):
-        lap = second_x[128 * part : 128 * part + 128] + along_rows(values, tiles_ref, 7)
-        local = share_block(lap * mass)
-        place = 8 * part + level
-        upper_lower[0, pl.ds(place, 1), :] = local[127:128]
-        upper_lower[1, pl.ds(place, 1), :] = local[0:1]
-        columns[...] = jnp.where(
-            lane // 2 == place, pltpu.roll(local, 2 * place + 1, 1), columns[...]
-        )
-        smoothed.append(local * inner_inverse[...])
-    second_x = jnp.dot(
-        jnp.concatenate(smoothed, 0), along_x_ref[1], precision=HIGH, preferred_element_type=f32
+
+    _, changed = changes(
+        velocity_ref[0, 0], velocity_ref[1, 0], height_ref[0], coriolis_ref[0], mass_in_ref[...],
+        inner_inverse[...], share_block, along_x_ref, tiles_ref,
     )
     for part in range(3):
-        lap = second_x[128 * part : 128 * part + 128] + along_rows(smoothed[part], tiles_ref, 7)
-        local = share_block((tendencies[part] - hyper_coef * lap) * mass)
-        partial_ref[part, 0] = local
-        place = 24 + 8 * part + level
-        upper_lower[0, pl.ds(place, 1), :] = local[127:128]
-        upper_lower[1, pl.ds(place, 1), :] = local[0:1]
-        columns[...] = jnp.where(
-            lane // 2 == place, pltpu.roll(local, 2 * place + 1, 1), columns[...]
-        )
-
-    @pl.when(level == 7)
-    def _():
-        turned[...] = jnp.transpose(columns[...])
-        for place in range(48):
-            side_ref[0, place : place + 1, :] = turned[2 * place : 2 * place + 1, :]
-            side_ref[1, place : place + 1, :] = turned[2 * place + 1 : 2 * place + 2, :]
-        mass_lines = (
-            turned[96:97, :], turned[97:98, :], node_mass[127:128, :], node_mass[0:1, :],
-        )
-        smooth_lines = (
-            side_ref[0, 0:24, :], side_ref[1, 0:24, :], upper_lower[0, 0:24, :], upper_lower[1, 0:24, :],
-        )
-        change_lines = {
-            UPPER: upper_lower[0, 24:48, :], LOWER: upper_lower[1, 24:48, :],
-        }
-        ends = {}
-        for side in range(4):
-            local_mass = share_lanes(mass_lines[side])
-            for high in (False, True):
-                ends[side, high] = pack_end(smooth_lines[side], high) + pack_mass(local_mass, high)
-        upright_ref[0, 0:48, :] = upper_lower[0, 0:48, :]
-        upright_ref[1, 0:48, :] = upper_lower[1, 0:48, :]
-        extras = (
-            ends[UPPER, True] + turn(ends[LOWER, True], 12),
-            ends[UPPER, False] + turn(ends[LOWER, False], 12),
-            ends[LEFT, True] + turn(ends[RIGHT, True], 12),
-            ends[LEFT, False] + turn(ends[RIGHT, False], 12),
-        )
-        for side in range(4):
-            tile = extras[side] + fold_line(mass_lines[side])
-            if side < 2:
-                side_ref[side, 48:56, :] = tile
-            else:
-                upright_ref[side - 2, 48:56, :] = tile
-        for across, sideways in ((RIGHT, True), (LEFT, False)):
-            for number, (along, upward) in enumerate(((UPPER, True), (LOWER, False))):
-                tile = ends[along, sideways] + turn(ends[across, upward], 12)
-                tile = tile + turn(pack_end(change_lines[along], sideways), 48)
-                side_ref[across, 56 + 8 * number : 64 + 8 * number, :] = tile
+        partial_ref[part, 0] = changed[part]
 
 
 def pack_kernel(table_ref, side_ref, upright_ref, ahead_ref, behind_ref, tops_ref, send_ref):
@@ -549,36 +600,28 @@
     triple = pl.BlockSpec((3, 1, 128, 128), lambda level: (0, level, 0, 0))
     shape = jax.ShapeDtypeStruct
     params = pltpu.CompilerParams(
-        dimension_semantics=("arbitrary",), vmem_limit_bytes=32 * 1024 * 1024
-    )
-    partial, side, upright, local_mass, table, top = pl.pallas_call(
-        functools.partial(first_kernel, cols_b),
-        grid=(8,),
-        in_specs=[
-            whole((1,), pltpu.SMEM), whole((4, 128)), pair, single, whole((1, 128, 128)),
-            whole((1, 32, 32)), whole((2, 128, 128)), whole((128, 32)), whole((32, 128)),
-            whole((27, 8, 128)),
-        ],
-        out_specs=[
-            triple, whole((2, 72, 128)), whole((2, 56, 128)), whole((128, 128)), whole((48, 128)),
-            whole((32, 128)),
-        ],
+        dimension_semantics=("arbitrary",), vmem_limit_bytes=BLOCK_VMEM
+    )
+    vmem = pltpu.VMEM
+    side, upright, mass, table, top = pl.pallas_call(
+        functools.partial(edge_kernel, cols_b),
+        in_specs=[pl.BlockSpec(memory_space=pltpu.SMEM)] + [pl.BlockSpec(memory_space=vmem)] * 9,
+        out_specs=[pl.BlockSpec(memory_space=vmem)] * 5,
         out_shape=[
-            shape((3, 8, 128, 128), f32), shape((2, 72, 128), f32), shape((2, 56, 128), f32),
-            shape((128, 128), f32), shape((48, 128), jnp.int32), shape((32, 128), f32),
+            shape((2, 72, 128), f32), shape((2, 56, 128), f32),
+            shape((128, 128), f32), shape((48, 128), jnp.int32), shape((TOP_ROWS, 128), f32),
         ],
         scratch_shapes=[
-            pltpu.VMEM((128, 128), f32), pltpu.VMEM((128, 128), f32), pltpu.VMEM((128, 128), f32),
-            pltpu.VMEM((128, 128), f32), pltpu.VMEM((2, 48, 128), f32),
+            pltpu.VMEM((2, 3, 128, 128), f32), pltpu.VMEM((2, 3, 128, 128), f32),
         ],
-        compiler_params=params,
-        name="first",
+        compiler_params=pltpu.CompilerParams(vmem_limit_bytes=EDGE_VMEM),
+        name="edge",
     )(device, block_owner, velocity, thickness, coriolis, elem_mass, along_x, expand, expand_t, tiles)
     squares = count // 16
     same_place = [[16 * s + i for s in range(squares)] for i in range(16)]
     same_square = [[16 * s + i for i in range(16)] for s in range(squares)]
     tops = lax.all_to_all(
-        top[:squares], axes, 0, 0, axis_index_groups=same_place, tiled=True
+        top[: 8 * squares], axes, 0, 0, axis_index_groups=same_place, tiled=True
     )
     ahead = lax.ppermute(side[1], axes, [(b, (b - 16) % count) for b in range(count)])
     behind = lax.ppermute(side[0], axes, [(b, (b + 16) % count) for b in range(count)])
@@ -587,12 +630,28 @@
         in_specs=[whole((48, 128), pltpu.SMEM)] + [pl.BlockSpec(memory_space=pltpu.VMEM)] * 5,
         out_specs=pl.BlockSpec(memory_space=pltpu.VMEM),
         out_shape=shape((32, 56, 128), f32),
-        compiler_params=pltpu.CompilerParams(vmem_limit_bytes=32 * 1024 * 1024),
+        compiler_params=pltpu.CompilerParams(vmem_limit_bytes=PACK_VMEM),
         name="pack",
     )(table, side, upright, ahead, behind, tops)
     received = lax.all_to_all(
         send.reshape(16, 112, 128), axes, 0, 0, axis_index_groups=same_square, tiled=True
     ).reshape(32, 56, 128)
+    partial, local_mass = pl.pallas_call(
+        block_kernel,
+        grid=(8,),
+        in_specs=[
+            pair, single, whole((1, 128, 128)), whole((128, 128)), whole((2, 128, 128)),
+            whole((27, 8, 128)), whole((1, 8, 128)),
+        ],
+        out_specs=[triple, whole((128, 128))],
+        out_shape=[shape((3, 8, 128, 128), f32), shape((128, 128), f32)],
+        scratch_shapes=[pltpu.VMEM((128, 128), f32)],
+        compiler_params=params,
+        cost_estimate=pl.CostEstimate(
+            flops=2_000_000_000, bytes_accessed=3_200_000, transcendentals=0
+        ),
+        name="block",
+    )(velocity, thickness, coriolis, mass, along_x, tiles, send)
     new_velocity, new_thickness = pl.pallas_call(
         last_kernel,
         grid=(8,),
@@ -605,7 +664,9 @@
         scratch_shapes=[
             pltpu.VMEM((4, 24, 128), f32), pltpu.VMEM((128, 128), f32), pltpu.VMEM((128, 128), f32),
         ],
-        compiler_params=params,
+        compiler_params=pltpu.CompilerParams(
+            dimension_semantics=("arbitrary",), vmem_limit_bytes=LAST_VMEM
+        ),
         name="last",
     )(table, side, upright, received, tiles, local_mass, velocity, thickness, partial)
     return new_velocity[:, :, None], new_thickness[:, None]

time: 87.9 us -> 70 us (0.80)
  blocking collectives: 40.5 us -> 0 us
  starting transfers between devices: 16.4 us -> 33.2 us
  Pallas kernels: 21.7 us -> 30 us
  local copies, waits for them, and re-layouts: 7.87 us -> 2.38 us
  waiting for transfers between devices: 0.01 us -> 3.1 us
    all_to_all x2 -> x0, blocking collectives: 40.5 us -> none  [the longest x1 22.2 us: per_device(): lax.all_to_all(send.reshape(16, 112, 128), axes, 0, 0, axis_index_groups=...]
    all_to_all x0 -> x2, starting transfers between devices: none -> 23.7 us  [the longest x1 16.5 us: per_device(): lax.all_to_all(top[:8 * squares], axes, 0, 0, axis_index_groups=same_plac...]
    unnamed x22 -> x8, local copies, waits for them, and re-layouts: 7.87 us -> 1.59 us
    pallas_call x1 -> x2, Pallas kernels: 12.4 us -> 17.5 us  [the longest x1 12.4 us: per_device(): pl.pallas_call(block_kernel, grid=(8,), in_specs=[pair, single, whole((1,...]
    ppermute x1, starting transfers between devices: 9.68 us -> 5.46 us  [per_device(): lax.ppermute(side[1], axes, [(b, (b - 16) % count) for b in range(count)])]
    ppermute x1, starting transfers between devices: 6.77 us -> 4.02 us  [per_device(): lax.ppermute(side[0], axes, [(b, (b + 16) % count) for b in range(count)])]
    pallas_call x1, Pallas kernels: 7.28 us -> 9.25 us  [per_device(): pl.pallas_call(last_kernel, grid=(8,), in_specs=[whole((48, 128), pltpu.S...]
    all_to_all x0 -> x2, waiting for transfers between devices: none -> 1.58 us  [the longest x1 1.57 us: per_device(): lax.all_to_all(send.reshape(16, 112, 128), axes, 0, 0, axis_index_groups=...]
  transfers between devices with their start and end apart: 2 -> 4, of which waited for: 0 -> 3; matrix products, arithmetic and copies ran while one was open for 0% -> 1% of each run, Pallas kernels for 0% -> 18%
where the time goes in v1:
time: 70 us; the launch traced here: 69.4 us
  starting transfers between devices  33.2 us (47%)
  Pallas kernels  30 us (43%)
  waiting for transfers between devices  3.1 us (4%)
  local copies, waits for them, and re-layouts  2.38 us (3%)
    all_to_all x1, starting transfers between devices, per_device(): lax.all_to_all(top[:8 * squares], axes, 0, 0, axis_index_groups=same_plac...  16.5 us
    pallas_call x1, Pallas kernels, per_device(): pl.pallas_call(block_kernel, grid=(8,), in_specs=[pair, single, whole((1,...  12.4 us
    pallas_call x1, Pallas kernels, per_device(): pl.pallas_call(last_kernel, grid=(8,), in_specs=[whole((48, 128), pltpu.S...  9.25 us
    all_to_all x1, starting transfers between devices, per_device(): lax.all_to_all(send.reshape(16, 112, 128), axes, 0, 0, axis_index_groups=...  7.17 us
    ppermute x1, starting transfers between devices, per_device(): lax.ppermute(side[1], axes, [(b, (b - 16) % count) for b in range(count)])  5.46 us
    pallas_call x1, Pallas kernels, per_device(): pl.pallas_call(functools.partial(edge_kernel, cols_b), in_specs=[pl.Block...  5.08 us
    ppermute x1, starting transfers between devices, per_device(): lax.ppermute(side[0], axes, [(b, (b + 16) % count) for b in range(count)])  4.02 us
    pallas_call x1, Pallas kernels, per_device(): pl.pallas_call(pack_kernel, in_specs=[whole((48, 128), pltpu.SMEM)] + [pl...  3.27 us
  transfers between devices with their start and end apart: 4, of which 3 were waited for; matrix products, arithmetic and copies ran while one was open for 1% of the time, Pallas kernels for 18%

profile of v1, /device:TPU:1, one launch (start us, length us, event | category | flops | bytes accessed | tf_op | source)
XLA Modules:
  0.0 69.4 jit_solution(14352901996900883764)
XLA Ops:
  0.6 5.1 %edge.1 = (f32[2,72,128]{2,1,0:T(8,128)}, f32[2,56,128]{2,1,0:T(8,128)}, f32[128,128]{1,0:T(8,128)}, s32[48,128]{1,0:T(8,128)}, f32[256,128]{1,0:T(8,128)}) custom-call(s32[1]{0:T(128)} %bitcast.device_ref, s32[4,128]{1,0:T(4,128)} %owner_ref.1, f32[2,8,128,128]{3,2,1,0:T(8,128)} %bitcast.17, f32[8,128,128]{2,1,0:T(8,128)} %bitcast.22, ...), custom_call_target="tpu_custom_call" | custom-call | tf_op jit(solution)/shard_map/edge/pallas_call | solution.py:606
  5.7 16.5 %all-to-all-start = ((f32[32,8,128]{2,1,0:T(8,128)}), f32[32,8,128]{2,1,0:T(8,128)S(1)}, u32[]{:S(2)}, u32[]{:S(2)}) async-start(f32[32,8,128]{2,1,0:T(8,128)} %bitcast.26), calls=%async_computation | async-start | bytes 262144 | tf_op jit(solution)/shard_map/all_to_all | solution.py:623
  22.2 0.8 %slice_bitcast_fusion = (f32[72,128]{1,0:T(8,128)S(1)}, f32[72,128]{1,0:T(8,128)S(1)}) fusion(f32[2,72,128]{2,1,0:T(8,128)} %get-tuple-element.12.side_ref), kind=kLoop, calls=%fused_computation | loop fusion | bytes 147456 | tf_op jit(solution)/shard_map/squeeze | solution.py:627
  23.0 4.0 %collective-permute-start.1 = (f32[72,128]{1,0:T(8,128)S(1)}, f32[72,128]{1,0:T(8,128)S(1)}, u32[]{:S(2)}, u32[]{:S(2)}) collective-permute-start(f32[72,128]{1,0:T(8,128)S(1)} %get-tuple-element.22), channel_id=1, source_target_pairs={{0,16},{1,17},{2,18},{3,19},{4,20},{5,21},{6,22},{7,23},{8,24},{9,... | collective-permute-start | bytes 110600 | tf_op jit(solution)/shard_map/ppermute | solution.py:627
  27.1 5.5 %collective-permute-start = (f32[72,128]{1,0:T(8,128)S(1)}, f32[72,128]{1,0:T(8,128)S(1)}, u32[]{:S(2)}, u32[]{:S(2)}) collective-permute-start(f32[72,128]{1,0:T(8,128)S(1)} %get-tuple-element.23), channel_id=1, source_target_pairs={{0,496},{1,497},{2,498},{3,499},{4,500},{5,501},{6,502},{7,503},{8... | collective-permute-start | bytes 110600 | tf_op jit(solution)/shard_map/ppermute | solution.py:626
  32.5 0.2 collective-permute-done.1.behind_ref
  32.7 0.0 copy-start.2
  32.7 1.4 %collective-permute-done.ahead_ref = f32[72,128]{1,0:T(8,128)S(1)} collective-permute-done((f32[72,128]{1,0:T(8,128)S(1)}, f32[72,128]{1,0:T(8,128)S(1)}, u32[]{:S(2)}, u32[]{:S(2)}) %collective-permute-start) | collective-permute-done | bytes 36896 | tf_op jit(solution)/shard_map/ppermute | solution.py:626
  34.1 0.0 copy-start.3
  34.1 0.0 all-to-all-done
  34.1 0.0 copy-start.1
  34.1 0.0 copy-done.2
  34.1 0.6 copy-done.3
  34.7 0.1 copy-done.1
  34.7 3.3 %pack.1.after_ref = f32[32,56,128]{2,1,0:T(8,128)} custom-call(s32[48,128]{1,0:T(8,128)} %get-tuple-element.11.table_ref, f32[2,72,128]{2,1,0:T(8,128)} %get-tuple-element.12.side_ref, f32[2,56,128]{2,1,0:T(8,128)} %get-tuple-element.13.upright_ref, f32[72,128]{1,0:T(8,128)} %copy-done.3, f32[72,128]{1,0:T(8,128)} %copy-done.2, f32[256,128]{1,0:T(8,128)} %bitcast.25), custom_call_target="tpu_custom_call" | custom-call | tf_op jit(solution)/shard_map/pack/pallas_call | solution.py:628
  38.0 7.2 %all-to-all-start.1 = ((f32[16,112,128]{2,1,0:T(8,128)}), f32[16,112,128]{2,1,0:T(8,128)S(1)}, u32[]{:S(2)}, u32[]{:S(2)}) async-start(f32[16,112,128]{2,1,0:T(8,128)} %bitcast.21), calls=%async_computation.1 | async-start | bytes 1835008 | tf_op jit(solution)/shard_map/all_to_all | solution.py:636
  45.2 12.4 %block.1 = (f32[3,8,128,128]{3,2,1,0:T(8,128)}, f32[128,128]{1,0:T(8,128)}) custom-call(f32[2,8,128,128]{3,2,1,0:T(8,128)} %bitcast.18, f32[8,128,128]{2,1,0:T(8,128)} %bitcast.23, f32[1,128,128]{2,1,0:T(8,128)} %coriolis_ref.3, f32[128,128]{1,0:T(8,128)} %get-tuple-element.15.mass_in_ref, f32[2,128,128]{2,1,0:T(8,128)} %constant.19.clone.along_x_ref, ...), custom_call_target="tpu_custom_call" | custom-call | flops 2000000000 | bytes 3200000 | tf_op jit(solution)/shard_map/block/pallas_call | solution.py:639
  57.6 1.6 %all-to-all-done.1 = f32[16,112,128]{2,1,0:T(8,128)S(1)} async-done(((f32[16,112,128]{2,1,0:T(8,128)}), f32[16,112,128]{2,1,0:T(8,128)S(1)}, u32[]{:S(2)}, u32[]{:S(2)}) %all-to-all-start.1) | async-done | bytes 917536 | tf_op jit(solution)/shard_map/all_to_all | solution.py:636
  59.2 0.0 copy-start
  59.2 0.9 %copy-done = f32[16,112,128]{2,1,0:T(8,128)} copy-done((f32[16,112,128]{2,1,0:T(8,128)}, f32[16,112,128]{2,1,0:T(8,128)S(1)}, u32[]{:S(2)}) %copy-start) | copy-done | bytes 917528
  60.1 9.3 %last.1 = (f32[2,8,128,128]{3,2,1,0:T(8,128)}, f32[8,128,128]{2,1,0:T(8,128)}) custom-call(s32[48,128]{1,0:T(8,128)} %get-tuple-element.11.table_ref, f32[2,72,128]{2,1,0:T(8,128)} %get-tuple-element.12.side_ref, f32[2,56,128]{2,1,0:T(8,128)} %get-tuple-element.13.upright_ref, f32[32,56,128]{2,1,0:T(8,128)} %bitcast.20, ...), custom_call_target="tpu_custom_call" | custom-call | tf_op jit(solution)/shard_map/last/pallas_call | solution.py:655
Async XLA Ops:
  5.7 28.3 %all-to-all-start = ((f32[32,8,128]{2,1,0:T(8,128)}), f32[32,8,128]{2,1,0:T(8,128)S(1)}, u32[]{:S(2)}, u32[]{:S(2)}) async-start(f32[32,8,128]{2,1,0:T(8,128)} %bitcast.26), calls=%async_computation | async-start | bytes 262144 | tf_op jit(solution)/shard_map/all_to_all | solution.py:623
  23.0 9.7 %collective-permute-start.1 = (f32[72,128]{1,0:T(8,128)S(1)}, f32[72,128]{1,0:T(8,128)S(1)}, u32[]{:S(2)}, u32[]{:S(2)}) collective-permute-start(f32[72,128]{1,0:T(8,128)S(1)} %get-tuple-element.22), channel_id=1, source_target_pairs={{0,16},{1,17},{2,18},{3,19},{4,20},{5,21},{6,22},{7,23},{8,24},{9,... | collective-permute-start | bytes 110600 | tf_op jit(solution)/shard_map/ppermute | solution.py:627
  27.1 7.0 %collective-permute-start = (f32[72,128]{1,0:T(8,128)S(1)}, f32[72,128]{1,0:T(8,128)S(1)}, u32[]{:S(2)}, u32[]{:S(2)}) collective-permute-start(f32[72,128]{1,0:T(8,128)S(1)} %get-tuple-element.23), channel_id=1, source_target_pairs={{0,496},{1,497},{2,498},{3,499},{4,500},{5,501},{6,502},{7,503},{8... | collective-permute-start | bytes 110600 | tf_op jit(solution)/shard_map/ppermute | solution.py:626
  32.7 1.4 %copy-start.2 = (f32[72,128]{1,0:T(8,128)}, f32[72,128]{1,0:T(8,128)S(1)}, u32[]{:S(2)}) copy-start(f32[72,128]{1,0:T(8,128)S(1)} %collective-permute-done.1.behind_ref) | copy-start | bytes 110596
  34.1 0.6 copy-start.3
  34.1 0.7 copy-start.1
  38.0 21.2 %all-to-all-start.1 = ((f32[16,112,128]{2,1,0:T(8,128)}), f32[16,112,128]{2,1,0:T(8,128)S(1)}, u32[]{:S(2)}, u32[]{:S(2)}) async-start(f32[16,112,128]{2,1,0:T(8,128)} %bitcast.21), calls=%async_computation.1 | async-start | bytes 1835008 | tf_op jit(solution)/shard_map/all_to_all | solution.py:636
  59.2 0.9 %copy-start = (f32[16,112,128]{2,1,0:T(8,128)}, f32[16,112,128]{2,1,0:T(8,128)S(1)}, u32[]{:S(2)}) copy-start(f32[16,112,128]{2,1,0:T(8,128)S(1)} %all-to-all-done.1) | copy-start | bytes 2752516

commit v2 on v1

--- a/solution.py
+++ b/solution.py
@@ -14,9 +14,11 @@
 TOP_ROWS = 256
 MIB = 1024 * 1024
 EDGE_VMEM = 60 * MIB
-PACK_VMEM = 60 * MIB
+PACK_VMEM = 53 * MIB
 BLOCK_VMEM = 60 * MIB
-LAST_VMEM = 60 * MIB
+LAST_VMEM = 52 * MIB
+GROUPS = 4
+LEVELS_EACH = 8 // GROUPS
 axes = ("elem", "sub")
 f32 = jnp.float32
 HIGH = lax.Precision.HIGHEST
@@ -194,7 +196,6 @@
     inside = jnp.full((16, 1), 8, jnp.int32)
     for number, (step_y, step_x) in enumerate(steps8):
         inside = jnp.where((down == step_y) & (over == step_x), number, inside)
-    table_ref[0:16, :] = jnp.broadcast_to(inside, (16, 128))
     crossing = jnp.full((16, 1), 6, jnp.int32)
     sixteen = lax.broadcasted_iota(jnp.int32, (16, 1), 0)
     for side, start, step_x in ((0, 32, 1), (1, 0, -1)):
@@ -208,7 +209,6 @@
             crossing = jnp.where(
                 beside & (here_rows - their_row == step_y), 3 * side + number, crossing
             )
-    table_ref[16:32, :] = jnp.broadcast_to(crossing, (16, 128))
     way = lax.broadcasted_iota(jnp.int32, (8, 1), 0)
     step_y = jnp.zeros((8, 1), jnp.int32)
     step_x = jnp.zeros((8, 1), jnp.int32)
@@ -224,8 +224,11 @@
     found = jnp.sum(found, axis=1, keepdims=True).astype(jnp.int32)
     there = (near_row >= 0) & (near_row < 4)
     slot = 2 * (found % 16) + jnp.where(found // 16 == square, 0, 1)
-    table_ref[32:40, :] = jnp.broadcast_to(slot, (8, 128))
-    table_ref[40:48, :] = jnp.broadcast_to(there.astype(jnp.int32), (8, 128))
+    column = jnp.concatenate([inside, crossing, slot, there.astype(jnp.int32)], 0).astype(f32)
+    picked = lax.broadcasted_iota(jnp.int32, (48, 128), 0) == lane_index(48)
+    table_ref[...] = jnp.sum(jnp.where(picked, column, 0.0), axis=0, keepdims=True).astype(
+        jnp.int32
+    )
 
 
 def share_band(values):
@@ -271,11 +274,27 @@
 
 
 def edge_kernel(
-    cols_b, device_ref, owner_ref, velocity_ref, height_ref, coriolis_ref, elem_mass_ref,
-    along_x_ref, expand_ref, expand_t_ref, tiles_ref,
-    side_ref, upright_ref, mass_ref, table_ref, top_ref,
-    smooth, change,
+    cols_b, device_ref, owner_far, velocity_far, height_far, coriolis_far, elem_mass_far,
+    along_x_far, expand_far, expand_t_far, tiles_far,
+    right_ref, left_ref, message_ref, mass_ref, table_ref, top_ref,
+    smooth, change, owner_ref, velocity_ref, height_ref, coriolis_ref, elem_mass_ref,
+    along_x_ref, expand_ref, expand_t_ref, tiles_ref, arrived,
 ):
+    far = (
+        expand_far, elem_mass_far, expand_t_far, owner_far, height_far, velocity_far,
+        coriolis_far, tiles_far, along_x_far,
+    )
+    near = (
+        expand_ref, elem_mass_ref, expand_t_ref, owner_ref, height_ref, velocity_ref,
+        coriolis_ref, tiles_ref, along_x_ref,
+    )
+    copies = [
+        pltpu.make_async_copy(far[k], near[k], arrived.at[k]) for k in range(len(far))
+    ]
+    for copy in copies:
+        copy.start()
+    for copy in copies:
+        copy.wait()
     lane = lane_index(128)
     top = jnp.zeros((128, 128), f32)
     for level in range(8):
@@ -333,14 +352,17 @@
             smooth[way, target] = locals_[part]
             change[way, target] = changed[part]
 
-    for way, ref in ((0, upright_ref), (1, side_ref)):
+    for way in range(2):
         for end in range(2):
+            side = 2 * (1 - way) + end
             for part in range(3):
                 place = pl.ds(7 + end, 8, stride=16)
-                ref[end, 8 * part : 8 * part + 8, :] = smooth.at[way, part][place, :]
-                ref[end, 24 + 8 * part : 32 + 8 * part, :] = change.at[way, part][place, :]
+                message_ref[side, 8 * part : 8 * part + 8, :] = smooth.at[way, part][place, :]
+                message_ref[side, 24 + 8 * part : 32 + 8 * part, :] = change.at[way, part][place, :]
+    right_ref[0:48, :] = message_ref[RIGHT, 0:48, :]
+    left_ref[0:48, :] = message_ref[LEFT, 0:48, :]
     mass_lines = (mass_t[127:128], mass_t[0:1], mass[127:128], mass[0:1])
-    lines = (side_ref[0], side_ref[1], upright_ref[0], upright_ref[1])
+    lines = [message_ref[side, 0:48, :] for side in range(4)]
     ends = {}
     for side in range(4):
         local_mass = share_lanes(mass_lines[side])
@@ -354,90 +376,77 @@
     )
     for side in range(4):
         tile = extras[side] + fold_line(mass_lines[side])
-        if side < 2:
-            side_ref[side, 48:56, :] = tile
-        else:
-            upright_ref[side - 2, 48:56, :] = tile
-    for across, sideways in ((RIGHT, True), (LEFT, False)):
-        for number, (along, upward) in enumerate(((UPPER, True), (LOWER, False))):
+        message_ref[side, 48:56, :] = tile
+        if side == RIGHT:
+            right_ref[48:56, :] = tile
+        elif side == LEFT:
+            left_ref[48:56, :] = tile
+    for number, (along, upward) in enumerate(((UPPER, True), (LOWER, False))):
+        for across, sideways, ref in ((RIGHT, True, right_ref), (LEFT, False, left_ref)):
             tile = ends[along, sideways] + turn(ends[across, upward], 12)
             tile = tile + turn(pack_end(lines[along][24:48], sideways), 48)
-            side_ref[across, 56 + 8 * number : 64 + 8 * number, :] = tile
+            message_ref[4 + 2 * number + across, 48:56, :] = tile
+            ref[56 + 8 * number : 64 + 8 * number, :] = tile
 
 
 def block_kernel(
     velocity_ref, height_ref, coriolis_ref, mass_in_ref, along_x_ref, tiles_ref, after_ref,
-    partial_ref, mass_ref, inner_inverse,
+    partial_ref, inner_inverse,
 ):
     lane = lane_index(128)
-
-    @pl.when(pl.program_id(0) == 0)
+    step = pl.program_id(0)
+
+    @pl.when(step == 0)
     def _():
         local_mass = share_block(mass_in_ref[...])
-        mass_ref[...] = local_mass
         row = lax.broadcasted_iota(jnp.int32, (128, 128), 0)
         inner = (row > 0) & (row < 127) & (lane > 0) & (lane < 127)
         inner_inverse[...] = jnp.where(inner, 1.0 / local_mass, 0.0)
 
-    _, changed = changes(
-        velocity_ref[0, 0], velocity_ref[1, 0], height_ref[0], coriolis_ref[0], mass_in_ref[...],
-        inner_inverse[...], share_block, along_x_ref, tiles_ref,
-    )
-    for part in range(3):
-        partial_ref[part, 0] = changed[part]
-
-
-def pack_kernel(table_ref, side_ref, upright_ref, ahead_ref, behind_ref, tops_ref, send_ref):
+    @pl.when(step < 8)
+    def _():
+        _, changed = changes(
+            velocity_ref[0, 0], velocity_ref[1, 0], height_ref[0], coriolis_ref[0],
+            mass_in_ref[...], inner_inverse[...], share_block, along_x_ref, tiles_ref,
+        )
+        for part in range(3):
+            partial_ref[part] = changed[part]
+
+    @pl.when(step == 8)
+    def _():
+        partial_ref[0] = share_block(mass_in_ref[...])
+
+
+def pack_kernel(table_ref, message_ref, ahead_ref, behind_ref, tops_ref, send_ref):
     lane = lane_index(8)
-    top = jnp.max(tops_ref[...])
+    top = jnp.max(tops_ref[...], axis=(0, 1), keepdims=True)[0]
     for place in range(16):
-        message = table_ref[place, 0]
-
-        @pl.when(message < 2)
-        def _():
-            send_ref[2 * place] = side_ref[jnp.minimum(message, 1), 0:56, :]
-
-        @pl.when((message >= 2) & (message < 4))
-        def _():
-            send_ref[2 * place] = upright_ref[jnp.clip(message - 2, 0, 1)]
-
-        for corner, (side, row) in enumerate(((0, 56), (1, 56), (0, 64), (1, 64))):
-
-            @pl.when(message == 4 + corner)
-            def _(side=side, row=row):
-                send_ref[2 * place, 48:56, :] = side_ref[side, row : row + 8, :]
-
-        send_ref[2 * place, 48:56, :] = jnp.where(lane >= 96, top, send_ref[2 * place, 48:56, :])
-        crossing = table_ref[16 + place, 0]
+        message = table_ref[0, place]
+        crossing = table_ref[0, 16 + place]
+
+        @pl.when(message < 4)
+        def _(place=place, message=message):
+            send_ref[2 * place, 0:48, :] = message_ref[message, 0:48, :]
+
+        tile = message_ref[jnp.minimum(message, 7), 48:56, :]
+        send_ref[2 * place, 48:56, :] = jnp.where(lane >= 96, top, tile)
         for base, ref in ((0, ahead_ref), (3, behind_ref)):
 
-            @pl.when(crossing == base)
-            def _(ref=ref):
-                send_ref[2 * place + 1] = ref[0:56, :]
-
-            @pl.when(crossing == base + 1)
-            def _(ref=ref):
-                send_ref[2 * place + 1, 48:56, :] = ref[56:64, :]
-
-            @pl.when(crossing == base + 2)
-            def _(ref=ref):
-                send_ref[2 * place + 1, 48:56, :] = ref[64:72, :]
-
-
-def edge_terms(table_ref, side_ref, upright_ref, received_ref, tiles_ref):
+            @pl.when((crossing >= base) & (crossing < base + 3))
+            def _(place=place, base=base, ref=ref, crossing=crossing):
+                start = pl.multiple_of(8 * (crossing - base), 8)
+                send_ref[2 * place + 1] = ref[pl.ds(start, 56), :]
+
+
+def edge_terms(table_ref, message_ref, received_ref, tiles_ref):
     lane = lane_index(1)
 
     def message(way, start, stop):
-        values = received_ref[table_ref[32 + way, 0], start:stop, :]
-        return jnp.where(table_ref[40 + way, 0] > 0, values, 0.0)
-
-    own = (
-        side_ref[0, 0:24, :], side_ref[1, 0:24, :], upright_ref[0, 0:24, :], upright_ref[1, 0:24, :],
-    )
-    own_mass = (
-        unfold_line(side_ref[0, 48:56, :]), unfold_line(side_ref[1, 48:56, :]),
-        unfold_line(upright_ref[0, 48:56, :]), unfold_line(upright_ref[1, 48:56, :]),
-    )
+        values = received_ref[table_ref[0, 32 + way], start:stop, :]
+        return jnp.where(table_ref[0, 40 + way] > 0, values, 0.0)
+
+    own = [message_ref[side, 0:24, :] for side in range(4)]
+    own_mass = [unfold_line(message_ref[side, 48:56, :]) for side in range(4)]
     near = [message(side, 0, 24) for side in range(4)]
     change = [message(side, 24, 48) for side in range(4)]
     extra = [message(side, 48, 56) for side in range(4)]
@@ -522,62 +531,97 @@
 
 
 def last_kernel(
-    table_ref, side_ref, upright_ref, received_ref, tiles_ref, mass_ref,
-    velocity_ref, height_ref, partial_ref, new_velocity_ref, new_height_ref,
-    rows, columns, inverse,
+    table_ref, message_ref, received_ref, tiles_ref,
+    velocity_far, height_far, partial_far, new_velocity_far, new_height_far,
+    rows, velocity_ref, height_ref, partial_ref, arrived, left_off,
 ):
-    level = pl.program_id(0)
     lane = lane_index(128)
-
-    @pl.when(level == 0)
-    def _():
-        plain, edge, total_mass = edge_terms(
-            table_ref, side_ref, upright_ref, received_ref, tiles_ref
+    mass_in = pltpu.make_async_copy(partial_far.at[24], partial_ref.at[24], arrived.at[3, 0])
+    mass_in.start()
+    incoming = []
+    for group in range(GROUPS):
+        part = pl.ds(LEVELS_EACH * group, LEVELS_EACH)
+        incoming.append(
+            (
+                pltpu.make_async_copy(
+                    partial_far.at[pl.ds(3 * LEVELS_EACH * group, 3 * LEVELS_EACH)],
+                    partial_ref.at[pl.ds(3 * LEVELS_EACH * group, 3 * LEVELS_EACH)],
+                    arrived.at[0, group],
+                ),
+                pltpu.make_async_copy(
+                    velocity_far.at[:, part], velocity_ref.at[:, part], arrived.at[1, group]
+                ),
+                pltpu.make_async_copy(
+                    height_far.at[part], height_ref.at[part], arrived.at[2, group]
+                ),
+            )
         )
-        rows[0] = plain[UPPER]
-        rows[1] = plain[LOWER]
-        rows[2] = edge[UPPER]
-        rows[3] = edge[LOWER]
-        stacked = jnp.concatenate(
-            [plain[LEFT], plain[RIGHT], edge[LEFT], edge[RIGHT]]
-            + [jnp.broadcast_to(total_mass[side], (16, 128)) for side in (LEFT, RIGHT)],
-            0,
-        )
-        columns[...] = jnp.transpose(stacked)
-        sides = columns[...]
-        mass = mass_ref[...]
-        mass = jnp.where(lane == 0, sides[:, 96:97], mass)
-        mass = jnp.where(lane == 127, sides[:, 112:113], mass)
-        row = lax.broadcasted_iota(jnp.int32, (128, 128), 0)
-        mass = jnp.where(row == 127, total_mass[UPPER], mass)
-        mass = jnp.where(row == 0, total_mass[LOWER], mass)
-        top = jnp.zeros((8, 128), f32)
-        for place in range(16):
-            top = jnp.maximum(top, received_ref[2 * place, 48:56, :])
-        top = jnp.max(jnp.where(lane_index(8) >= 96, top, 0.0))
-        inverse[...] = (courant / top) / mass
-
-    moved = pltpu.roll(columns[...], (128 - level) % 128, 1)
-    factor = inverse[...]
+        for copy in incoming[-1]:
+            copy.start()
+
+    plain, edge, total_mass = edge_terms(table_ref, message_ref, received_ref, tiles_ref)
+    rows[0] = plain[UPPER]
+    rows[1] = plain[LOWER]
+    rows[2] = edge[UPPER]
+    rows[3] = edge[LOWER]
+    stacked = jnp.concatenate(
+        [plain[LEFT], plain[RIGHT], edge[LEFT], edge[RIGHT]]
+        + [jnp.broadcast_to(total_mass[side], (16, 128)) for side in (LEFT, RIGHT)],
+        0,
+    )
+    columns = jnp.transpose(stacked)
+    mass_in.wait()
+    mass = partial_ref[24]
+    mass = jnp.where(lane == 0, columns[:, 96:97], mass)
+    mass = jnp.where(lane == 127, columns[:, 112:113], mass)
+    row = lax.broadcasted_iota(jnp.int32, (128, 128), 0)
+    mass = jnp.where(row == 127, total_mass[UPPER], mass)
+    mass = jnp.where(row == 0, total_mass[LOWER], mass)
+    top = jnp.zeros((8, 128), f32)
+    for place in range(16):
+        top = jnp.maximum(top, received_ref[2 * place, 48:56, :])
+    top = jnp.max(
+        jnp.where(lane_index(8) >= 96, top, 0.0), axis=(0, 1), keepdims=True
+    )
+    factor = (courant / top) / mass
     left = lane < 64
     across = tiles_ref[25, 0:1]
     ends = tiles_ref[26, 0:1]
-    for part in range(3):
-        start = 8 * part
-        plain = jnp.where(left, moved[:, start : start + 1], moved[:, start + 24 : start + 25])
-        edge = jnp.where(left, moved[:, start + 48 : start + 49], moved[:, start + 72 : start + 73])
-        value = partial_ref[part, 0] + across * plain + ends * edge
-        place = pl.ds(start + level, 1)
-        upper = tiles_ref[23] * rows[0, place, :]
-        lower = tiles_ref[24] * rows[1, place, :]
-        row = lax.broadcasted_iota(jnp.int32, (8, 128), 0)
-        upper = upper + jnp.where(row == 7, rows[2, place, :], 0.0)
-        lower = lower + jnp.where(row == 0, rows[3, place, :], 0.0)
-        value = jnp.concatenate([value[:8] + lower, value[8:120], value[120:] + upper], 0)
-        if part < 2:
-            new_velocity_ref[part, 0] = velocity_ref[part, 0] + factor * value
-        else:
-            new_height_ref[0] = height_ref[0] + factor * value
+    row = lax.broadcasted_iota(jnp.int32, (8, 128), 0)
+    outgoing = []
+    for group in range(GROUPS):
+        for copy in incoming[group]:
+            copy.wait()
+        for level in range(LEVELS_EACH * group, LEVELS_EACH * (group + 1)):
+            for part in range(3):
+                at = 8 * part + level
+                plain = jnp.where(left, columns[:, at : at + 1], columns[:, at + 24 : at + 25])
+                edge = jnp.where(
+                    left, columns[:, at + 48 : at + 49], columns[:, at + 72 : at + 73]
+                )
+                value = partial_ref[3 * level + part] + across * plain + ends * edge
+                upper = tiles_ref[23] * rows[0, at : at + 1, :]
+                lower = tiles_ref[24] * rows[1, at : at + 1, :]
+                upper = upper + jnp.where(row == 7, rows[2, at : at + 1, :], 0.0)
+                lower = lower + jnp.where(row == 0, rows[3, at : at + 1, :], 0.0)
+                value = jnp.concatenate([value[:8] + lower, value[8:120], value[120:] + upper], 0)
+                if part < 2:
+                    velocity_ref[part, level] = velocity_ref[part, level] + factor * value
+                else:
+                    height_ref[level] = height_ref[level] + factor * value
+        part = pl.ds(LEVELS_EACH * group, LEVELS_EACH)
+        for copy in (
+            pltpu.make_async_copy(
+                velocity_ref.at[:, part], new_velocity_far.at[:, part], left_off.at[0, group]
+            ),
+            pltpu.make_async_copy(
+                height_ref.at[part], new_height_far.at[part], left_off.at[1, group]
+            ),
+        ):
+            copy.start()
+            outgoing.append(copy)
+    for copy in outgoing:
+        copy.wait()
 
 
 def whole(shape, space=None):
@@ -595,56 +639,63 @@
     device = (lax.axis_index("elem") * lax.axis_size("sub") + lax.axis_index("sub")).reshape(1)
     if cols_b < 128:
         block_owner = jnp.pad(block_owner, ((0, 0), (0, 128 - cols_b)), constant_values=-1)
-    pair = pl.BlockSpec((2, 1, 128, 128), lambda level: (0, level, 0, 0))
-    single = pl.BlockSpec((1, 128, 128), lambda level: (level, 0, 0))
-    triple = pl.BlockSpec((3, 1, 128, 128), lambda level: (0, level, 0, 0))
     shape = jax.ShapeDtypeStruct
     params = pltpu.CompilerParams(
         dimension_semantics=("arbitrary",), vmem_limit_bytes=BLOCK_VMEM
     )
     vmem = pltpu.VMEM
-    side, upright, mass, table, top = pl.pallas_call(
+    far = pl.BlockSpec(memory_space=pltpu.HBM)
+    held = pl.BlockSpec(memory_space=vmem)
+    small = pl.BlockSpec(memory_space=pltpu.SMEM)
+    arrays = (
+        block_owner, velocity, thickness, coriolis, elem_mass, along_x, expand, expand_t, tiles,
+    )
+    right, left, message, mass, table, top = pl.pallas_call(
         functools.partial(edge_kernel, cols_b),
-        in_specs=[pl.BlockSpec(memory_space=pltpu.SMEM)] + [pl.BlockSpec(memory_space=vmem)] * 9,
-        out_specs=[pl.BlockSpec(memory_space=vmem)] * 5,
+        in_specs=[small] + [far] * 9,
+        out_specs=[held] * 6,
         out_shape=[
-            shape((2, 72, 128), f32), shape((2, 56, 128), f32),
-            shape((128, 128), f32), shape((48, 128), jnp.int32), shape((TOP_ROWS, 128), f32),
+            shape((72, 128), f32), shape((72, 128), f32), shape((8, 56, 128), f32),
+            shape((128, 128), f32), shape((1, 128), jnp.int32), shape((TOP_ROWS, 128), f32),
         ],
         scratch_shapes=[
             pltpu.VMEM((2, 3, 128, 128), f32), pltpu.VMEM((2, 3, 128, 128), f32),
-        ],
+        ]
+        + [pltpu.VMEM(array.shape, array.dtype) for array in arrays]
+        + [pltpu.SemaphoreType.DMA((9,))],
         compiler_params=pltpu.CompilerParams(vmem_limit_bytes=EDGE_VMEM),
         name="edge",
-    )(device, block_owner, velocity, thickness, coriolis, elem_mass, along_x, expand, expand_t, tiles)
+    )(device, *arrays)
     squares = count // 16
     same_place = [[16 * s + i for s in range(squares)] for i in range(16)]
     same_square = [[16 * s + i for i in range(16)] for s in range(squares)]
     tops = lax.all_to_all(
         top[: 8 * squares], axes, 0, 0, axis_index_groups=same_place, tiled=True
     )
-    ahead = lax.ppermute(side[1], axes, [(b, (b - 16) % count) for b in range(count)])
-    behind = lax.ppermute(side[0], axes, [(b, (b + 16) % count) for b in range(count)])
+    ahead = lax.ppermute(left, axes, [(b, (b - 16) % count) for b in range(count)])
+    behind = lax.ppermute(right, axes, [(b, (b + 16) % count) for b in range(count)])
     send = pl.pallas_call(
         pack_kernel,
-        in_specs=[whole((48, 128), pltpu.SMEM)] + [pl.BlockSpec(memory_space=pltpu.VMEM)] * 5,
-        out_specs=pl.BlockSpec(memory_space=pltpu.VMEM),
+        in_specs=[small] + [held] * 4,
+        out_specs=held,
         out_shape=shape((32, 56, 128), f32),
         compiler_params=pltpu.CompilerParams(vmem_limit_bytes=PACK_VMEM),
         name="pack",
-    )(table, side, upright, ahead, behind, tops)
+    )(table, message, ahead, behind, tops)
     received = lax.all_to_all(
         send.reshape(16, 112, 128), axes, 0, 0, axis_index_groups=same_square, tiled=True
     ).reshape(32, 56, 128)
-    partial, local_mass = pl.pallas_call(
+    pair = pl.BlockSpec((2, 1, 128, 128), lambda step: (0, jnp.minimum(step, 7), 0, 0))
+    single = pl.BlockSpec((1, 128, 128), lambda step: (jnp.minimum(step, 7), 0, 0))
+    partial = pl.pallas_call(
         block_kernel,
-        grid=(8,),
+        grid=(9,),
         in_specs=[
             pair, single, whole((1, 128, 128)), whole((128, 128)), whole((2, 128, 128)),
             whole((27, 8, 128)), whole((1, 8, 128)),
         ],
-        out_specs=[triple, whole((128, 128))],
-        out_shape=[shape((3, 8, 128, 128), f32), shape((128, 128), f32)],
+        out_specs=pl.BlockSpec((3, 128, 128), lambda step: (step, 0, 0)),
+        out_shape=shape((27, 128, 128), f32),
         scratch_shapes=[pltpu.VMEM((128, 128), f32)],
         compiler_params=params,
         cost_estimate=pl.CostEstimate(
@@ -654,21 +705,17 @@
     )(velocity, thickness, coriolis, mass, along_x, tiles, send)
     new_velocity, new_thickness = pl.pallas_call(
         last_kernel,
-        grid=(8,),
-        in_specs=[
-            whole((48, 128), pltpu.SMEM), whole((2, 72, 128)), whole((2, 56, 128)),
-            whole((32, 56, 128)), whole((27, 8, 128)), whole((128, 128)), pair, single, triple,
-        ],
-        out_specs=[pair, single],
+        in_specs=[small] + [held] * 3 + [far] * 3,
+        out_specs=[far] * 2,
         out_shape=[shape((2, 8, 128, 128), f32), shape((8, 128, 128), f32)],
         scratch_shapes=[
-            pltpu.VMEM((4, 24, 128), f32), pltpu.VMEM((128, 128), f32), pltpu.VMEM((128, 128), f32),
+            pltpu.VMEM((4, 24, 128), f32), pltpu.VMEM((2, 8, 128, 128), f32),
+            pltpu.VMEM((8, 128, 128), f32), pltpu.VMEM((25, 128, 128), f32),
+            pltpu.SemaphoreType.DMA((4, GROUPS)), pltpu.SemaphoreType.DMA((2, GROUPS)),
         ],
-        compiler_params=pltpu.CompilerParams(
-            dimension_semantics=("arbitrary",), vmem_limit_bytes=LAST_VMEM
-        ),
+        compiler_params=pltpu.CompilerParams(vmem_limit_bytes=LAST_VMEM),
         name="last",
-    )(table, side, upright, received, tiles, local_mass, velocity, thickness, partial)
+    )(table, message, received, tiles, velocity, thickness, partial)
     return new_velocity[:, :, None], new_thickness[:, None]
 
 

time: 70 us -> 70.5 us (level)
  waiting for transfers between devices: 3.1 us -> 8.83 us
  Pallas kernels: 30 us -> 25.2 us
  local copies, waits for them, and re-layouts: 2.38 us -> 1.64 us
    ppermute x2, waiting for transfers between devices: 1.53 us -> 7.57 us  [the longest x1 7.57 us: per_device(): lax.ppermute(right, axes, [(b, (b + 16) % count) for b in range(count)])]
    pallas_call x4, Pallas kernels: 30 us -> 25.2 us  [the longest x1 12.7 us: per_device(): pl.pallas_call(block_kernel, grid=(9,), in_specs=[pair, single, whole((1,...]
    squeeze x1 -> x0, local copies, waits for them, and re-layouts: 0.79 us -> none  [per_device(): side[0]]
    all_to_all x1, starting transfers between devices: 7.17 us -> 7.89 us  [per_device(): lax.all_to_all(send.reshape(16, 112, 128), axes, 0, 0, axis_index_groups=...]
    unnamed x8 -> x12, local copies, waits for them, and re-layouts: 1.59 us -> 1.64 us
  transfers between devices with their start and end apart: 4 -> 4, of which waited for: 3 -> 2; matrix products, arithmetic and copies ran while one was open for 1% -> 0% of each run, Pallas kernels for 18% -> 18%
where the time goes in v2:
time: 70.5 us; the launch traced here: 70.1 us
  starting transfers between devices  33.8 us (48%)
  Pallas kernels  25.2 us (36%)
  waiting for transfers between devices  8.83 us (13%)
  local copies, waits for them, and re-layouts  1.64 us (2%)
  between operations  0.72 us (1%)
    all_to_all x1, starting transfers between devices, per_device(): lax.all_to_all(top[:8 * squares], axes, 0, 0, axis_index_groups=same_plac...  16.5 us
    pallas_call x1, Pallas kernels, per_device(): pl.pallas_call(block_kernel, grid=(9,), in_specs=[pair, single, whole((1,...  12.7 us
    all_to_all x1, starting transfers between devices, per_device(): lax.all_to_all(send.reshape(16, 112, 128), axes, 0, 0, axis_index_groups=...  7.89 us
    ppermute x1, waiting for transfers between devices, per_device(): lax.ppermute(right, axes, [(b, (b + 16) % count) for b in range(count)])  7.57 us
    ppermute x1, starting transfers between devices, per_device(): lax.ppermute(left, axes, [(b, (b - 16) % count) for b in range(count)])  7.45 us
    pallas_call x1, Pallas kernels, per_device(): pl.pallas_call(last_kernel, in_specs=[small] + [held] * 3 + [far] * 3, ou...  5.35 us
    pallas_call x1, Pallas kernels, per_device(): pl.pallas_call(functools.partial(edge_kernel, cols_b), in_specs=[small] +...  5.16 us
    ppermute x1, starting transfers between devices, per_device(): lax.ppermute(right, axes, [(b, (b + 16) % count) for b in range(count)])  1.92 us
  transfers between devices with their start and end apart: 4, of which 2 were waited for; matrix products, arithmetic and copies ran while one was open for 0% of the time, Pallas kernels for 18%

profile of v2, /device:TPU:1, one launch (start us, length us, event | category | flops | bytes accessed | tf_op | source)
XLA Modules:
  0.0 70.1 jit_solution(2884563469875555074)
XLA Ops:
  0.6 5.2 %edge.1 = (f32[72,128]{1,0:T(8,128)}, f32[72,128]{1,0:T(8,128)}, f32[8,56,128]{2,1,0:T(8,128)}, f32[128,128]{1,0:T(8,128)}, s32[1,128]{1,0:T(1,128)}, /*index=5*/f32[256,128]{1,0:T(8,128)}) custom-call(s32[1]{0:T(128)} %bitcast.device_ref, s32[4,128]{1,0:T(4,128)} %owner_far.1, f32[2,8,128,128]{3,2,1,0:T(8,128)} %bitcast.18, f32[8,128,128]{2,1,0:T(8,128)} %bitcast.14, ...), custom_call_target="tpu_custom_call" | custom-call | tf_op jit(solution)/shard_map/edge/pallas_call | solution.py:653
  5.8 16.5 %all-to-all-start = ((f32[32,8,128]{2,1,0:T(8,128)}), f32[32,8,128]{2,1,0:T(8,128)S(1)}, u32[]{:S(2)}, u32[]{:S(2)}) async-start(f32[32,8,128]{2,1,0:T(8,128)} %bitcast.22), calls=%async_computation | async-start | bytes 262144 | tf_op jit(solution)/shard_map/all_to_all | solution.py:672
  22.3 7.4 %collective-permute-start = (f32[72,128]{1,0:T(8,128)}, f32[72,128]{1,0:T(8,128)S(1)}, u32[]{:S(2)}, u32[]{:S(2)}) collective-permute-start(f32[72,128]{1,0:T(8,128)} %get-tuple-element.12), channel_id=1, source_target_pairs={{0,496},{1,497},{2,498},{3,499},{4,500},{5,501},{6,502},{7,503},{8... | collective-permute-start | bytes 110600 | tf_op jit(solution)/shard_map/ppermute | solution.py:675
  29.8 1.9 %collective-permute-start.1 = (f32[72,128]{1,0:T(8,128)}, f32[72,128]{1,0:T(8,128)S(1)}, u32[]{:S(2)}, u32[]{:S(2)}) collective-permute-start(f32[72,128]{1,0:T(8,128)} %get-tuple-element.13), channel_id=1, source_target_pairs={{0,16},{1,17},{2,18},{3,19},{4,20},{5,21},{6,22},{7,23},{8,24},{9,... | collective-permute-start | bytes 110600 | tf_op jit(solution)/shard_map/ppermute | solution.py:676
  31.7 0.0 collective-permute-done.ahead_ref
  31.7 7.6 %collective-permute-done.1.behind_ref = f32[72,128]{1,0:T(8,128)S(1)} collective-permute-done((f32[72,128]{1,0:T(8,128)}, f32[72,128]{1,0:T(8,128)S(1)}, u32[]{:S(2)}, u32[]{:S(2)}) %collective-permute-start.1) | collective-permute-done | bytes 36896 | tf_op jit(solution)/shard_map/ppermute | solution.py:676
  39.3 0.0 all-to-all-done
  39.3 0.0 copy-start.1
  39.3 0.9 %copy-done.1 = f32[8,56,128]{2,1,0:T(8,128)S(1)} copy-done((f32[8,56,128]{2,1,0:T(8,128)S(1)}, f32[8,56,128]{2,1,0:T(8,128)}, u32[]{:S(2)}) %copy-start.1) | copy-done | bytes 229400
  40.2 0.0 copy-start.4
  40.2 0.7 copy-done.4
  40.9 1.9 %pack.1.after_ref = f32[32,56,128]{2,1,0:T(8,128)} custom-call(s32[1,128]{1,0:T(1,128)S(1)} %copy-done.4, f32[8,56,128]{2,1,0:T(8,128)S(1)} %copy-done.1, f32[72,128]{1,0:T(8,128)S(1)} %collective-permute-done.ahead_ref, f32[72,128]{1,0:T(8,128)S(1)} %collective-permute-done.1.behind_ref, f32[256,128]{1,0:T(8,128)S(1)} %bitcast.17), custom_call_target="tpu_custom_call" | custom-call | tf_op jit(solution)/shard_map/pack/pallas_call | solution.py:677
  42.8 7.9 %all-to-all-start.1 = ((f32[16,112,128]{2,1,0:T(8,128)}), f32[16,112,128]{2,1,0:T(8,128)S(1)}, u32[]{:S(2)}, u32[]{:S(2)}) async-start(f32[16,112,128]{2,1,0:T(8,128)} %bitcast.21), calls=%async_computation.1 | async-start | bytes 1835008 | tf_op jit(solution)/shard_map/all_to_all | solution.py:685
  50.7 0.0 copy-start
  50.7 0.0 copy-start.2
  50.7 0.0 copy-start.3
  50.8 0.0 copy-start.5
  50.8 12.7 %block.1.partial_far = f32[27,128,128]{2,1,0:T(8,128)} custom-call(f32[2,8,128,128]{3,2,1,0:T(8,128)} %bitcast.19, f32[8,128,128]{2,1,0:T(8,128)} %bitcast.15, f32[1,128,128]{2,1,0:T(8,128)} %coriolis_ref.1, f32[128,128]{1,0:T(8,128)} %get-tuple-element.15.mass_in_ref, f32[2,128,128]{2,1,0:T(8,128)} %constant.19.clone.along_x_far.along_x_ref, ...), custom_call_target="tpu_custom_call" | custom-call | flops 2000000000 | bytes 3200000 | tf_op jit(solution)/shard_map/block/pallas_call | solution.py:690
  63.5 1.3 %all-to-all-done.1 = f32[16,112,128]{2,1,0:T(8,128)S(1)} async-done(((f32[16,112,128]{2,1,0:T(8,128)}), f32[16,112,128]{2,1,0:T(8,128)S(1)}, u32[]{:S(2)}, u32[]{:S(2)}) %all-to-all-start.1) | async-done | bytes 917536 | tf_op jit(solution)/shard_map/all_to_all | solution.py:685
  64.7 0.0 copy-done
  64.7 0.0 copy-done.2
  64.8 0.0 copy-done.3
  64.8 0.0 copy-done.5
  64.8 5.4 %last.1 = (f32[2,8,128,128]{3,2,1,0:T(8,128)}, f32[8,128,128]{2,1,0:T(8,128)}) custom-call(s32[1,128]{1,0:T(1,128)S(1)} %copy-done.5, f32[8,56,128]{2,1,0:T(8,128)S(1)} %copy-done.2, f32[32,56,128]{2,1,0:T(8,128)S(1)} %bitcast.13, f32[27,8,128]{2,1,0:T(8,128)S(1)} %copy-done.3, f32[2,8,128,128]{3,2,1,0:T(8,128)} %bitcast.20, f32[8,128,128]{2,1,0:T(8,128)S(1)} %bitcast.16, ...), custom_call_target="tpu_custom_call" | custom-call | tf_op jit(solution)/shard_map/last/pallas_call | solution.py:706
Async XLA Ops:
  5.8 33.5 %all-to-all-start = ((f32[32,8,128]{2,1,0:T(8,128)}), f32[32,8,128]{2,1,0:T(8,128)S(1)}, u32[]{:S(2)}, u32[]{:S(2)}) async-start(f32[32,8,128]{2,1,0:T(8,128)} %bitcast.22), calls=%async_computation | async-start | bytes 262144 | tf_op jit(solution)/shard_map/all_to_all | solution.py:672
  22.3 9.4 %collective-permute-start = (f32[72,128]{1,0:T(8,128)}, f32[72,128]{1,0:T(8,128)S(1)}, u32[]{:S(2)}, u32[]{:S(2)}) collective-permute-start(f32[72,128]{1,0:T(8,128)} %get-tuple-element.12), channel_id=1, source_target_pairs={{0,496},{1,497},{2,498},{3,499},{4,500},{5,501},{6,502},{7,503},{8... | collective-permute-start | bytes 110600 | tf_op jit(solution)/shard_map/ppermute | solution.py:675
  29.8 9.5 %collective-permute-start.1 = (f32[72,128]{1,0:T(8,128)}, f32[72,128]{1,0:T(8,128)S(1)}, u32[]{:S(2)}, u32[]{:S(2)}) collective-permute-start(f32[72,128]{1,0:T(8,128)} %get-tuple-element.13), channel_id=1, source_target_pairs={{0,16},{1,17},{2,18},{3,19},{4,20},{5,21},{6,22},{7,23},{8,24},{9,... | collective-permute-start | bytes 110600 | tf_op jit(solution)/shard_map/ppermute | solution.py:676
  39.3 0.9 %copy-start.1 = (f32[8,56,128]{2,1,0:T(8,128)S(1)}, f32[8,56,128]{2,1,0:T(8,128)}, u32[]{:S(2)}) copy-start(f32[8,56,128]{2,1,0:T(8,128)} %get-tuple-element.11.message_ref) | copy-start | bytes 688132
  40.2 0.7 copy-start.4
  42.8 21.9 %all-to-all-start.1 = ((f32[16,112,128]{2,1,0:T(8,128)}), f32[16,112,128]{2,1,0:T(8,128)S(1)}, u32[]{:S(2)}, u32[]{:S(2)}) async-start(f32[16,112,128]{2,1,0:T(8,128)} %bitcast.21), calls=%async_computation.1 | async-start | bytes 1835008 | tf_op jit(solution)/shard_map/all_to_all | solution.py:685
  50.7 14.0 %copy-start = (f32[8,1,128,128]{3,2,1,0:T(8,128)S(1)}, f32[8,1,128,128]{3,2,1,0:T(8,128)}, u32[]{:S(2)}) copy-start(f32[8,1,128,128]{3,2,1,0:T(8,128)} %param.10) | copy-start | bytes 1572868
  50.7 14.0 %copy-start.2 = (f32[8,56,128]{2,1,0:T(8,128)S(1)}, f32[8,56,128]{2,1,0:T(8,128)}, u32[]{:S(2)}) copy-start(f32[8,56,128]{2,1,0:T(8,128)} %get-tuple-element.11.message_ref) | copy-start | bytes 688132
  50.7 14.0 %copy-start.3 = (f32[27,8,128]{2,1,0:T(8,128)S(1)}, f32[27,8,128]{2,1,0:T(8,128)}, u32[]{:S(2)}) copy-start(f32[27,8,128]{2,1,0:T(8,128)} %constant.22.clone.tiles_far.tiles_ref) | copy-start | bytes 331780
  50.8 14.0 %copy-start.5 = (s32[1,128]{1,0:T(1,128)S(1)}, s32[1,128]{1,0:T(1,128)}, u32[]{:S(2)}) copy-start(s32[1,128]{1,0:T(1,128)} %get-tuple-element.10.table_ref) | copy-start | bytes 1540

commit v3 on v2

--- a/solution.py
+++ b/solution.py
@@ -15,14 +15,16 @@
 MIB = 1024 * 1024
 EDGE_VMEM = 60 * MIB
 PACK_VMEM = 53 * MIB
+FILL_VMEM = 53 * MIB
 BLOCK_VMEM = 60 * MIB
 LAST_VMEM = 52 * MIB
-GROUPS = 4
+GROUPS = 2
 LEVELS_EACH = 8 // GROUPS
 axes = ("elem", "sub")
 f32 = jnp.float32
 HIGH = lax.Precision.HIGHEST
 RIGHT, LEFT, UPPER, LOWER = range(4)
+STARTS = (0, 72, 144, 200, 8, 80, 16, 88)
 steps8 = ((0, 1), (0, -1), (1, 0), (-1, 0), (1, 1), (1, -1), (-1, 1), (-1, -1))
 
 
@@ -64,7 +66,9 @@
 def constant_tables():
     along_x = np.stack([np.kron(np.eye(32), FIRST.T), np.kron(np.eye(32), SECOND.T)])
     expand = np.kron(np.eye(32), WEIGHTS[:, None])
-    tiles = np.zeros((27, 8, 128))
+    tiles = np.zeros((25, 8, 128))
+    expand_tiles = np.zeros((128, 128))
+    expand_tiles[:, :32] = expand
     for base, table in ((0, FIRST), (7, SECOND)):
         tiles[base : base + 7] = np.tile(offset_rows(table), (1, 2))[:, :, None]
     tiles[14:21] = np.tile(offset_rows(SECOND), (1, 32))[:, None, :]
@@ -79,15 +83,19 @@
     across = np.zeros(128)
     across[:5] = [*low, low[3]]
     across[123:] = [high[0], *high]
-    tiles[25] = across[None]
-    ends = np.zeros(128)
-    ends[0] = ends[127] = 1.0
-    tiles[26] = ends[None]
+    widen = np.zeros((128, 256))
+    for plane in range(24):
+        start = 128 * (plane // 12) + 10 * (plane % 12)
+        for lane in range(10):
+            widen[24 * (lane < 5) + plane, start + lane] = across[(123 + lane) % 128]
+        widen[72 + plane, start + 4] = 1.0
+        widen[48 + plane, start + 5] = 1.0
     return (
-        jnp.asarray(along_x, f32),
-        jnp.asarray(expand, f32),
-        jnp.asarray(expand.T, f32),
-        jnp.asarray(tiles, f32),
+        split_matrix(widen),
+        split_matrix(along_x),
+        jnp.asarray(
+            np.concatenate([tiles, expand_tiles.reshape(16, 8, 128), expand.T.reshape(4, 8, 128)]), f32
+        ),
     )
 
 
@@ -118,6 +126,20 @@
 
 def share_block(values):
     return share_rows(share_lanes(values))
+
+
+def split_matrix(table):
+    high = jnp.asarray(table, f32).astype(jnp.bfloat16)
+    low = (jnp.asarray(table, f32) - high.astype(f32)).astype(jnp.bfloat16)
+    return jnp.concatenate([high, high, low], -2)
+
+
+def product(values, matrix):
+    high = values.astype(jnp.bfloat16)
+    low = (values - high.astype(f32)).astype(jnp.bfloat16)
+    return jnp.dot(
+        jnp.concatenate([high, low, high], 1), matrix, preferred_element_type=f32
+    )
 
 
 def along_rows(values, tiles_ref, base):
@@ -171,6 +193,14 @@
     for part in range(4):
         line = jnp.where(lane // 32 == part, turn(tile[part : part + 1], 32 * part - 64), line)
     return line
+
+
+def mass_of_nodes(elem_mass, tiles_ref):
+    wide = tiles_ref[25:41].reshape(128, 128)[:, :32]
+    rows = jnp.dot(wide, elem_mass, precision=HIGH, preferred_element_type=f32)
+    return jnp.dot(
+        rows, tiles_ref[41:45].reshape(32, 128), precision=HIGH, preferred_element_type=f32
+    )
 
 
 def find_tables(device, owner_ref, table_ref, cols_b):
@@ -193,9 +223,9 @@
     member = device % 16
     here_rows, here_cols = rows[16:32], cols[16:32]
     down, over = here_rows - own_row, here_cols - own_col
-    inside = jnp.full((16, 1), 8, jnp.int32)
-    for number, (step_y, step_x) in enumerate(steps8):
-        inside = jnp.where((down == step_y) & (over == step_x), number, inside)
+    inside = jnp.full((16, 1), -1, jnp.int32)
+    for start, (step_y, step_x) in zip(STARTS, steps8):
+        inside = jnp.where((down == step_y) & (over == step_x), start, inside)
     crossing = jnp.full((16, 1), 6, jnp.int32)
     sixteen = lax.broadcasted_iota(jnp.int32, (16, 1), 0)
     for side, start, step_x in ((0, 32, 1), (1, 0, -1)):
@@ -243,14 +273,8 @@
 def changes(east, north, height, coriolis, mass, inverse, share, along_x_ref, tiles_ref):
     energy = 0.5 * (east * east + north * north) + height
     flux_x, flux_y = height * east, height * north
-    first_x = jnp.dot(
-        jnp.concatenate([north, energy, flux_x], 0), along_x_ref[0],
-        precision=HIGH, preferred_element_type=f32,
-    )
-    second_x = jnp.dot(
-        jnp.concatenate([east, north, height], 0), along_x_ref[1],
-        precision=HIGH, preferred_element_type=f32,
-    )
+    first_x = product(jnp.concatenate([north, energy, flux_x], 0), along_x_ref[0])
+    second_x = product(jnp.concatenate([east, north, height], 0), along_x_ref[1])
     absolute = first_x[:128] - along_rows(east, tiles_ref, 0) + coriolis
     tendencies = (
         absolute * north - first_x[128:256],
@@ -263,9 +287,7 @@
         local = share(lap * mass)
         locals_.append(local)
         smoothed.append(local * inverse)
-    second_x = jnp.dot(
-        jnp.concatenate(smoothed, 0), along_x_ref[1], precision=HIGH, preferred_element_type=f32
-    )
+    second_x = product(jnp.concatenate(smoothed, 0), along_x_ref[1])
     changed = []
     for part in range(3):
         lap = second_x[128 * part : 128 * part + 128] + along_rows(smoothed[part], tiles_ref, 7)
@@ -274,40 +296,25 @@
 
 
 def edge_kernel(
-    cols_b, device_ref, owner_far, velocity_far, height_far, coriolis_far, elem_mass_far,
-    along_x_far, expand_far, expand_t_far, tiles_far,
-    right_ref, left_ref, message_ref, mass_ref, table_ref, top_ref,
-    smooth, change, owner_ref, velocity_ref, height_ref, coriolis_ref, elem_mass_ref,
-    along_x_ref, expand_ref, expand_t_ref, tiles_ref, arrived,
+    velocity_far, height_far, coriolis_far, elem_mass_far, along_x_far, tiles_far,
+    right_ref, left_ref, lines_ref, top_ref,
+    smooth, change, velocity_ref, height_ref, coriolis_ref, elem_mass_ref,
+    along_x_ref, tiles_ref, arrived,
 ):
-    far = (
-        expand_far, elem_mass_far, expand_t_far, owner_far, height_far, velocity_far,
-        coriolis_far, tiles_far, along_x_far,
-    )
-    near = (
-        expand_ref, elem_mass_ref, expand_t_ref, owner_ref, height_ref, velocity_ref,
-        coriolis_ref, tiles_ref, along_x_ref,
-    )
+    far = (elem_mass_far, tiles_far, height_far, velocity_far, coriolis_far, along_x_far)
+    near = (elem_mass_ref, tiles_ref, height_ref, velocity_ref, coriolis_ref, along_x_ref)
     copies = [
         pltpu.make_async_copy(far[k], near[k], arrived.at[k]) for k in range(len(far))
     ]
     for copy in copies:
         copy.start()
-    for copy in copies:
+    lane = lane_index(128)
+    copies[0].wait()
+    copies[1].wait()
+    mass = mass_of_nodes(elem_mass_ref[0], tiles_ref)
+    mass_t = jnp.transpose(mass)
+    for copy in copies[2:]:
         copy.wait()
-    lane = lane_index(128)
-    top = jnp.zeros((128, 128), f32)
-    for level in range(8):
-        east, north = velocity_ref[0, level], velocity_ref[1, level]
-        top = jnp.maximum(
-            top, jnp.sqrt(east * east + north * north) + jnp.sqrt(height_ref[level])
-        )
-    top_ref[...] = jnp.broadcast_to(jnp.max(top), top_ref.shape)
-    rows = jnp.dot(expand_ref[...], elem_mass_ref[0], precision=HIGH, preferred_element_type=f32)
-    mass = jnp.dot(rows, expand_t_ref[...], precision=HIGH, preferred_element_type=f32)
-    mass_ref[...] = mass
-    find_tables(device_ref[0], owner_ref, table_ref, cols_b)
-    mass_t = jnp.transpose(mass)
     coriolis = coriolis_ref[0]
 
     def upright_band(ref_value):
@@ -338,6 +345,13 @@
             turning = repeat(upright_band(coriolis))
             band_mass = repeat(upright_band(mass))
         else:
+            top = jnp.zeros((128, 128), f32)
+            for level in range(8):
+                east, north = velocity_ref[0, level], velocity_ref[1, level]
+                top = jnp.maximum(
+                    top, jnp.sqrt(east * east + north * north) + jnp.sqrt(height_ref[level])
+                )
+            top_ref[...] = jnp.broadcast_to(jnp.max(top), top_ref.shape)
             planes = [
                 sideways_plane(lambda level, c=c: velocity_ref[c, level]) for c in (1, 0)
             ] + [sideways_plane(lambda level: height_ref[level])]
@@ -352,17 +366,17 @@
             smooth[way, target] = locals_[part]
             change[way, target] = changed[part]
 
+    sizes = (72, 72, 56, 56)
+    targets = [lines_ref.at[pl.ds(STARTS[side], sizes[side])] for side in range(4)]
     for way in range(2):
         for end in range(2):
-            side = 2 * (1 - way) + end
+            target = targets[2 * (1 - way) + end]
             for part in range(3):
                 place = pl.ds(7 + end, 8, stride=16)
-                message_ref[side, 8 * part : 8 * part + 8, :] = smooth.at[way, part][place, :]
-                message_ref[side, 24 + 8 * part : 32 + 8 * part, :] = change.at[way, part][place, :]
-    right_ref[0:48, :] = message_ref[RIGHT, 0:48, :]
-    left_ref[0:48, :] = message_ref[LEFT, 0:48, :]
+                target[8 * part : 8 * part + 8, :] = smooth.at[way, part][place, :]
+                target[24 + 8 * part : 32 + 8 * part, :] = change.at[way, part][place, :]
     mass_lines = (mass_t[127:128], mass_t[0:1], mass[127:128], mass[0:1])
-    lines = [message_ref[side, 0:48, :] for side in range(4)]
+    lines = [targets[side][0:48, :] for side in range(4)]
     ends = {}
     for side in range(4):
         local_mass = share_lanes(mass_lines[side])
@@ -375,30 +389,43 @@
         ends[LEFT, False] + turn(ends[RIGHT, False], 12),
     )
     for side in range(4):
-        tile = extras[side] + fold_line(mass_lines[side])
-        message_ref[side, 48:56, :] = tile
-        if side == RIGHT:
-            right_ref[48:56, :] = tile
-        elif side == LEFT:
-            left_ref[48:56, :] = tile
+        targets[side][48:56, :] = extras[side] + fold_line(mass_lines[side])
     for number, (along, upward) in enumerate(((UPPER, True), (LOWER, False))):
-        for across, sideways, ref in ((RIGHT, True, right_ref), (LEFT, False, left_ref)):
+        for across, sideways in ((RIGHT, True), (LEFT, False)):
             tile = ends[along, sideways] + turn(ends[across, upward], 12)
             tile = tile + turn(pack_end(lines[along][24:48], sideways), 48)
-            message_ref[4 + 2 * number + across, 48:56, :] = tile
-            ref[56 + 8 * number : 64 + 8 * number, :] = tile
+            targets[across][56 + 8 * number : 64 + 8 * number, :] = tile
+    right_ref[...] = targets[RIGHT][...]
+    left_ref[...] = targets[LEFT][...]
+
+
+def fill_kernel(
+    cols_b, device_ref, owner_ref, lines_ref, send_ref, table_ref,
+    near_ref, sem,
+):
+    find_tables(device_ref[0], owner_ref, table_ref, cols_b)
+    copy = pltpu.make_async_copy(table_ref, near_ref, sem)
+    copy.start()
+    copy.wait()
+    for place in range(16):
+        start = near_ref[0, place]
+
+        @pl.when(start >= 0)
+        def _(place=place, start=start):
+            send_ref[place, 0] = lines_ref[pl.ds(pl.multiple_of(start, 8), 56), :]
 
 
 def block_kernel(
-    velocity_ref, height_ref, coriolis_ref, mass_in_ref, along_x_ref, tiles_ref, after_ref,
-    partial_ref, inner_inverse,
+    velocity_ref, height_ref, coriolis_ref, elem_mass_ref, along_x_ref, tiles_ref, after_ref,
+    partial_ref, node_mass, inner_inverse,
 ):
     lane = lane_index(128)
     step = pl.program_id(0)
 
     @pl.when(step == 0)
     def _():
-        local_mass = share_block(mass_in_ref[...])
+        node_mass[...] = mass_of_nodes(elem_mass_ref[0], tiles_ref)
+        local_mass = share_block(node_mass[...])
         row = lax.broadcasted_iota(jnp.int32, (128, 128), 0)
         inner = (row > 0) & (row < 127) & (lane > 0) & (lane < 127)
         inner_inverse[...] = jnp.where(inner, 1.0 / local_mass, 0.0)
@@ -407,46 +434,43 @@
     def _():
         _, changed = changes(
             velocity_ref[0, 0], velocity_ref[1, 0], height_ref[0], coriolis_ref[0],
-            mass_in_ref[...], inner_inverse[...], share_block, along_x_ref, tiles_ref,
+            node_mass[...], inner_inverse[...], share_block, along_x_ref, tiles_ref,
         )
         for part in range(3):
             partial_ref[part] = changed[part]
 
     @pl.when(step == 8)
     def _():
-        partial_ref[0] = share_block(mass_in_ref[...])
-
-
-def pack_kernel(table_ref, message_ref, ahead_ref, behind_ref, tops_ref, send_ref):
+        partial_ref[0] = share_block(node_mass[...])
+
+
+def pack_kernel(table_ref, ahead_ref, behind_ref, tops_ref, send_in, send_far, crossing_ref, sem):
     lane = lane_index(8)
     top = jnp.max(tops_ref[...], axis=(0, 1), keepdims=True)[0]
     for place in range(16):
-        message = table_ref[0, place]
         crossing = table_ref[0, 16 + place]
-
-        @pl.when(message < 4)
-        def _(place=place, message=message):
-            send_ref[2 * place, 0:48, :] = message_ref[message, 0:48, :]
-
-        tile = message_ref[jnp.minimum(message, 7), 48:56, :]
-        send_ref[2 * place, 48:56, :] = jnp.where(lane >= 96, top, tile)
         for base, ref in ((0, ahead_ref), (3, behind_ref)):
 
             @pl.when((crossing >= base) & (crossing < base + 3))
             def _(place=place, base=base, ref=ref, crossing=crossing):
                 start = pl.multiple_of(8 * (crossing - base), 8)
-                send_ref[2 * place + 1] = ref[pl.ds(start, 56), :]
-
-
-def edge_terms(table_ref, message_ref, received_ref, tiles_ref):
+                crossing_ref[place] = ref[pl.ds(start, 56), :]
+
+        crossing_ref[place, 48:56, :] = jnp.where(lane >= 96, top, crossing_ref[place, 48:56, :])
+    copy = pltpu.make_async_copy(crossing_ref, send_far.at[:, 1], sem)
+    copy.start()
+    copy.wait()
+
+
+def edge_terms(table_ref, lines, received_ref, tiles_ref):
     lane = lane_index(1)
 
     def message(way, start, stop):
         values = received_ref[table_ref[0, 32 + way], start:stop, :]
         return jnp.where(table_ref[0, 40 + way] > 0, values, 0.0)
 
-    own = [message_ref[side, 0:24, :] for side in range(4)]
-    own_mass = [unfold_line(message_ref[side, 48:56, :]) for side in range(4)]
+    own = [line[0:24, :] for line in lines]
+    own_mass = [unfold_line(line[48:56, :]) for line in lines]
     near = [message(side, 0, 24) for side in range(4)]
     change = [message(side, 24, 48) for side in range(4)]
     extra = [message(side, 48, 56) for side in range(4)]
@@ -531,7 +555,7 @@
 
 
 def last_kernel(
-    table_ref, message_ref, received_ref, tiles_ref,
+    table_ref, lines_ref, received_ref, tiles_ref, widen_ref,
     velocity_far, height_far, partial_far, new_velocity_far, new_height_far,
     rows, velocity_ref, height_ref, partial_ref, arrived, left_off,
 ):
@@ -559,7 +583,8 @@
         for copy in incoming[-1]:
             copy.start()
 
-    plain, edge, total_mass = edge_terms(table_ref, message_ref, received_ref, tiles_ref)
+    lines = [lines_ref.at[pl.ds(STARTS[side], 56)] for side in range(4)]
+    plain, edge, total_mass = edge_terms(table_ref, lines, received_ref, tiles_ref)
     rows[0] = plain[UPPER]
     rows[1] = plain[LOWER]
     rows[2] = edge[UPPER]
@@ -579,14 +604,13 @@
     mass = jnp.where(row == 0, total_mass[LOWER], mass)
     top = jnp.zeros((8, 128), f32)
     for place in range(16):
-        top = jnp.maximum(top, received_ref[2 * place, 48:56, :])
+        top = jnp.maximum(top, received_ref[2 * place + 1, 48:56, :])
     top = jnp.max(
         jnp.where(lane_index(8) >= 96, top, 0.0), axis=(0, 1), keepdims=True
     )
     factor = (courant / top) / mass
-    left = lane < 64
-    across = tiles_ref[25, 0:1]
-    ends = tiles_ref[26, 0:1]
+    near_edge = (lane < 5) | (lane > 122)
+    widened = product(columns, widen_ref[...])
     row = lax.broadcasted_iota(jnp.int32, (8, 128), 0)
     outgoing = []
     for group in range(GROUPS):
@@ -595,11 +619,9 @@
         for level in range(LEVELS_EACH * group, LEVELS_EACH * (group + 1)):
             for part in range(3):
                 at = 8 * part + level
-                plain = jnp.where(left, columns[:, at : at + 1], columns[:, at + 24 : at + 25])
-                edge = jnp.where(
-                    left, columns[:, at + 48 : at + 49], columns[:, at + 72 : at + 73]
-                )
-                value = partial_ref[3 * level + part] + across * plain + ends * edge
+                half = 128 * (at // 12)
+                beside = turn(widened[:, half : half + 128], 123 - 10 * (at % 12))
+                value = partial_ref[3 * level + part] + jnp.where(near_edge, beside, 0.0)
                 upper = tiles_ref[23] * rows[0, at : at + 1, :]
                 lower = tiles_ref[24] * rows[1, at : at + 1, :]
                 upper = upper + jnp.where(row == 7, rows[2, at : at + 1, :], 0.0)
@@ -635,7 +657,7 @@
     count = 4 * cols_b
     velocity = velocity[:, :, 0]
     thickness = thickness[:, 0]
-    along_x, expand, expand_t, tiles = constant_tables()
+    widen, along_x, tiles = constant_tables()
     device = (lax.axis_index("elem") * lax.axis_size("sub") + lax.axis_index("sub")).reshape(1)
     if cols_b < 128:
         block_owner = jnp.pad(block_owner, ((0, 0), (0, 128 - cols_b)), constant_values=-1)
@@ -647,25 +669,23 @@
     far = pl.BlockSpec(memory_space=pltpu.HBM)
     held = pl.BlockSpec(memory_space=vmem)
     small = pl.BlockSpec(memory_space=pltpu.SMEM)
-    arrays = (
-        block_owner, velocity, thickness, coriolis, elem_mass, along_x, expand, expand_t, tiles,
-    )
-    right, left, message, mass, table, top = pl.pallas_call(
-        functools.partial(edge_kernel, cols_b),
-        in_specs=[small] + [far] * 9,
-        out_specs=[held] * 6,
+    arrays = (velocity, thickness, coriolis, elem_mass, along_x, tiles)
+    right, left, lines, top = pl.pallas_call(
+        edge_kernel,
+        in_specs=[far] * 6,
+        out_specs=[held] * 4,
         out_shape=[
-            shape((72, 128), f32), shape((72, 128), f32), shape((8, 56, 128), f32),
-            shape((128, 128), f32), shape((1, 128), jnp.int32), shape((TOP_ROWS, 128), f32),
+            shape((72, 128), f32), shape((72, 128), f32), shape((256, 128), f32),
+            shape((TOP_ROWS, 128), f32),
         ],
         scratch_shapes=[
             pltpu.VMEM((2, 3, 128, 128), f32), pltpu.VMEM((2, 3, 128, 128), f32),
         ]
         + [pltpu.VMEM(array.shape, array.dtype) for array in arrays]
-        + [pltpu.SemaphoreType.DMA((9,))],
+        + [pltpu.SemaphoreType.DMA((6,))],
         compiler_params=pltpu.CompilerParams(vmem_limit_bytes=EDGE_VMEM),
         name="edge",
-    )(device, *arrays)
+    )(*arrays)
     squares = count // 16
     same_place = [[16 * s + i for s in range(squares)] for i in range(16)]
     same_square = [[16 * s + i for i in range(16)] for s in range(squares)]
@@ -674,14 +694,26 @@
     )
     ahead = lax.ppermute(left, axes, [(b, (b - 16) % count) for b in range(count)])
     behind = lax.ppermute(right, axes, [(b, (b + 16) % count) for b in range(count)])
+    send, table = pl.pallas_call(
+        functools.partial(fill_kernel, cols_b),
+        in_specs=[small] + [held] * 2,
+        out_specs=[held] * 2,
+        out_shape=[shape((16, 2, 56, 128), f32), shape((1, 128), jnp.int32)],
+        scratch_shapes=[pltpu.SMEM((1, 128), jnp.int32), pltpu.SemaphoreType.DMA(())],
+        compiler_params=pltpu.CompilerParams(vmem_limit_bytes=FILL_VMEM),
+        cost_estimate=pl.CostEstimate(flops=0, bytes_accessed=2_000_000, transcendentals=0),
+        name="fill",
+    )(device, block_owner, lines)
     send = pl.pallas_call(
         pack_kernel,
-        in_specs=[small] + [held] * 4,
-        out_specs=held,
-        out_shape=shape((32, 56, 128), f32),
+        in_specs=[small] + [held] * 3 + [far],
+        out_specs=far,
+        out_shape=shape((16, 2, 56, 128), f32),
+        input_output_aliases={4: 0},
+        scratch_shapes=[pltpu.VMEM((16, 56, 128), f32), pltpu.SemaphoreType.DMA(())],
         compiler_params=pltpu.CompilerParams(vmem_limit_bytes=PACK_VMEM),
         name="pack",
-    )(table, message, ahead, behind, tops)
+    )(table, ahead, behind, tops, send)
     received = lax.all_to_all(
         send.reshape(16, 112, 128), axes, 0, 0, axis_index_groups=same_square, tiled=True
     ).reshape(32, 56, 128)
@@ -691,21 +723,21 @@
         block_kernel,
         grid=(9,),
         in_specs=[
-            pair, single, whole((1, 128, 128)), whole((128, 128)), whole((2, 128, 128)),
-            whole((27, 8, 128)), whole((1, 8, 128)),
+            pair, single, whole((1, 128, 128)), whole((1, 32, 32)), whole((2, 384, 128)),
+            whole((45, 8, 128)), whole((1, 8, 128)),
         ],
         out_specs=pl.BlockSpec((3, 128, 128), lambda step: (step, 0, 0)),
         out_shape=shape((27, 128, 128), f32),
-        scratch_shapes=[pltpu.VMEM((128, 128), f32)],
+        scratch_shapes=[pltpu.VMEM((128, 128), f32), pltpu.VMEM((128, 128), f32)],
         compiler_params=params,
         cost_estimate=pl.CostEstimate(
             flops=2_000_000_000, bytes_accessed=3_200_000, transcendentals=0
         ),
         name="block",
-    )(velocity, thickness, coriolis, mass, along_x, tiles, send)
+    )(velocity, thickness, coriolis, elem_mass, along_x, tiles, send.reshape(32, 56, 128))
     new_velocity, new_thickness = pl.pallas_call(
         last_kernel,
-        in_specs=[small] + [held] * 3 + [far] * 3,
+        in_specs=[small] + [held] * 4 + [far] * 3,
         out_specs=[far] * 2,
         out_shape=[shape((2, 8, 128, 128), f32), shape((8, 128, 128), f32)],
         scratch_shapes=[
@@ -715,7 +747,7 @@
         ],
         compiler_params=pltpu.CompilerParams(vmem_limit_bytes=LAST_VMEM),
         name="last",
-    )(table, message, received, tiles, velocity, thickness, partial)
+    )(table, lines, received, tiles, widen, velocity, thickness, partial)
     return new_velocity[:, :, None], new_thickness[:, None]
 
 

time: 70.5 us -> 66.2 us (0.939)
  Pallas kernels: 25.2 us -> 21.3 us
  local copies, waits for them, and re-layouts: 1.64 us -> 0.93 us
    pallas_call x1, Pallas kernels: 12.7 us -> 9.85 us  [per_device(): pl.pallas_call(block_kernel, grid=(9,), in_specs=[pair, single, whole((1,...]
    all_to_all x1, waiting for transfers between devices: 1.25 us -> 4.12 us  [per_device(): lax.all_to_all(send.reshape(16, 112, 128), axes, 0, 0, axis_index_groups=...]
    ppermute x1, waiting for transfers between devices: 7.57 us -> 4.75 us  [per_device(): lax.ppermute(right, axes, [(b, (b + 16) % count) for b in range(count)])]
    pallas_call x3 -> x4, Pallas kernels: 12.4 us -> 11.5 us  [the longest x1 4.41 us: per_device(): pl.pallas_call(edge_kernel, in_specs=[far] * 6, out_specs=[held] * 4, out...]
    unnamed x12, local copies, waits for them, and re-layouts: 1.64 us -> 0.93 us
where the time goes in v3:
time: 66.2 us; the launch traced here: 65.7 us
  starting transfers between devices  33.8 us (51%)
  Pallas kernels  21.3 us (32%)
  waiting for transfers between devices  8.88 us (13%)
  local copies, waits for them, and re-layouts  0.93 us (1%)
  between operations  0.76 us (1%)
    all_to_all x1, starting transfers between devices, per_device(): lax.all_to_all(top[:8 * squares], axes, 0, 0, axis_index_groups=same_plac...  16.5 us
    pallas_call x1, Pallas kernels, per_device(): pl.pallas_call(block_kernel, grid=(9,), in_specs=[pair, single, whole((1,...  9.85 us
    all_to_all x1, starting transfers between devices, per_device(): lax.all_to_all(send.reshape(16, 112, 128), axes, 0, 0, axis_index_groups=...  7.91 us
    ppermute x1, starting transfers between devices, per_device(): lax.ppermute(left, axes, [(b, (b - 16) % count) for b in range(count)])  7.45 us
    ppermute x1, waiting for transfers between devices, per_device(): lax.ppermute(right, axes, [(b, (b + 16) % count) for b in range(count)])  4.75 us
    pallas_call x1, Pallas kernels, per_device(): pl.pallas_call(edge_kernel, in_specs=[far] * 6, out_specs=[held] * 4, out...  4.41 us
    all_to_all x1, waiting for transfers between devices, per_device(): lax.all_to_all(send.reshape(16, 112, 128), axes, 0, 0, axis_index_groups=...  4.12 us
    pallas_call x1, Pallas kernels, per_device(): pl.pallas_call(last_kernel, in_specs=[small] + [held] * 4 + [far] * 3, ou...  3.49 us
  transfers between devices with their start and end apart: 4, of which 2 were waited for; matrix products, arithmetic and copies ran while one was open for 0% of the time, Pallas kernels for 18%

profile of v3, /device:TPU:1, one launch (start us, length us, event | category | flops | bytes accessed | tf_op | source)
XLA Modules:
  0.0 65.7 jit_solution(15905039097670812150)
XLA Ops:
  0.6 0.0 copy-start.5
  0.6 4.4 %edge.1 = (f32[72,128]{1,0:T(8,128)}, f32[72,128]{1,0:T(8,128)}, f32[256,128]{1,0:T(8,128)}, f32[256,128]{1,0:T(8,128)}) custom-call(f32[2,8,128,128]{3,2,1,0:T(8,128)} %bitcast.19, f32[8,128,128]{2,1,0:T(8,128)} %bitcast.15, f32[1,128,128]{2,1,0:T(8,128)} %coriolis_ref.1, f32[1,32,32]{2,1,0:T(8,128)} %elem_mass_ref.1, ...), custom_call_target="tpu_custom_call" | custom-call | tf_op jit(solution)/shard_map/edge/pallas_call | solution.py:673
  5.1 16.5 %all-to-all-start = ((f32[32,8,128]{2,1,0:T(8,128)}), f32[32,8,128]{2,1,0:T(8,128)S(1)}, u32[]{:S(2)}, u32[]{:S(2)}) async-start(f32[32,8,128]{2,1,0:T(8,128)} %bitcast.24), calls=%async_computation | async-start | bytes 262144 | tf_op jit(solution)/shard_map/all_to_all | solution.py:692
  21.6 7.4 %collective-permute-start = (f32[72,128]{1,0:T(8,128)}, f32[72,128]{1,0:T(8,128)S(1)}, u32[]{:S(2)}, u32[]{:S(2)}) collective-permute-start(f32[72,128]{1,0:T(8,128)} %get-tuple-element.12), channel_id=1, source_target_pairs={{0,496},{1,497},{2,498},{3,499},{4,500},{5,501},{6,502},{7,503},{8... | collective-permute-start | bytes 110600 | tf_op jit(solution)/shard_map/ppermute | solution.py:695
  29.0 1.9 %collective-permute-start.1 = (f32[72,128]{1,0:T(8,128)}, f32[72,128]{1,0:T(8,128)S(1)}, u32[]{:S(2)}, u32[]{:S(2)}) collective-permute-start(f32[72,128]{1,0:T(8,128)} %get-tuple-element.13), channel_id=1, source_target_pairs={{0,16},{1,17},{2,18},{3,19},{4,20},{5,21},{6,22},{7,23},{8,24},{9,... | collective-permute-start | bytes 110600 | tf_op jit(solution)/shard_map/ppermute | solution.py:696
  31.0 0.0 copy-done.5
  31.0 0.0 copy-start.2
  31.0 0.9 %copy-done.2 = f32[256,128]{1,0:T(8,128)S(1)} copy-done((f32[256,128]{1,0:T(8,128)S(1)}, f32[256,128]{1,0:T(8,128)}, u32[]{:S(2)}) %copy-start.2) | copy-done | bytes 131096
  31.9 1.9 %fill.1 = (f32[16,2,56,128]{3,2,1,0:T(8,128)}, s32[1,128]{1,0:T(1,128)S(1)}) custom-call(s32[1]{0:T(128)} %bitcast.device_ref, s32[4,128]{1,0:T(4,128)S(1)} %copy-done.5, f32[256,128]{1,0:T(8,128)S(1)} %copy-done.2), custom_call_target="tpu_custom_call" | custom-call | bytes 2000000 | tf_op jit(solution)/shard_map/fill/pallas_call | solution.py:697
  33.8 0.0 collective-permute-done.ahead_ref
  33.8 4.8 %collective-permute-done.1.behind_ref = f32[72,128]{1,0:T(8,128)S(1)} collective-permute-done((f32[72,128]{1,0:T(8,128)}, f32[72,128]{1,0:T(8,128)S(1)}, u32[]{:S(2)}, u32[]{:S(2)}) %collective-permute-start.1) | collective-permute-done | bytes 36896 | tf_op jit(solution)/shard_map/ppermute | solution.py:696
  38.5 0.0 all-to-all-done
  38.5 1.7 %pack.1 = f32[16,2,56,128]{3,2,1,0:T(8,128)} custom-call(s32[1,128]{1,0:T(1,128)S(1)} %get-tuple-element.11.table_ref, f32[72,128]{1,0:T(8,128)S(1)} %collective-permute-done.ahead_ref, f32[72,128]{1,0:T(8,128)S(1)} %collective-permute-done.1.behind_ref, f32[256,128]{1,0:T(8,128)S(1)} %bitcast.18, ...), custom_call_target="tpu_custom_call", output_to_operand_aliasing={{}: (4, {})} | custom-call | tf_op jit(solution)/shard_map/pack/pallas_call | solution.py:707
  40.2 7.9 %all-to-all-start.1 = ((f32[16,112,128]{2,1,0:T(8,128)}), f32[16,112,128]{2,1,0:T(8,128)S(1)}, u32[]{:S(2)}, u32[]{:S(2)}) async-start(f32[16,112,128]{2,1,0:T(8,128)} %bitcast.22), calls=%async_computation.1 | async-start | bytes 1835008 | tf_op jit(solution)/shard_map/all_to_all | solution.py:717
  48.1 0.0 copy-start.1
  48.2 0.0 copy-start.3
  48.2 0.0 copy-start.4
  48.2 9.9 %block.1.partial_far = f32[27,128,128]{2,1,0:T(8,128)} custom-call(f32[2,8,128,128]{3,2,1,0:T(8,128)} %bitcast.20, f32[8,128,128]{2,1,0:T(8,128)} %bitcast.16, f32[1,128,128]{2,1,0:T(8,128)} %coriolis_ref.1, f32[1,32,32]{2,1,0:T(8,128)} %elem_mass_ref.1, bf16[2,384,128]{2,1,0:T(8,128)(2,1)} %constant.28.along_x_far.along_x_ref, ...), custom_call_target="tpu_custom_call" | custom-call | flops 2000000000 | bytes 3200000 | tf_op jit(solution)/shard_map/block/pallas_call | solution.py:722
  58.0 4.1 %all-to-all-done.1 = f32[16,112,128]{2,1,0:T(8,128)S(1)} async-done(((f32[16,112,128]{2,1,0:T(8,128)}), f32[16,112,128]{2,1,0:T(8,128)S(1)}, u32[]{:S(2)}, u32[]{:S(2)}) %all-to-all-start.1) | async-done | bytes 917536 | tf_op jit(solution)/shard_map/all_to_all | solution.py:717
  62.2 0.0 copy-done
  62.2 0.0 copy-done.1
  62.2 0.0 copy-done.3
  62.2 0.0 copy-done.4
  62.2 3.5 %last.1 = (f32[2,8,128,128]{3,2,1,0:T(8,128)}, f32[8,128,128]{2,1,0:T(8,128)}) custom-call(s32[1,128]{1,0:T(1,128)S(1)} %get-tuple-element.11.table_ref, f32[256,128]{1,0:T(8,128)S(1)} %copy-done.3, f32[32,56,128]{2,1,0:T(8,128)S(1)} %bitcast.14, f32[45,8,128]{2,1,0:T(8,128)S(1)} %copy-done.1, bf16[384,256]{1,0:T(8,128)(2,1)S(1)} %copy-done.4, ...), custom_call_target="tpu_custom_call" | custom-call | tf_op jit(solution)/shard_map/last/pallas_call | solution.py:738
  (1 shorter events, 0.0 us)
Async XLA Ops:
  0.6 30.3 %copy-start.5 = (s32[4,128]{1,0:T(4,128)S(1)}, s32[4,128]{1,0:T(4,128)}, u32[]{:S(2)}) copy-start(s32[4,128]{1,0:T(4,128)} %owner_ref.1) | copy-start | bytes 6148
  5.1 33.5 %all-to-all-start = ((f32[32,8,128]{2,1,0:T(8,128)}), f32[32,8,128]{2,1,0:T(8,128)S(1)}, u32[]{:S(2)}, u32[]{:S(2)}) async-start(f32[32,8,128]{2,1,0:T(8,128)} %bitcast.24), calls=%async_computation | async-start | bytes 262144 | tf_op jit(solution)/shard_map/all_to_all | solution.py:692
  21.6 12.2 %collective-permute-start = (f32[72,128]{1,0:T(8,128)}, f32[72,128]{1,0:T(8,128)S(1)}, u32[]{:S(2)}, u32[]{:S(2)}) collective-permute-start(f32[72,128]{1,0:T(8,128)} %get-tuple-element.12), channel_id=1, source_target_pairs={{0,496},{1,497},{2,498},{3,499},{4,500},{5,501},{6,502},{7,503},{8... | collective-permute-start | bytes 110600 | tf_op jit(solution)/shard_map/ppermute | solution.py:695
  29.0 9.5 %collective-permute-start.1 = (f32[72,128]{1,0:T(8,128)}, f32[72,128]{1,0:T(8,128)S(1)}, u32[]{:S(2)}, u32[]{:S(2)}) collective-permute-start(f32[72,128]{1,0:T(8,128)} %get-tuple-element.13), channel_id=1, source_target_pairs={{0,16},{1,17},{2,18},{3,19},{4,20},{5,21},{6,22},{7,23},{8,24},{9,... | collective-permute-start | bytes 110600 | tf_op jit(solution)/shard_map/ppermute | solution.py:696
  31.0 0.9 %copy-start.2 = (f32[256,128]{1,0:T(8,128)S(1)}, f32[256,128]{1,0:T(8,128)}, u32[]{:S(2)}) copy-start(f32[256,128]{1,0:T(8,128)} %get-tuple-element.10.lines_ref) | copy-start | bytes 393220
  40.2 21.9 %all-to-all-start.1 = ((f32[16,112,128]{2,1,0:T(8,128)}), f32[16,112,128]{2,1,0:T(8,128)S(1)}, u32[]{:S(2)}, u32[]{:S(2)}) async-start(f32[16,112,128]{2,1,0:T(8,128)} %bitcast.22), calls=%async_computation.1 | async-start | bytes 1835008 | tf_op jit(solution)/shard_map/all_to_all | solution.py:717
  48.1 14.0 %copy-start = (f32[8,1,128,128]{3,2,1,0:T(8,128)S(1)}, f32[8,1,128,128]{3,2,1,0:T(8,128)}, u32[]{:S(2)}) copy-start(f32[8,1,128,128]{3,2,1,0:T(8,128)} %param.11) | copy-start | bytes 1572868
  48.1 14.0 %copy-start.1 = (f32[45,8,128]{2,1,0:T(8,128)S(1)}, f32[45,8,128]{2,1,0:T(8,128)}, u32[]{:S(2)}) copy-start(f32[45,8,128]{2,1,0:T(8,128)} %constant.19.clone.tiles_far.tiles_ref) | copy-start | bytes 552964
  48.2 14.0 %copy-start.3 = (f32[256,128]{1,0:T(8,128)S(1)}, f32[256,128]{1,0:T(8,128)}, u32[]{:S(2)}) copy-start(f32[256,128]{1,0:T(8,128)} %get-tuple-element.10.lines_ref) | copy-start | bytes 393220
  48.2 14.0 %copy-start.4 = (bf16[384,256]{1,0:T(8,128)(2,1)S(1)}, bf16[384,256]{1,0:T(8,128)(2,1)}, u32[]{:S(2)}) copy-start(bf16[384,256]{1,0:T(8,128)(2,1)} %constant.33.widen_ref) | copy-start | bytes 589828

commit v4 on v3

--- a/solution.py
+++ b/solution.py
@@ -11,13 +11,12 @@
 
 courant = 0.1
 hyper_coef = 0.002
-TOP_ROWS = 256
+TOP_ROWS = 8
 MIB = 1024 * 1024
 EDGE_VMEM = 60 * MIB
-PACK_VMEM = 53 * MIB
-FILL_VMEM = 53 * MIB
+PACK_VMEM = 52 * MIB
 BLOCK_VMEM = 60 * MIB
-LAST_VMEM = 52 * MIB
+LAST_VMEM = 51 * MIB
 GROUPS = 2
 LEVELS_EACH = 8 // GROUPS
 axes = ("elem", "sub")
@@ -226,18 +225,26 @@
     inside = jnp.full((16, 1), -1, jnp.int32)
     for start, (step_y, step_x) in zip(STARTS, steps8):
         inside = jnp.where((down == step_y) & (over == step_x), start, inside)
-    crossing = jnp.full((16, 1), 6, jnp.int32)
+    crossing = jnp.full((16, 1), -1, jnp.int32)
     sixteen = lax.broadcasted_iota(jnp.int32, (16, 1), 0)
-    for side, start, step_x in ((0, 32, 1), (1, 0, -1)):
+    sources = []
+    for side, begin, step_x in ((RIGHT, 32, 1), (LEFT, 0, -1)):
+        there_rows, there_cols = rows[begin : begin + 16], cols[begin : begin + 16]
+        beside = there_cols == (own_col + step_x + cols_b) % cols_b
         picked = sixteen == member
         their = jnp.sum(
-            jnp.where(picked, place[start : start + 16], 0).astype(f32), axis=0, keepdims=True
+            jnp.where(picked, place[begin : begin + 16], 0).astype(f32), axis=0, keepdims=True
         ).astype(jnp.int32)
         their_row, their_col = their // 128, their % 128
-        beside = their_col == (here_cols + step_x + cols_b) % cols_b
+        facing = here_cols == (their_col - step_x + cols_b) % cols_b
         for number, step_y in enumerate((0, 1, -1)):
-            crossing = jnp.where(
-                beside & (here_rows - their_row == step_y), 3 * side + number, crossing
+            start = STARTS[side] if step_y == 0 else STARTS[side] + 8 * number
+            crossing = jnp.where(beside & (there_rows - own_row == step_y), start, crossing)
+            found = facing & (their_row - here_rows == step_y)
+            sources.append(
+                jnp.sum(jnp.where(found, sixteen, 0).astype(f32), axis=0, keepdims=True).astype(
+                    jnp.int32
+                )
             )
     way = lax.broadcasted_iota(jnp.int32, (8, 1), 0)
     step_y = jnp.zeros((8, 1), jnp.int32)
@@ -253,9 +260,13 @@
         found = found + jnp.where((near_row == row) & (near_col == lane), line, 0.0)
     found = jnp.sum(found, axis=1, keepdims=True).astype(jnp.int32)
     there = (near_row >= 0) & (near_row < 4)
-    slot = 2 * (found % 16) + jnp.where(found // 16 == square, 0, 1)
-    column = jnp.concatenate([inside, crossing, slot, there.astype(jnp.int32)], 0).astype(f32)
-    picked = lax.broadcasted_iota(jnp.int32, (48, 128), 0) == lane_index(48)
+    slot = 2 * (found % 16)
+    kind = jnp.where(there, jnp.where(found // 16 == square, 1, 2), 0)
+    ahead_of = jnp.where(way == 0, sources[0], 0)
+    for number in range(1, 6):
+        ahead_of = jnp.where(way == number, sources[number], ahead_of)
+    column = jnp.concatenate([inside, crossing, slot, kind, ahead_of], 0).astype(f32)
+    picked = lax.broadcasted_iota(jnp.int32, (56, 128), 0) == lane_index(56)
     table_ref[...] = jnp.sum(jnp.where(picked, column, 0.0), axis=0, keepdims=True).astype(
         jnp.int32
     )
@@ -296,13 +307,18 @@
 
 
 def edge_kernel(
+    cols_b, device_ref, owner_far,
     velocity_far, height_far, coriolis_far, elem_mass_far, along_x_far, tiles_far,
-    right_ref, left_ref, lines_ref, top_ref,
-    smooth, change, velocity_ref, height_ref, coriolis_ref, elem_mass_ref,
+    lines_ref, send_ref, table_ref,
+    smooth, change, owner_ref, near_ref, velocity_ref, height_ref, coriolis_ref, elem_mass_ref,
     along_x_ref, tiles_ref, arrived,
 ):
-    far = (elem_mass_far, tiles_far, height_far, velocity_far, coriolis_far, along_x_far)
-    near = (elem_mass_ref, tiles_ref, height_ref, velocity_ref, coriolis_ref, along_x_ref)
+    far = (
+        owner_far, elem_mass_far, tiles_far, height_far, velocity_far, coriolis_far, along_x_far,
+    )
+    near = (
+        owner_ref, elem_mass_ref, tiles_ref, height_ref, velocity_ref, coriolis_ref, along_x_ref,
+    )
     copies = [
         pltpu.make_async_copy(far[k], near[k], arrived.at[k]) for k in range(len(far))
     ]
@@ -310,10 +326,14 @@
         copy.start()
     lane = lane_index(128)
     copies[0].wait()
+    find_tables(device_ref[0], owner_ref, table_ref, cols_b)
+    table_copy = pltpu.make_async_copy(table_ref, near_ref, arrived.at[7])
+    table_copy.start()
     copies[1].wait()
+    copies[2].wait()
     mass = mass_of_nodes(elem_mass_ref[0], tiles_ref)
     mass_t = jnp.transpose(mass)
-    for copy in copies[2:]:
+    for copy in copies[3:]:
         copy.wait()
     coriolis = coriolis_ref[0]
 
@@ -351,7 +371,7 @@
                 top = jnp.maximum(
                     top, jnp.sqrt(east * east + north * north) + jnp.sqrt(height_ref[level])
                 )
-            top_ref[...] = jnp.broadcast_to(jnp.max(top), top_ref.shape)
+            top = jnp.max(top, axis=(0, 1), keepdims=True)
             planes = [
                 sideways_plane(lambda level, c=c: velocity_ref[c, level]) for c in (1, 0)
             ] + [sideways_plane(lambda level: height_ref[level])]
@@ -395,24 +415,17 @@
             tile = ends[along, sideways] + turn(ends[across, upward], 12)
             tile = tile + turn(pack_end(lines[along][24:48], sideways), 48)
             targets[across][56 + 8 * number : 64 + 8 * number, :] = tile
-    right_ref[...] = targets[RIGHT][...]
-    left_ref[...] = targets[LEFT][...]
-
-
-def fill_kernel(
-    cols_b, device_ref, owner_ref, lines_ref, send_ref, table_ref,
-    near_ref, sem,
-):
-    find_tables(device_ref[0], owner_ref, table_ref, cols_b)
-    copy = pltpu.make_async_copy(table_ref, near_ref, sem)
-    copy.start()
-    copy.wait()
+    table_copy.wait()
+    after = lane_index(8) >= 96
     for place in range(16):
-        start = near_ref[0, place]
-
-        @pl.when(start >= 0)
-        def _(place=place, start=start):
-            send_ref[place, 0] = lines_ref[pl.ds(pl.multiple_of(start, 8), 56), :]
+        for part in range(2):
+            start = near_ref[0, 16 * part + place]
+
+            @pl.when(start >= 0)
+            def _(place=place, part=part, start=start):
+                send_ref[place, part] = lines_ref[pl.ds(pl.multiple_of(start, 8), 56), :]
+
+        send_ref[place, 0, 48:56, :] = jnp.where(after, top, send_ref[place, 0, 48:56, :])
 
 
 def block_kernel(
@@ -444,30 +457,30 @@
         partial_ref[0] = share_block(node_mass[...])
 
 
-def pack_kernel(table_ref, ahead_ref, behind_ref, tops_ref, send_in, send_far, crossing_ref, sem):
-    lane = lane_index(8)
-    top = jnp.max(tops_ref[...], axis=(0, 1), keepdims=True)[0]
+def pack_kernel(table_ref, received_ref, after_ref, ahead_ref, behind_ref, top_ref):
+    top = jnp.zeros((8, 128), f32)
     for place in range(16):
-        crossing = table_ref[0, 16 + place]
-        for base, ref in ((0, ahead_ref), (3, behind_ref)):
-
-            @pl.when((crossing >= base) & (crossing < base + 3))
-            def _(place=place, base=base, ref=ref, crossing=crossing):
-                start = pl.multiple_of(8 * (crossing - base), 8)
-                crossing_ref[place] = ref[pl.ds(start, 56), :]
-
-        crossing_ref[place, 48:56, :] = jnp.where(lane >= 96, top, crossing_ref[place, 48:56, :])
-    copy = pltpu.make_async_copy(crossing_ref, send_far.at[:, 1], sem)
-    copy.start()
-    copy.wait()
-
-
-def edge_terms(table_ref, lines, received_ref, tiles_ref):
+        top = jnp.maximum(top, received_ref[2 * place, 48:56, :])
+    top = jnp.max(jnp.where(lane_index(8) >= 96, top, 0.0), axis=(0, 1), keepdims=True)
+    top_ref[...] = jnp.broadcast_to(top, top_ref.shape)
+    for base, ref in ((48, ahead_ref), (51, behind_ref)):
+        ref[0:56, :] = received_ref[2 * table_ref[0, base] + 1]
+        ref[56:64, :] = received_ref[2 * table_ref[0, base + 1] + 1, 48:56, :]
+        ref[64:72, :] = received_ref[2 * table_ref[0, base + 2] + 1, 48:56, :]
+
+
+def edge_terms(table_ref, lines, received_ref, ahead_ref, behind_ref, tiles_ref):
     lane = lane_index(1)
 
     def message(way, start, stop):
+        kind = table_ref[0, 40 + way]
         values = received_ref[table_ref[0, 32 + way], start:stop, :]
-        return jnp.where(table_ref[0, 40 + way] > 0, values, 0.0)
+        step_y, step_x = steps8[way]
+        if step_x != 0:
+            crossed = ahead_ref if step_x > 0 else behind_ref
+            shift = (0, 16, 8)[step_y]
+            values = jnp.where(kind == 2, crossed[start + shift : stop + shift, :], values)
+        return jnp.where(kind > 0, values, 0.0)
 
     own = [line[0:24, :] for line in lines]
     own_mass = [unfold_line(line[48:56, :]) for line in lines]
@@ -555,7 +568,7 @@
 
 
 def last_kernel(
-    table_ref, lines_ref, received_ref, tiles_ref, widen_ref,
+    table_ref, lines_ref, received_ref, ahead_ref, behind_ref, tops_ref, tiles_ref, widen_ref,
     velocity_far, height_far, partial_far, new_velocity_far, new_height_far,
     rows, velocity_ref, height_ref, partial_ref, arrived, left_off,
 ):
@@ -584,7 +597,9 @@
             copy.start()
 
     lines = [lines_ref.at[pl.ds(STARTS[side], 56)] for side in range(4)]
-    plain, edge, total_mass = edge_terms(table_ref, lines, received_ref, tiles_ref)
+    plain, edge, total_mass = edge_terms(
+        table_ref, lines, received_ref, ahead_ref, behind_ref, tiles_ref
+    )
     rows[0] = plain[UPPER]
     rows[1] = plain[LOWER]
     rows[2] = edge[UPPER]
@@ -602,12 +617,7 @@
     row = lax.broadcasted_iota(jnp.int32, (128, 128), 0)
     mass = jnp.where(row == 127, total_mass[UPPER], mass)
     mass = jnp.where(row == 0, total_mass[LOWER], mass)
-    top = jnp.zeros((8, 128), f32)
-    for place in range(16):
-        top = jnp.maximum(top, received_ref[2 * place + 1, 48:56, :])
-    top = jnp.max(
-        jnp.where(lane_index(8) >= 96, top, 0.0), axis=(0, 1), keepdims=True
-    )
+    top = jnp.max(tops_ref[...], axis=(0, 1), keepdims=True)
     factor = (courant / top) / mass
     near_edge = (lane < 5) | (lane > 122)
     widened = product(columns, widen_ref[...])
@@ -669,51 +679,26 @@
     far = pl.BlockSpec(memory_space=pltpu.HBM)
     held = pl.BlockSpec(memory_space=vmem)
     small = pl.BlockSpec(memory_space=pltpu.SMEM)
-    arrays = (velocity, thickness, coriolis, elem_mass, along_x, tiles)
-    right, left, lines, top = pl.pallas_call(
-        edge_kernel,
-        in_specs=[far] * 6,
-        out_specs=[held] * 4,
+    arrays = (block_owner, velocity, thickness, coriolis, elem_mass, along_x, tiles)
+    lines, send, table = pl.pallas_call(
+        functools.partial(edge_kernel, cols_b),
+        in_specs=[small] + [far] * 7,
+        out_specs=[held] * 3,
         out_shape=[
-            shape((72, 128), f32), shape((72, 128), f32), shape((256, 128), f32),
-            shape((TOP_ROWS, 128), f32),
+            shape((256, 128), f32), shape((16, 2, 56, 128), f32), shape((1, 128), jnp.int32),
         ],
         scratch_shapes=[
             pltpu.VMEM((2, 3, 128, 128), f32), pltpu.VMEM((2, 3, 128, 128), f32),
+            pltpu.VMEM(block_owner.shape, jnp.int32), pltpu.SMEM((1, 128), jnp.int32),
         ]
-        + [pltpu.VMEM(array.shape, array.dtype) for array in arrays]
-        + [pltpu.SemaphoreType.DMA((6,))],
+        + [pltpu.VMEM(array.shape, array.dtype) for array in arrays[1:]]
+        + [pltpu.SemaphoreType.DMA((8,))],
         compiler_params=pltpu.CompilerParams(vmem_limit_bytes=EDGE_VMEM),
         name="edge",
-    )(*arrays)
+    )(device, *arrays)
     squares = count // 16
     same_place = [[16 * s + i for s in range(squares)] for i in range(16)]
     same_square = [[16 * s + i for i in range(16)] for s in range(squares)]
-    tops = lax.all_to_all(
-        top[: 8 * squares], axes, 0, 0, axis_index_groups=same_place, tiled=True
-    )
-    ahead = lax.ppermute(left, axes, [(b, (b - 16) % count) for b in range(count)])
-    behind = lax.ppermute(right, axes, [(b, (b + 16) % count) for b in range(count)])
-    send, table = pl.pallas_call(
-        functools.partial(fill_kernel, cols_b),
-        in_specs=[small] + [held] * 2,
-        out_specs=[held] * 2,
-        out_shape=[shape((16, 2, 56, 128), f32), shape((1, 128), jnp.int32)],
-        scratch_shapes=[pltpu.SMEM((1, 128), jnp.int32), pltpu.SemaphoreType.DMA(())],
-        compiler_params=pltpu.CompilerParams(vmem_limit_bytes=FILL_VMEM),
-        cost_estimate=pl.CostEstimate(flops=0, bytes_accessed=2_000_000, transcendentals=0),
-        name="fill",
-    )(device, block_owner, lines)
-    send = pl.pallas_call(
-        pack_kernel,
-        in_specs=[small] + [held] * 3 + [far],
-        out_specs=far,
-        out_shape=shape((16, 2, 56, 128), f32),
-        input_output_aliases={4: 0},
-        scratch_shapes=[pltpu.VMEM((16, 56, 128), f32), pltpu.SemaphoreType.DMA(())],
-        compiler_params=pltpu.CompilerParams(vmem_limit_bytes=PACK_VMEM),
-        name="pack",
-    )(table, ahead, behind, tops, send)
     received = lax.all_to_all(
         send.reshape(16, 112, 128), axes, 0, 0, axis_index_groups=same_square, tiled=True
     ).reshape(32, 56, 128)
@@ -735,9 +720,28 @@
         ),
         name="block",
     )(velocity, thickness, coriolis, elem_mass, along_x, tiles, send.reshape(32, 56, 128))
+    to_ahead, to_behind, top = pl.pallas_call(
+        pack_kernel,
+        grid=(1,),
+        in_specs=[
+            whole((1, 128), pltpu.SMEM), whole((32, 56, 128)),
+            pl.BlockSpec((1, 8, 128), lambda step: (0, 0, 0)),
+        ],
+        out_specs=[
+            whole((72, 128)), whole((72, 128)), whole((squares * TOP_ROWS, 128)),
+        ],
+        out_shape=[
+            shape((72, 128), f32), shape((72, 128), f32), shape((squares * TOP_ROWS, 128), f32),
+        ],
+        compiler_params=pltpu.CompilerParams(vmem_limit_bytes=PACK_VMEM),
+        name="pack",
+    )(table, received, partial)
+    tops = lax.all_to_all(top, axes, 0, 0, axis_index_groups=same_place, tiled=True)
+    ahead = lax.ppermute(to_behind, axes, [(b, (b - 16) % count) for b in range(count)])
+    behind = lax.ppermute(to_ahead, axes, [(b, (b + 16) % count) for b in range(count)])
     new_velocity, new_thickness = pl.pallas_call(
         last_kernel,
-        in_specs=[small] + [held] * 4 + [far] * 3,
+        in_specs=[small] + [held] * 7 + [far] * 3,
         out_specs=[far] * 2,
         out_shape=[shape((2, 8, 128, 128), f32), shape((8, 128, 128), f32)],
         scratch_shapes=[
@@ -747,7 +751,7 @@
         ],
         compiler_params=pltpu.CompilerParams(vmem_limit_bytes=LAST_VMEM),
         name="last",
-    )(table, lines, received, tiles, widen, velocity, thickness, partial)
+    )(table, lines, received, ahead, behind, tops, tiles, widen, velocity, thickness, partial)
     return new_velocity[:, :, None], new_thickness[:, None]
 
 

time: 66.2 us -> 64.6 us (0.976)
  waiting for transfers between devices: 8.88 us -> 11.5 us
  starting transfers between devices: 33.8 us -> 31.7 us
  Pallas kernels: 21.3 us -> 19.8 us
  local copies, waits for them, and re-layouts: 0.93 us -> 0.02 us
    all_to_all x1, starting transfers between devices: 16.5 us -> 12 us  [per_device(): lax.all_to_all(top, axes, 0, 0, axis_index_groups=same_place, tiled=True)]
    ppermute x2, waiting for transfers between devices: 4.76 us -> 7.28 us  [the longest x1 7.28 us: per_device(): lax.ppermute(to_ahead, axes, [(b, (b + 16) % count) for b in range(count)])]
    all_to_all x1, starting transfers between devices: 7.91 us -> 10.3 us  [per_device(): lax.all_to_all(send.reshape(16, 112, 128), axes, 0, 0, axis_index_groups=...]
    pallas_call x4 -> x3, Pallas kernels: 11.5 us -> 9.99 us  [the longest x1 5.01 us: per_device(): pl.pallas_call(functools.partial(edge_kernel, cols_b), in_specs=[small] +...]
    unnamed x12 -> x10, local copies, waits for them, and re-layouts: 0.93 us -> 0.02 us
  transfers between devices with their start and end apart: 4 -> 4, of which waited for: 2 -> 2; matrix products, arithmetic and copies ran while one was open for 0% -> 0% of each run, Pallas kernels for 18% -> 15%
where the time goes in v4:
time: 64.6 us; the launch traced here: 63.8 us
  starting transfers between devices  31.7 us (49%)
  Pallas kernels  19.8 us (31%)
  waiting for transfers between devices  11.5 us (18%)
  between operations  0.72 us (1%)
    all_to_all x1, starting transfers between devices, per_device(): lax.all_to_all(top, axes, 0, 0, axis_index_groups=same_place, tiled=True)  12 us
    all_to_all x1, starting transfers between devices, per_device(): lax.all_to_all(send.reshape(16, 112, 128), axes, 0, 0, axis_index_groups=...  10.3 us
    pallas_call x1, Pallas kernels, per_device(): pl.pallas_call(block_kernel, grid=(9,), in_specs=[pair, single, whole((1,...  9.78 us
    ppermute x1, starting transfers between devices, per_device(): lax.ppermute(to_behind, axes, [(b, (b - 16) % count) for b in range(count)])  7.45 us
    ppermute x1, waiting for transfers between devices, per_device(): lax.ppermute(to_ahead, axes, [(b, (b + 16) % count) for b in range(count)])  7.28 us
    pallas_call x1, Pallas kernels, per_device(): pl.pallas_call(functools.partial(edge_kernel, cols_b), in_specs=[small] +...  5.01 us
    all_to_all x1, waiting for transfers between devices, per_device(): lax.all_to_all(send.reshape(16, 112, 128), axes, 0, 0, axis_index_groups=...  4.25 us
    pallas_call x1, Pallas kernels, per_device(): pl.pallas_call(last_kernel, in_specs=[small] + [held] * 7 + [far] * 3, ou...  3.49 us
  transfers between devices with their start and end apart: 4, of which 2 were waited for; matrix products, arithmetic and copies ran while one was open for 0% of the time, Pallas kernels for 15%

profile of v4, /device:TPU:1, one launch (start us, length us, event | category | flops | bytes accessed | tf_op | source)
XLA Modules:
  0.0 63.8 jit_solution(14800865673715509349)
XLA Ops:
  0.6 5.0 %edge.1 = (f32[256,128]{1,0:T(8,128)}, f32[16,2,56,128]{3,2,1,0:T(8,128)}, s32[1,128]{1,0:T(1,128)}) custom-call(s32[1]{0:T(128)} %bitcast.device_ref, s32[4,128]{1,0:T(4,128)} %owner_far.1, f32[2,8,128,128]{3,2,1,0:T(8,128)} %bitcast.20, f32[8,128,128]{2,1,0:T(8,128)} %bitcast.16, f32[1,128,128]{2,1,0:T(8,128)} %coriolis_ref.1, f32[1,32,32]{2,1,0:T(8,128)} %elem_mass_ref.1, ...), custom_call_target="tpu_custom_call" | custom-call | tf_op jit(solution)/shard_map/edge/pallas_call | solution.py:683
  5.7 10.3 %all-to-all-start = ((f32[16,112,128]{2,1,0:T(8,128)}), f32[16,112,128]{2,1,0:T(8,128)S(1)}, u32[]{:S(2)}, u32[]{:S(2)}) async-start(f32[16,112,128]{2,1,0:T(8,128)} %bitcast.23), calls=%async_computation | async-start | bytes 1835008 | tf_op jit(solution)/shard_map/all_to_all | solution.py:702
  16.0 0.0 copy-start.4
  16.0 9.8 %block.1.after_ref.partial_far = f32[27,128,128]{2,1,0:T(8,128)} custom-call(f32[2,8,128,128]{3,2,1,0:T(8,128)} %bitcast.21, f32[8,128,128]{2,1,0:T(8,128)} %bitcast.17, f32[1,128,128]{2,1,0:T(8,128)} %coriolis_ref.1, f32[1,32,32]{2,1,0:T(8,128)} %elem_mass_ref.1, bf16[2,384,128]{2,1,0:T(8,128)(2,1)} %constant.28.along_x_far.along_x_ref, ...), custom_call_target="tpu_custom_call" | custom-call | flops 2000000000 | bytes 3200000 | tf_op jit(solution)/shard_map/block/pallas_call | solution.py:707
  25.8 0.0 copy-start
  25.8 0.0 copy-start.1
  25.8 0.0 copy-start.2
  25.8 0.0 copy-start.3
  25.8 4.2 %all-to-all-done = f32[16,112,128]{2,1,0:T(8,128)S(1)} async-done(((f32[16,112,128]{2,1,0:T(8,128)}), f32[16,112,128]{2,1,0:T(8,128)S(1)}, u32[]{:S(2)}, u32[]{:S(2)}) %all-to-all-start) | async-done | bytes 917536 | tf_op jit(solution)/shard_map/all_to_all | solution.py:702
  30.1 0.0 copy-done.4
  30.1 1.5 %pack.1 = (f32[72,128]{1,0:T(8,128)S(1)}, f32[72,128]{1,0:T(8,128)S(1)}, f32[256,128]{1,0:T(8,128)}) custom-call(s32[1,128]{1,0:T(1,128)S(1)} %copy-done.4, f32[32,56,128]{2,1,0:T(8,128)S(1)} %bitcast.14, f32[27,128,128]{2,1,0:T(8,128)} %block.1.after_ref.partial_far), custom_call_target="tpu_custom_call" | custom-call | tf_op jit(solution)/shard_map/pack/pallas_call | solution.py:723
  31.5 12.0 %all-to-all-start.1 = ((f32[32,8,128]{2,1,0:T(8,128)}), f32[32,8,128]{2,1,0:T(8,128)S(1)}, u32[]{:S(2)}, u32[]{:S(2)}) async-start(f32[32,8,128]{2,1,0:T(8,128)} %bitcast.6), calls=%async_computation.1 | async-start | bytes 262144 | tf_op jit(solution)/shard_map/all_to_all | solution.py:739
  43.6 7.5 %collective-permute-start = (f32[72,128]{1,0:T(8,128)S(1)}, f32[72,128]{1,0:T(8,128)S(1)}, u32[]{:S(2)}, u32[]{:S(2)}) collective-permute-start(f32[72,128]{1,0:T(8,128)S(1)} %get-tuple-element.13), channel_id=1, source_target_pairs={{0,496},{1,497},{2,498},{3,499},{4,500},{5,501},{6,502},{7,503},{8... | collective-permute-start | bytes 110600 | tf_op jit(solution)/shard_map/ppermute | solution.py:740
  51.0 1.9 %collective-permute-start.1 = (f32[72,128]{1,0:T(8,128)S(1)}, f32[72,128]{1,0:T(8,128)S(1)}, u32[]{:S(2)}, u32[]{:S(2)}) collective-permute-start(f32[72,128]{1,0:T(8,128)S(1)} %get-tuple-element.14), channel_id=1, source_target_pairs={{0,16},{1,17},{2,18},{3,19},{4,20},{5,21},{6,22},{7,23},{8,24},{9,... | collective-permute-start | bytes 110600 | tf_op jit(solution)/shard_map/ppermute | solution.py:741
  53.0 0.0 collective-permute-done.ahead_ref
  53.0 7.3 %collective-permute-done.1.behind_ref = f32[72,128]{1,0:T(8,128)S(1)} collective-permute-done((f32[72,128]{1,0:T(8,128)S(1)}, f32[72,128]{1,0:T(8,128)S(1)}, u32[]{:S(2)}, u32[]{:S(2)}) %collective-permute-start.1) | collective-permute-done | bytes 36896 | tf_op jit(solution)/shard_map/ppermute | solution.py:741
  60.3 0.0 all-to-all-done.1
  60.3 0.0 copy-done
  60.3 0.0 copy-done.1
  60.3 0.0 copy-done.2
  60.3 0.0 copy-done.3
  60.3 3.5 %last.1 = (f32[2,8,128,128]{3,2,1,0:T(8,128)}, f32[8,128,128]{2,1,0:T(8,128)}) custom-call(s32[1,128]{1,0:T(1,128)S(1)} %copy-done.4, f32[256,128]{1,0:T(8,128)S(1)} %copy-done.3, f32[32,56,128]{2,1,0:T(8,128)S(1)} %bitcast.15, f32[72,128]{1,0:T(8,128)S(1)} %collective-permute-done.ahead_ref, f32[72,128]{1,0:T(8,128)S(1)} %collective-permute-done.1.behind_ref, ...), custom_call_target="tpu_custom_call" | custom-call | tf_op jit(solution)/shard_map/last/pallas_call | solution.py:742
Async XLA Ops:
  5.7 24.4 %all-to-all-start = ((f32[16,112,128]{2,1,0:T(8,128)}), f32[16,112,128]{2,1,0:T(8,128)S(1)}, u32[]{:S(2)}, u32[]{:S(2)}) async-start(f32[16,112,128]{2,1,0:T(8,128)} %bitcast.23), calls=%async_computation | async-start | bytes 1835008 | tf_op jit(solution)/shard_map/all_to_all | solution.py:702
  16.0 14.1 %copy-start.4 = (s32[1,128]{1,0:T(1,128)S(1)}, s32[1,128]{1,0:T(1,128)}, u32[]{:S(2)}) copy-start(s32[1,128]{1,0:T(1,128)} %get-tuple-element.10.table_ref) | copy-start | bytes 1540
  25.8 34.5 %copy-start = (f32[8,1,128,128]{3,2,1,0:T(8,128)S(1)}, f32[8,1,128,128]{3,2,1,0:T(8,128)}, u32[]{:S(2)}) copy-start(f32[8,1,128,128]{3,2,1,0:T(8,128)} %param.11) | copy-start | bytes 1572868
  25.8 34.5 %copy-start.1 = (f32[45,8,128]{2,1,0:T(8,128)S(1)}, f32[45,8,128]{2,1,0:T(8,128)}, u32[]{:S(2)}) copy-start(f32[45,8,128]{2,1,0:T(8,128)} %constant.19.clone.tiles_far.tiles_ref) | copy-start | bytes 552964
  25.8 34.5 %copy-start.2 = (bf16[384,256]{1,0:T(8,128)(2,1)S(1)}, bf16[384,256]{1,0:T(8,128)(2,1)}, u32[]{:S(2)}) copy-start(bf16[384,256]{1,0:T(8,128)(2,1)} %constant.33.widen_ref) | copy-start | bytes 589828
  25.8 34.5 %copy-start.3 = (f32[256,128]{1,0:T(8,128)S(1)}, f32[256,128]{1,0:T(8,128)}, u32[]{:S(2)}) copy-start(f32[256,128]{1,0:T(8,128)} %get-tuple-element.11.lines_ref) | copy-start | bytes 393220
  31.5 28.7 %all-to-all-start.1 = ((f32[32,8,128]{2,1,0:T(8,128)}), f32[32,8,128]{2,1,0:T(8,128)S(1)}, u32[]{:S(2)}, u32[]{:S(2)}) async-start(f32[32,8,128]{2,1,0:T(8,128)} %bitcast.6), calls=%async_computation.1 | async-start | bytes 262144 | tf_op jit(solution)/shard_map/all_to_all | solution.py:739
  43.6 9.4 %collective-permute-start = (f32[72,128]{1,0:T(8,128)S(1)}, f32[72,128]{1,0:T(8,128)S(1)}, u32[]{:S(2)}, u32[]{:S(2)}) collective-permute-start(f32[72,128]{1,0:T(8,128)S(1)} %get-tuple-element.13), channel_id=1, source_target_pairs={{0,496},{1,497},{2,498},{3,499},{4,500},{5,501},{6,502},{7,503},{8... | collective-permute-start | bytes 110600 | tf_op jit(solution)/shard_map/ppermute | solution.py:740
  51.0 9.2 %collective-permute-start.1 = (f32[72,128]{1,0:T(8,128)S(1)}, f32[72,128]{1,0:T(8,128)S(1)}, u32[]{:S(2)}, u32[]{:S(2)}) collective-permute-start(f32[72,128]{1,0:T(8,128)S(1)} %get-tuple-element.14), channel_id=1, source_target_pairs={{0,16},{1,17},{2,18},{3,19},{4,20},{5,21},{6,22},{7,23},{8,24},{9,... | collective-permute-start | bytes 110600 | tf_op jit(solution)/shard_map/ppermute | solution.py:741

commit v5 on v4

--- a/solution.py
+++ b/solution.py
@@ -181,17 +181,22 @@
     row = lax.broadcasted_iota(jnp.int32, (8, 128), 0)
     wide = jnp.broadcast_to(line, (8, 128))
     folded = jnp.zeros((8, 128), f32)
-    for part in range(4):
-        folded = jnp.where((row == part) & (lane // 32 == 2), turn(wide, 64 - 32 * part), folded)
+    for part in range(8):
+        folded = jnp.where((row == part) & (lane // 16 == 3), turn(wide, 48 - 16 * part), folded)
     return folded
 
 
 def unfold_line(tile):
-    lane = lane_index(1)
-    line = jnp.zeros((1, 128), f32)
-    for part in range(4):
-        line = jnp.where(lane // 32 == part, turn(tile[part : part + 1], 32 * part - 64), line)
-    return line
+    lane = lane_index(8)
+    row = lax.broadcasted_iota(jnp.int32, (8, 128), 0)
+    moved = pltpu.roll(turn(tile, -48), 0, 1, stride=16, stride_axis=0)
+    return jnp.sum(jnp.where(lane // 16 == row, moved, 0.0), axis=0, keepdims=True)
+
+
+def top_lanes():
+    lane = lane_index(8)
+    row = lax.broadcasted_iota(jnp.int32, (8, 128), 0)
+    return (row == 7) & (lane >= 24) & (lane < 48)
 
 
 def mass_of_nodes(elem_mass, tiles_ref):
@@ -260,7 +265,7 @@
         found = found + jnp.where((near_row == row) & (near_col == lane), line, 0.0)
     found = jnp.sum(found, axis=1, keepdims=True).astype(jnp.int32)
     there = (near_row >= 0) & (near_row < 4)
-    slot = 2 * (found % 16)
+    slot = found % 16
     kind = jnp.where(there, jnp.where(found // 16 == square, 1, 2), 0)
     ahead_of = jnp.where(way == 0, sources[0], 0)
     for number in range(1, 6):
@@ -416,16 +421,18 @@
             tile = tile + turn(pack_end(lines[along][24:48], sideways), 48)
             targets[across][56 + 8 * number : 64 + 8 * number, :] = tile
     table_copy.wait()
-    after = lane_index(8) >= 96
+    starts = [
+        [pl.multiple_of(jnp.maximum(near_ref[0, 16 * part + place], 0), 8) for part in range(2)]
+        for place in range(16)
+    ]
     for place in range(16):
         for part in range(2):
-            start = near_ref[0, 16 * part + place]
-
-            @pl.when(start >= 0)
-            def _(place=place, part=part, start=start):
-                send_ref[place, part] = lines_ref[pl.ds(pl.multiple_of(start, 8), 56), :]
-
-        send_ref[place, 0, 48:56, :] = jnp.where(after, top, send_ref[place, 0, 48:56, :])
+            rows = pl.ds(starts[place][part], 48)
+            send_ref[place, 48 * part : 48 * part + 48, :] = lines_ref[rows, :]
+    for place in range(16):
+        tiles = [lines_ref[pl.ds(starts[place][part] + 48, 8), :] for part in range(2)]
+        tile = jnp.where(lane_index(8) < 64, tiles[0], turn(tiles[1], 64))
+        send_ref[place, 96:104, :] = jnp.where(top_lanes(), top, tile)
 
 
 def block_kernel(
@@ -460,13 +467,14 @@
 def pack_kernel(table_ref, received_ref, after_ref, ahead_ref, behind_ref, top_ref):
     top = jnp.zeros((8, 128), f32)
     for place in range(16):
-        top = jnp.maximum(top, received_ref[2 * place, 48:56, :])
-    top = jnp.max(jnp.where(lane_index(8) >= 96, top, 0.0), axis=(0, 1), keepdims=True)
+        top = jnp.maximum(top, received_ref[place, 96:104, :])
+    top = jnp.max(jnp.where(top_lanes(), top, 0.0), axis=(0, 1), keepdims=True)
     top_ref[...] = jnp.broadcast_to(top, top_ref.shape)
     for base, ref in ((48, ahead_ref), (51, behind_ref)):
-        ref[0:56, :] = received_ref[2 * table_ref[0, base] + 1]
-        ref[56:64, :] = received_ref[2 * table_ref[0, base + 1] + 1, 48:56, :]
-        ref[64:72, :] = received_ref[2 * table_ref[0, base + 2] + 1, 48:56, :]
+        ref[0:48, :] = received_ref[table_ref[0, base], 48:96, :]
+        for number in range(3):
+            tile = received_ref[table_ref[0, base + number], 96:104, :]
+            ref[48 + 8 * number : 56 + 8 * number, :] = turn(tile, 64)
 
 
 def edge_terms(table_ref, lines, received_ref, ahead_ref, behind_ref, tiles_ref):
@@ -474,7 +482,8 @@
 
     def message(way, start, stop):
         kind = table_ref[0, 40 + way]
-        values = received_ref[table_ref[0, 32 + way], start:stop, :]
+        skip = 48 if start == 48 else 0
+        values = received_ref[table_ref[0, 32 + way], start + skip : stop + skip, :]
         step_y, step_x = steps8[way]
         if step_x != 0:
             crossed = ahead_ref if step_x > 0 else behind_ref
@@ -532,7 +541,7 @@
 
     def arm(beside, diagonal, coefs):
         both = beside + diagonal
-        weight = turn(both, -24)
+        weight = jnp.broadcast_to(turn(both, -24)[0:1], (8, 128))
         value = jnp.where(weight > 0.0, both / jnp.where(weight > 0.0, weight, 1.0), 0.0) * coefs
         value = value + turn(value, -1)
         return value + turn(value, -2)
@@ -685,7 +694,7 @@
         in_specs=[small] + [far] * 7,
         out_specs=[held] * 3,
         out_shape=[
-            shape((256, 128), f32), shape((16, 2, 56, 128), f32), shape((1, 128), jnp.int32),
+            shape((256, 128), f32), shape((16, 104, 128), f32), shape((1, 128), jnp.int32),
         ],
         scratch_shapes=[
             pltpu.VMEM((2, 3, 128, 128), f32), pltpu.VMEM((2, 3, 128, 128), f32),
@@ -700,8 +709,8 @@
     same_place = [[16 * s + i for s in range(squares)] for i in range(16)]
     same_square = [[16 * s + i for i in range(16)] for s in range(squares)]
     received = lax.all_to_all(
-        send.reshape(16, 112, 128), axes, 0, 0, axis_index_groups=same_square, tiled=True
-    ).reshape(32, 56, 128)
+        send, axes, 0, 0, axis_index_groups=same_square, tiled=True
+    )
     pair = pl.BlockSpec((2, 1, 128, 128), lambda step: (0, jnp.minimum(step, 7), 0, 0))
     single = pl.BlockSpec((1, 128, 128), lambda step: (jnp.minimum(step, 7), 0, 0))
     partial = pl.pallas_call(
@@ -719,12 +728,12 @@
             flops=2_000_000_000, bytes_accessed=3_200_000, transcendentals=0
         ),
         name="block",
-    )(velocity, thickness, coriolis, elem_mass, along_x, tiles, send.reshape(32, 56, 128))
+    )(velocity, thickness, coriolis, elem_mass, along_x, tiles, send)
     to_ahead, to_behind, top = pl.pallas_call(
         pack_kernel,
         grid=(1,),
         in_specs=[
-            whole((1, 128), pltpu.SMEM), whole((32, 56, 128)),
+            whole((1, 128), pltpu.SMEM), whole((16, 104, 128)),
             pl.BlockSpec((1, 8, 128), lambda step: (0, 0, 0)),
         ],
         out_specs=[

time: 64.6 us -> 63.7 us (0.986)
  waiting for transfers between devices: 11.5 us -> 10.8 us
  transfers between devices with their start and end apart: 4 -> 4, of which waited for: 2 -> 2; matrix products, arithmetic and copies ran while one was open for 0% -> 0% of each run, Pallas kernels for 15% -> 16%
where the time goes in v5:
time: 63.7 us; the launch traced here: 62.9 us
  starting transfers between devices  31.7 us (50%)
  Pallas kernels  19.6 us (31%)
  waiting for transfers between devices  10.8 us (17%)
  between operations  0.72 us (1%)
    all_to_all x1, starting transfers between devices, per_device(): lax.all_to_all(top, axes, 0, 0, axis_index_groups=same_place, tiled=True)  12.1 us
    all_to_all x1, starting transfers between devices, per_device(): lax.all_to_all(send, axes, 0, 0, axis_index_groups=same_square, tiled=True)  10.3 us
    pallas_call x1, Pallas kernels, per_device(): pl.pallas_call(block_kernel, grid=(9,), in_specs=[pair, single, whole((1,...  9.77 us
    ppermute x1, starting transfers between devices, per_device(): lax.ppermute(to_behind, axes, [(b, (b - 16) % count) for b in range(count)])  7.45 us
    ppermute x1, waiting for transfers between devices, per_device(): lax.ppermute(to_ahead, axes, [(b, (b + 16) % count) for b in range(count)])  7.17 us
    pallas_call x1, Pallas kernels, per_device(): pl.pallas_call(functools.partial(edge_kernel, cols_b), in_specs=[small] +...  4.85 us
    all_to_all x1, waiting for transfers between devices, per_device(): lax.all_to_all(send, axes, 0, 0, axis_index_groups=same_square, tiled=True)  3.65 us
    pallas_call x1, Pallas kernels, per_device(): pl.pallas_call(last_kernel, in_specs=[small] + [held] * 7 + [far] * 3, ou...  3.49 us
  transfers between devices with their start and end apart: 4, of which 2 were waited for; matrix products, arithmetic and copies ran while one was open for 0% of the time, Pallas kernels for 16%

profile of v5, /device:TPU:1, one launch (start us, length us, event | category | flops | bytes accessed | tf_op | source)
XLA Modules:
  0.0 62.9 jit_solution(5465871678588811830)
XLA Ops:
  0.6 4.8 %edge.1 = (f32[256,128]{1,0:T(8,128)}, f32[16,104,128]{2,1,0:T(8,128)}, s32[1,128]{1,0:T(1,128)}) custom-call(s32[1]{0:T(128)} %bitcast.device_ref, s32[4,128]{1,0:T(4,128)} %owner_far.1, f32[2,8,128,128]{3,2,1,0:T(8,128)} %bitcast.15, f32[8,128,128]{2,1,0:T(8,128)} %bitcast.11, f32[1,128,128]{2,1,0:T(8,128)} %coriolis_ref.1, f32[1,32,32]{2,1,0:T(8,128)} %elem_mass_ref.1, ...), custom_call_target="tpu_custom_call" | custom-call | tf_op jit(solution)/shard_map/edge/pallas_call | solution.py:692
  5.5 10.3 %all-to-all-start = ((f32[16,104,128]{2,1,0:T(8,128)}), f32[16,104,128]{2,1,0:T(8,128)S(1)}, u32[]{:S(2)}, u32[]{:S(2)}) async-start(f32[16,104,128]{2,1,0:T(8,128)} %get-tuple-element.12.after_ref), calls=%async_computation | async-start | bytes 1703936 | tf_op jit(solution)/shard_map/all_to_all | solution.py:711
  15.8 0.0 copy-start.4
  15.8 9.8 %block.1.after_ref.partial_far = f32[27,128,128]{2,1,0:T(8,128)} custom-call(f32[2,8,128,128]{3,2,1,0:T(8,128)} %bitcast.16, f32[8,128,128]{2,1,0:T(8,128)} %bitcast.12, f32[1,128,128]{2,1,0:T(8,128)} %coriolis_ref.1, f32[1,32,32]{2,1,0:T(8,128)} %elem_mass_ref.1, bf16[2,384,128]{2,1,0:T(8,128)(2,1)} %constant.28.along_x_far.along_x_ref, ...), custom_call_target="tpu_custom_call" | custom-call | flops 2000000000 | bytes 3200000 | tf_op jit(solution)/shard_map/block/pallas_call | solution.py:716
  25.6 0.0 copy-start
  25.6 0.0 copy-start.1
  25.6 0.0 copy-start.2
  25.6 0.0 copy-start.3
  25.6 3.7 %all-to-all-done.received_ref = f32[16,104,128]{2,1,0:T(8,128)S(1)} async-done(((f32[16,104,128]{2,1,0:T(8,128)}), f32[16,104,128]{2,1,0:T(8,128)S(1)}, u32[]{:S(2)}, u32[]{:S(2)}) %all-to-all-start) | async-done | bytes 852000 | tf_op jit(solution)/shard_map/all_to_all | solution.py:711
  29.3 0.0 copy-done.4
  29.3 1.5 %pack.1 = (f32[72,128]{1,0:T(8,128)S(1)}, f32[72,128]{1,0:T(8,128)S(1)}, f32[256,128]{1,0:T(8,128)}) custom-call(s32[1,128]{1,0:T(1,128)S(1)} %copy-done.4, f32[16,104,128]{2,1,0:T(8,128)S(1)} %all-to-all-done.received_ref, f32[27,128,128]{2,1,0:T(8,128)} %block.1.after_ref.partial_far), custom_call_target="tpu_custom_call" | custom-call | tf_op jit(solution)/shard_map/pack/pallas_call | solution.py:732
  30.8 12.1 %all-to-all-start.1 = ((f32[32,8,128]{2,1,0:T(8,128)}), f32[32,8,128]{2,1,0:T(8,128)S(1)}, u32[]{:S(2)}, u32[]{:S(2)}) async-start(f32[32,8,128]{2,1,0:T(8,128)} %bitcast.3), calls=%async_computation.1 | async-start | bytes 262144 | tf_op jit(solution)/shard_map/all_to_all | solution.py:748
  42.8 7.5 %collective-permute-start = (f32[72,128]{1,0:T(8,128)S(1)}, f32[72,128]{1,0:T(8,128)S(1)}, u32[]{:S(2)}, u32[]{:S(2)}) collective-permute-start(f32[72,128]{1,0:T(8,128)S(1)} %get-tuple-element.13), channel_id=1, source_target_pairs={{0,496},{1,497},{2,498},{3,499},{4,500},{5,501},{6,502},{7,503},{8... | collective-permute-start | bytes 110600 | tf_op jit(solution)/shard_map/ppermute | solution.py:749
  50.3 1.9 %collective-permute-start.1 = (f32[72,128]{1,0:T(8,128)S(1)}, f32[72,128]{1,0:T(8,128)S(1)}, u32[]{:S(2)}, u32[]{:S(2)}) collective-permute-start(f32[72,128]{1,0:T(8,128)S(1)} %get-tuple-element.14), channel_id=1, source_target_pairs={{0,16},{1,17},{2,18},{3,19},{4,20},{5,21},{6,22},{7,23},{8,24},{9,... | collective-permute-start | bytes 110600 | tf_op jit(solution)/shard_map/ppermute | solution.py:750
  52.2 0.0 collective-permute-done.ahead_ref
  52.2 7.2 %collective-permute-done.1.behind_ref = f32[72,128]{1,0:T(8,128)S(1)} collective-permute-done((f32[72,128]{1,0:T(8,128)S(1)}, f32[72,128]{1,0:T(8,128)S(1)}, u32[]{:S(2)}, u32[]{:S(2)}) %collective-permute-start.1) | collective-permute-done | bytes 36896 | tf_op jit(solution)/shard_map/ppermute | solution.py:750
  59.4 0.0 all-to-all-done.1
  59.4 0.0 copy-done
  59.4 0.0 copy-done.1
  59.4 0.0 copy-done.2
  59.4 0.0 copy-done.3
  59.4 3.5 %last.1 = (f32[2,8,128,128]{3,2,1,0:T(8,128)}, f32[8,128,128]{2,1,0:T(8,128)}) custom-call(s32[1,128]{1,0:T(1,128)S(1)} %copy-done.4, f32[256,128]{1,0:T(8,128)S(1)} %copy-done.3, f32[16,104,128]{2,1,0:T(8,128)S(1)} %all-to-all-done.received_ref, f32[72,128]{1,0:T(8,128)S(1)} %collective-permute-done.ahead_ref, ...), custom_call_target="tpu_custom_call" | custom-call | tf_op jit(solution)/shard_map/last/pallas_call | solution.py:751
Async XLA Ops:
  5.5 23.8 %all-to-all-start = ((f32[16,104,128]{2,1,0:T(8,128)}), f32[16,104,128]{2,1,0:T(8,128)S(1)}, u32[]{:S(2)}, u32[]{:S(2)}) async-start(f32[16,104,128]{2,1,0:T(8,128)} %get-tuple-element.12.after_ref), calls=%async_computation | async-start | bytes 1703936 | tf_op jit(solution)/shard_map/all_to_all | solution.py:711
  15.8 13.5 %copy-start.4 = (s32[1,128]{1,0:T(1,128)S(1)}, s32[1,128]{1,0:T(1,128)}, u32[]{:S(2)}) copy-start(s32[1,128]{1,0:T(1,128)} %get-tuple-element.10.table_ref) | copy-start | bytes 1540
  25.6 33.8 %copy-start = (f32[8,1,128,128]{3,2,1,0:T(8,128)S(1)}, f32[8,1,128,128]{3,2,1,0:T(8,128)}, u32[]{:S(2)}) copy-start(f32[8,1,128,128]{3,2,1,0:T(8,128)} %param.11) | copy-start | bytes 1572868
  25.6 33.8 %copy-start.1 = (f32[45,8,128]{2,1,0:T(8,128)S(1)}, f32[45,8,128]{2,1,0:T(8,128)}, u32[]{:S(2)}) copy-start(f32[45,8,128]{2,1,0:T(8,128)} %constant.19.clone.tiles_far.tiles_ref) | copy-start | bytes 552964
  25.6 33.8 %copy-start.2 = (bf16[384,256]{1,0:T(8,128)(2,1)S(1)}, bf16[384,256]{1,0:T(8,128)(2,1)}, u32[]{:S(2)}) copy-start(bf16[384,256]{1,0:T(8,128)(2,1)} %constant.33.widen_ref) | copy-start | bytes 589828
  25.6 33.8 %copy-start.3 = (f32[256,128]{1,0:T(8,128)S(1)}, f32[256,128]{1,0:T(8,128)}, u32[]{:S(2)}) copy-start(f32[256,128]{1,0:T(8,128)} %get-tuple-element.11.lines_ref) | copy-start | bytes 393220
  30.8 28.6 %all-to-all-start.1 = ((f32[32,8,128]{2,1,0:T(8,128)}), f32[32,8,128]{2,1,0:T(8,128)S(1)}, u32[]{:S(2)}, u32[]{:S(2)}) async-start(f32[32,8,128]{2,1,0:T(8,128)} %bitcast.3), calls=%async_computation.1 | async-start | bytes 262144 | tf_op jit(solution)/shard_map/all_to_all | solution.py:748
  42.8 9.4 %collective-permute-start = (f32[72,128]{1,0:T(8,128)S(1)}, f32[72,128]{1,0:T(8,128)S(1)}, u32[]{:S(2)}, u32[]{:S(2)}) collective-permute-start(f32[72,128]{1,0:T(8,128)S(1)} %get-tuple-element.13), channel_id=1, source_target_pairs={{0,496},{1,497},{2,498},{3,499},{4,500},{5,501},{6,502},{7,503},{8... | collective-permute-start | bytes 110600 | tf_op jit(solution)/shard_map/ppermute | solution.py:749
  50.3 9.1 %collective-permute-start.1 = (f32[72,128]{1,0:T(8,128)S(1)}, f32[72,128]{1,0:T(8,128)S(1)}, u32[]{:S(2)}, u32[]{:S(2)}) collective-permute-start(f32[72,128]{1,0:T(8,128)S(1)} %get-tuple-element.14), channel_id=1, source_target_pairs={{0,16},{1,17},{2,18},{3,19},{4,20},{5,21},{6,22},{7,23},{8,24},{9,... | collective-permute-start | bytes 110600 | tf_op jit(solution)/shard_map/ppermute | solution.py:750

commit v6 on v5

--- a/solution.py
+++ b/solution.py
@@ -11,7 +11,7 @@
 
 courant = 0.1
 hyper_coef = 0.002
-TOP_ROWS = 8
+TOP_ROWS = 3
 MIB = 1024 * 1024
 EDGE_VMEM = 60 * MIB
 PACK_VMEM = 52 * MIB

time: 63.7 us -> 63.5 us (level)
  Pallas kernels: 19.6 us -> 18.7 us
  local copies, waits for them, and re-layouts: 0.02 us -> 0.71 us
    ppermute x1, waiting for transfers between devices: 7.17 us -> 5.31 us  [per_device(): lax.ppermute(to_ahead, axes, [(b, (b + 16) % count) for b in range(count)])]
    all_to_all x1, waiting for transfers between devices: 0.01 us -> 1.83 us  [per_device(): lax.all_to_all(top, axes, 0, 0, axis_index_groups=same_place, tiled=True)]
    all_to_all x0 -> x2, local copies, waits for them, and re-layouts: none -> 0.68 us  [per_device(): lax.all_to_all(top, axes, 0, 0, axis_index_groups=same_place, tiled=True)]
    pallas_call x1, Pallas kernels: 1.48 us -> 0.83 us  [per_device(): pl.pallas_call(pack_kernel, grid=(1,), in_specs=[whole((1, 128), pltpu.SM...]
  transfers between devices with their start and end apart: 4 -> 4, of which waited for: 2 -> 3; matrix products, arithmetic and copies ran while one was open for 0% -> 0% of each run, Pallas kernels for 16% -> 16%
where the time goes in v6:
time: 63.5 us; the launch traced here: 62.7 us
  starting transfers between devices  31.7 us (50%)
  Pallas kernels  18.7 us (29%)
  waiting for transfers between devices  10.8 us (17%)
  between operations  0.74 us (1%)
  local copies, waits for them, and re-layouts  0.71 us (1%)
    all_to_all x1, starting transfers between devices, per_device(): lax.all_to_all(top, axes, 0, 0, axis_index_groups=same_place, tiled=True)  12.1 us
    all_to_all x1, starting transfers between devices, per_device(): lax.all_to_all(send, axes, 0, 0, axis_index_groups=same_square, tiled=True)  10.3 us
    pallas_call x1, Pallas kernels, per_device(): pl.pallas_call(block_kernel, grid=(9,), in_specs=[pair, single, whole((1,...  9.79 us
    ppermute x1, starting transfers between devices, per_device(): lax.ppermute(to_behind, axes, [(b, (b - 16) % count) for b in range(count)])  7.45 us
    ppermute x1, waiting for transfers between devices, per_device(): lax.ppermute(to_ahead, axes, [(b, (b + 16) % count) for b in range(count)])  5.31 us
    pallas_call x1, Pallas kernels, per_device(): pl.pallas_call(functools.partial(edge_kernel, cols_b), in_specs=[small] +...  4.85 us
    all_to_all x1, waiting for transfers between devices, per_device(): lax.all_to_all(send, axes, 0, 0, axis_index_groups=same_square, tiled=True)  3.62 us
    pallas_call x1, Pallas kernels, per_device(): pl.pallas_call(last_kernel, in_specs=[small] + [held] * 7 + [far] * 3, ou...  3.23 us
  transfers between devices with their start and end apart: 4, of which 3 were waited for; matrix products, arithmetic and copies ran while one was open for 0% of the time, Pallas kernels for 16%

profile of v6, /device:TPU:1, one launch (start us, length us, event | category | flops | bytes accessed | tf_op | source)
XLA Modules:
  0.0 62.7 jit_solution(3233468393759153082)
XLA Ops:
  0.6 4.8 %edge.1 = (f32[256,128]{1,0:T(8,128)}, f32[16,104,128]{2,1,0:T(8,128)}, s32[1,128]{1,0:T(1,128)}) custom-call(s32[1]{0:T(128)} %bitcast.device_ref, s32[4,128]{1,0:T(4,128)} %owner_far.1, f32[2,8,128,128]{3,2,1,0:T(8,128)} %bitcast.9, f32[8,128,128]{2,1,0:T(8,128)} %bitcast.12, f32[1,128,128]{2,1,0:T(8,128)} %coriolis_ref.1, f32[1,32,32]{2,1,0:T(8,128)} %elem_mass_ref.1, ...), custom_call_target="tpu_custom_call" | custom-call | tf_op jit(solution)/shard_map/edge/pallas_call | solution.py:692
  5.5 10.3 %all-to-all-start = ((f32[16,104,128]{2,1,0:T(8,128)}), f32[16,104,128]{2,1,0:T(8,128)S(1)}, u32[]{:S(2)}, u32[]{:S(2)}) async-start(f32[16,104,128]{2,1,0:T(8,128)} %get-tuple-element.12.after_ref), calls=%async_computation | async-start | bytes 1703936 | tf_op jit(solution)/shard_map/all_to_all | solution.py:711
  15.8 0.0 copy-start.5
  15.8 9.8 %block.1.after_ref.partial_far = f32[27,128,128]{2,1,0:T(8,128)} custom-call(f32[2,8,128,128]{3,2,1,0:T(8,128)} %bitcast.10, f32[8,128,128]{2,1,0:T(8,128)} %bitcast.13, f32[1,128,128]{2,1,0:T(8,128)} %coriolis_ref.1, f32[1,32,32]{2,1,0:T(8,128)} %elem_mass_ref.1, bf16[2,384,128]{2,1,0:T(8,128)(2,1)} %constant.28.along_x_far.along_x_ref, ...), custom_call_target="tpu_custom_call" | custom-call | flops 2000000000 | bytes 3200000 | tf_op jit(solution)/shard_map/block/pallas_call | solution.py:716
  25.6 0.0 copy-start
  25.6 0.0 copy-start.2
  25.6 0.0 copy-start.3
  25.6 0.0 copy-start.4
  25.7 3.6 %all-to-all-done.received_ref = f32[16,104,128]{2,1,0:T(8,128)S(1)} async-done(((f32[16,104,128]{2,1,0:T(8,128)}), f32[16,104,128]{2,1,0:T(8,128)S(1)}, u32[]{:S(2)}, u32[]{:S(2)}) %all-to-all-start) | async-done | bytes 852000 | tf_op jit(solution)/shard_map/all_to_all | solution.py:711
  29.3 0.0 copy-done.5
  29.3 0.8 %pack.1 = (f32[72,128]{1,0:T(8,128)S(1)}, f32[72,128]{1,0:T(8,128)S(1)}, f32[96,128]{1,0:T(8,128)S(1)}) custom-call(s32[1,128]{1,0:T(1,128)S(1)} %copy-done.5, f32[16,104,128]{2,1,0:T(8,128)S(1)} %all-to-all-done.received_ref, f32[27,128,128]{2,1,0:T(8,128)} %block.1.after_ref.partial_far), custom_call_target="tpu_custom_call" | custom-call | tf_op jit(solution)/shard_map/pack/pallas_call | solution.py:732
  30.1 0.7 %all_to_all.11 = f32[32,3,128]{2,1,0:T(4,128)} reshape(f32[96,128]{1,0:T(8,128)S(1)} %get-tuple-element.15) | data formatting | bytes 98304 | tf_op jit(solution)/shard_map/all_to_all | solution.py:748
  30.8 12.1 %all-to-all-start.1 = ((f32[32,3,128]{2,1,0:T(4,128)}), f32[32,3,128]{2,1,0:T(4,128)S(1)}, u32[]{:S(2)}, u32[]{:S(2)}) async-start(f32[32,3,128]{2,1,0:T(4,128)} %all_to_all.11), calls=%async_computation.1 | async-start | bytes 131072 | tf_op jit(solution)/shard_map/all_to_all | solution.py:748
  42.8 7.5 %collective-permute-start = (f32[72,128]{1,0:T(8,128)S(1)}, f32[72,128]{1,0:T(8,128)S(1)}, u32[]{:S(2)}, u32[]{:S(2)}) collective-permute-start(f32[72,128]{1,0:T(8,128)S(1)} %get-tuple-element.13), channel_id=1, source_target_pairs={{0,496},{1,497},{2,498},{3,499},{4,500},{5,501},{6,502},{7,503},{8... | collective-permute-start | bytes 110600 | tf_op jit(solution)/shard_map/ppermute | solution.py:749
  50.3 1.9 %collective-permute-start.1 = (f32[72,128]{1,0:T(8,128)S(1)}, f32[72,128]{1,0:T(8,128)S(1)}, u32[]{:S(2)}, u32[]{:S(2)}) collective-permute-start(f32[72,128]{1,0:T(8,128)S(1)} %get-tuple-element.14), channel_id=1, source_target_pairs={{0,16},{1,17},{2,18},{3,19},{4,20},{5,21},{6,22},{7,23},{8,24},{9,... | collective-permute-start | bytes 110600 | tf_op jit(solution)/shard_map/ppermute | solution.py:750
  52.2 1.8 %all-to-all-done.1 = f32[32,3,128]{2,1,0:T(4,128)S(1)} async-done(((f32[32,3,128]{2,1,0:T(4,128)}), f32[32,3,128]{2,1,0:T(4,128)S(1)}, u32[]{:S(2)}, u32[]{:S(2)}) %all-to-all-start.1) | async-done | bytes 49184 | tf_op jit(solution)/shard_map/all_to_all | solution.py:748
  54.1 0.0 collective-permute-done.ahead_ref
  54.1 5.3 %collective-permute-done.1.behind_ref = f32[72,128]{1,0:T(8,128)S(1)} collective-permute-done((f32[72,128]{1,0:T(8,128)S(1)}, f32[72,128]{1,0:T(8,128)S(1)}, u32[]{:S(2)}, u32[]{:S(2)}) %collective-permute-start.1) | collective-permute-done | bytes 36896 | tf_op jit(solution)/shard_map/ppermute | solution.py:750
  59.4 0.0 copy-done
  59.4 0.0 copy-done.1
  59.4 0.0 copy-done.2
  59.4 0.0 copy-done.3
  59.4 0.0 copy-done.4
  59.4 3.2 %last.1 = (f32[2,8,128,128]{3,2,1,0:T(8,128)}, f32[8,128,128]{2,1,0:T(8,128)}) custom-call(s32[1,128]{1,0:T(1,128)S(1)} %copy-done.5, f32[256,128]{1,0:T(8,128)S(1)} %copy-done.4, f32[16,104,128]{2,1,0:T(8,128)S(1)} %all-to-all-done.received_ref, f32[72,128]{1,0:T(8,128)S(1)} %collective-permute-done.ahead_ref, ...), custom_call_target="tpu_custom_call" | custom-call | tf_op jit(solution)/shard_map/last/pallas_call | solution.py:751
  (2 shorter events, 0.0 us)
Async XLA Ops:
  5.5 23.8 %all-to-all-start = ((f32[16,104,128]{2,1,0:T(8,128)}), f32[16,104,128]{2,1,0:T(8,128)S(1)}, u32[]{:S(2)}, u32[]{:S(2)}) async-start(f32[16,104,128]{2,1,0:T(8,128)} %get-tuple-element.12.after_ref), calls=%async_computation | async-start | bytes 1703936 | tf_op jit(solution)/shard_map/all_to_all | solution.py:711
  15.8 13.5 %copy-start.5 = (s32[1,128]{1,0:T(1,128)S(1)}, s32[1,128]{1,0:T(1,128)}, u32[]{:S(2)}) copy-start(s32[1,128]{1,0:T(1,128)} %get-tuple-element.10.table_ref) | copy-start | bytes 1540
  25.6 33.8 %copy-start = (f32[2,8,1,128,128]{4,3,2,1,0:T(8,128)S(1)}, f32[2,8,1,128,128]{4,3,2,1,0:T(8,128)}, u32[]{:S(2)}) copy-start(f32[2,8,1,128,128]{4,3,2,1,0:T(8,128)} %param.10) | copy-start | bytes 3145732
  25.6 33.8 %copy-start.1 = (f32[8,1,128,128]{3,2,1,0:T(8,128)S(1)}, f32[8,1,128,128]{3,2,1,0:T(8,128)}, u32[]{:S(2)}) copy-start(f32[8,1,128,128]{3,2,1,0:T(8,128)} %param.11) | copy-start | bytes 1572868
  25.6 33.8 %copy-start.2 = (f32[45,8,128]{2,1,0:T(8,128)S(1)}, f32[45,8,128]{2,1,0:T(8,128)}, u32[]{:S(2)}) copy-start(f32[45,8,128]{2,1,0:T(8,128)} %constant.19.clone.tiles_far.tiles_ref) | copy-start | bytes 552964
  25.6 33.8 %copy-start.3 = (bf16[384,256]{1,0:T(8,128)(2,1)S(1)}, bf16[384,256]{1,0:T(8,128)(2,1)}, u32[]{:S(2)}) copy-start(bf16[384,256]{1,0:T(8,128)(2,1)} %constant.33.widen_ref) | copy-start | bytes 589828
  25.6 33.8 %copy-start.4 = (f32[256,128]{1,0:T(8,128)S(1)}, f32[256,128]{1,0:T(8,128)}, u32[]{:S(2)}) copy-start(f32[256,128]{1,0:T(8,128)} %get-tuple-element.11.lines_ref) | copy-start | bytes 393220
  30.8 23.3 %all-to-all-start.1 = ((f32[32,3,128]{2,1,0:T(4,128)}), f32[32,3,128]{2,1,0:T(4,128)S(1)}, u32[]{:S(2)}, u32[]{:S(2)}) async-start(f32[32,3,128]{2,1,0:T(4,128)} %all_to_all.11), calls=%async_computation.1 | async-start | bytes 131072 | tf_op jit(solution)/shard_map/all_to_all | solution.py:748
  42.8 11.2 %collective-permute-start = (f32[72,128]{1,0:T(8,128)S(1)}, f32[72,128]{1,0:T(8,128)S(1)}, u32[]{:S(2)}, u32[]{:S(2)}) collective-permute-start(f32[72,128]{1,0:T(8,128)S(1)} %get-tuple-element.13), channel_id=1, source_target_pairs={{0,496},{1,497},{2,498},{3,499},{4,500},{5,501},{6,502},{7,503},{8... | collective-permute-start | bytes 110600 | tf_op jit(solution)/shard_map/ppermute | solution.py:749
  50.3 9.1 %collective-permute-start.1 = (f32[72,128]{1,0:T(8,128)S(1)}, f32[72,128]{1,0:T(8,128)S(1)}, u32[]{:S(2)}, u32[]{:S(2)}) collective-permute-start(f32[72,128]{1,0:T(8,128)S(1)} %get-tuple-element.14), channel_id=1, source_target_pairs={{0,16},{1,17},{2,18},{3,19},{4,20},{5,21},{6,22},{7,23},{8,24},{9,... | collective-permute-start | bytes 110600 | tf_op jit(solution)/shard_map/ppermute | solution.py:750

commit v7 on v6

--- a/solution.py
+++ b/solution.py
@@ -11,7 +11,7 @@
 
 courant = 0.1
 hyper_coef = 0.002
-TOP_ROWS = 3
+TOP_ROWS = 2
 MIB = 1024 * 1024
 EDGE_VMEM = 60 * MIB
 PACK_VMEM = 52 * MIB

time: 63.5 us -> 63.4 us (level)
  local copies, waits for them, and re-layouts: 0.71 us -> 0.03 us
    ppermute x1, waiting for transfers between devices: 5.31 us -> 7.17 us  [per_device(): lax.ppermute(to_ahead, axes, [(b, (b + 16) % count) for b in range(count)])]
    all_to_all x1, waiting for transfers between devices: 1.83 us -> 0.01 us  [per_device(): lax.all_to_all(top, axes, 0, 0, axis_index_groups=same_place, tiled=True)]
    all_to_all x2 -> x0, local copies, waits for them, and re-layouts: 0.68 us -> none  [per_device(): lax.all_to_all(top, axes, 0, 0, axis_index_groups=same_place, tiled=True)]
  transfers between devices with their start and end apart: 4 -> 4, of which waited for: 3 -> 2; matrix products, arithmetic and copies ran while one was open for 0% -> 0% of each run, Pallas kernels for 16% -> 16%
where the time goes in v7:
time: 63.4 us; the launch traced here: 62.6 us
  starting transfers between devices  31.7 us (50%)
  Pallas kernels  19.3 us (30%)
  waiting for transfers between devices  10.8 us (17%)
  between operations  0.74 us (1%)
    all_to_all x1, starting transfers between devices, per_device(): lax.all_to_all(top, axes, 0, 0, axis_index_groups=same_place, tiled=True)  12.1 us
    all_to_all x1, starting transfers between devices, per_device(): lax.all_to_all(send, axes, 0, 0, axis_index_groups=same_square, tiled=True)  10.3 us
    pallas_call x1, Pallas kernels, per_device(): pl.pallas_call(block_kernel, grid=(9,), in_specs=[pair, single, whole((1,...  9.79 us
    ppermute x1, starting transfers between devices, per_device(): lax.ppermute(to_behind, axes, [(b, (b - 16) % count) for b in range(count)])  7.45 us
    ppermute x1, waiting for transfers between devices, per_device(): lax.ppermute(to_ahead, axes, [(b, (b + 16) % count) for b in range(count)])  7.17 us
    pallas_call x1, Pallas kernels, per_device(): pl.pallas_call(functools.partial(edge_kernel, cols_b), in_specs=[small] +...  4.85 us
    all_to_all x1, waiting for transfers between devices, per_device(): lax.all_to_all(send, axes, 0, 0, axis_index_groups=same_square, tiled=True)  3.62 us
    pallas_call x1, Pallas kernels, per_device(): pl.pallas_call(last_kernel, in_specs=[small] + [held] * 7 + [far] * 3, ou...  3.23 us
  transfers between devices with their start and end apart: 4, of which 2 were waited for; matrix products, arithmetic and copies ran while one was open for 0% of the time, Pallas kernels for 16%

profile of v7, /device:TPU:1, one launch (start us, length us, event | category | flops | bytes accessed | tf_op | source)
XLA Modules:
  0.0 62.6 jit_solution(324904607083600982)
XLA Ops:
  0.6 4.8 %edge.1 = (f32[256,128]{1,0:T(8,128)}, f32[16,104,128]{2,1,0:T(8,128)}, s32[1,128]{1,0:T(1,128)}) custom-call(s32[1]{0:T(128)} %bitcast.device_ref, s32[4,128]{1,0:T(4,128)} %owner_far.1, f32[2,8,128,128]{3,2,1,0:T(8,128)} %bitcast.11, f32[8,128,128]{2,1,0:T(8,128)} %bitcast.14, f32[1,128,128]{2,1,0:T(8,128)} %coriolis_ref.1, f32[1,32,32]{2,1,0:T(8,128)} %elem_mass_ref.1, ...), custom_call_target="tpu_custom_call" | custom-call | tf_op jit(solution)/shard_map/edge/pallas_call | solution.py:692
  5.5 10.3 %all-to-all-start = ((f32[16,104,128]{2,1,0:T(8,128)}), f32[16,104,128]{2,1,0:T(8,128)S(1)}, u32[]{:S(2)}, u32[]{:S(2)}) async-start(f32[16,104,128]{2,1,0:T(8,128)} %get-tuple-element.12.after_ref), calls=%async_computation | async-start | bytes 1703936 | tf_op jit(solution)/shard_map/all_to_all | solution.py:711
  15.8 0.0 copy-start.5
  15.8 9.8 %block.1.after_ref.partial_far = f32[27,128,128]{2,1,0:T(8,128)} custom-call(f32[2,8,128,128]{3,2,1,0:T(8,128)} %bitcast.12, f32[8,128,128]{2,1,0:T(8,128)} %bitcast.15, f32[1,128,128]{2,1,0:T(8,128)} %coriolis_ref.1, f32[1,32,32]{2,1,0:T(8,128)} %elem_mass_ref.1, bf16[2,384,128]{2,1,0:T(8,128)(2,1)} %constant.28.along_x_far.along_x_ref, ...), custom_call_target="tpu_custom_call" | custom-call | flops 2000000000 | bytes 3200000 | tf_op jit(solution)/shard_map/block/pallas_call | solution.py:716
  25.6 0.0 copy-start
  25.6 0.0 copy-start.1
  25.6 0.0 copy-start.2
  25.6 0.0 copy-start.3
  25.6 0.0 copy-start.4
  25.7 3.6 %all-to-all-done.received_ref = f32[16,104,128]{2,1,0:T(8,128)S(1)} async-done(((f32[16,104,128]{2,1,0:T(8,128)}), f32[16,104,128]{2,1,0:T(8,128)S(1)}, u32[]{:S(2)}, u32[]{:S(2)}) %all-to-all-start) | async-done | bytes 852000 | tf_op jit(solution)/shard_map/all_to_all | solution.py:711
  29.3 0.0 copy-done.5
  29.3 1.4 %pack.1 = (f32[72,128]{1,0:T(8,128)S(1)}, f32[72,128]{1,0:T(8,128)S(1)}, f32[64,128]{1,0:T(8,128)}) custom-call(s32[1,128]{1,0:T(1,128)S(1)} %copy-done.5, f32[16,104,128]{2,1,0:T(8,128)S(1)} %all-to-all-done.received_ref, f32[27,128,128]{2,1,0:T(8,128)} %block.1.after_ref.partial_far), custom_call_target="tpu_custom_call" | custom-call | tf_op jit(solution)/shard_map/pack/pallas_call | solution.py:732
  30.7 12.1 %all-to-all-start.1 = ((f32[32,2,128]{2,1,0:T(2,128)}), f32[32,2,128]{2,1,0:T(2,128)S(1)}, u32[]{:S(2)}, u32[]{:S(2)}) async-start(f32[32,2,128]{2,1,0:T(2,128)} %bitcast.3), calls=%async_computation.1 | async-start | bytes 65536 | tf_op jit(solution)/shard_map/all_to_all | solution.py:748
  42.8 7.5 %collective-permute-start = (f32[72,128]{1,0:T(8,128)S(1)}, f32[72,128]{1,0:T(8,128)S(1)}, u32[]{:S(2)}, u32[]{:S(2)}) collective-permute-start(f32[72,128]{1,0:T(8,128)S(1)} %get-tuple-element.13), channel_id=1, source_target_pairs={{0,496},{1,497},{2,498},{3,499},{4,500},{5,501},{6,502},{7,503},{8... | collective-permute-start | bytes 110600 | tf_op jit(solution)/shard_map/ppermute | solution.py:749
  50.2 1.9 %collective-permute-start.1 = (f32[72,128]{1,0:T(8,128)S(1)}, f32[72,128]{1,0:T(8,128)S(1)}, u32[]{:S(2)}, u32[]{:S(2)}) collective-permute-start(f32[72,128]{1,0:T(8,128)S(1)} %get-tuple-element.14), channel_id=1, source_target_pairs={{0,16},{1,17},{2,18},{3,19},{4,20},{5,21},{6,22},{7,23},{8,24},{9,... | collective-permute-start | bytes 110600 | tf_op jit(solution)/shard_map/ppermute | solution.py:750
  52.2 0.0 collective-permute-done.ahead_ref
  52.2 7.2 %collective-permute-done.1.behind_ref = f32[72,128]{1,0:T(8,128)S(1)} collective-permute-done((f32[72,128]{1,0:T(8,128)S(1)}, f32[72,128]{1,0:T(8,128)S(1)}, u32[]{:S(2)}, u32[]{:S(2)}) %collective-permute-start.1) | collective-permute-done | bytes 36896 | tf_op jit(solution)/shard_map/ppermute | solution.py:750
  59.4 0.0 all-to-all-done.1
  59.4 0.0 copy-done
  59.4 0.0 copy-done.1
  59.4 0.0 copy-done.2
  59.4 0.0 copy-done.3
  59.4 0.0 copy-done.4
  59.4 3.2 %last.1 = (f32[2,8,128,128]{3,2,1,0:T(8,128)}, f32[8,128,128]{2,1,0:T(8,128)}) custom-call(s32[1,128]{1,0:T(1,128)S(1)} %copy-done.5, f32[256,128]{1,0:T(8,128)S(1)} %copy-done.4, f32[16,104,128]{2,1,0:T(8,128)S(1)} %all-to-all-done.received_ref, f32[72,128]{1,0:T(8,128)S(1)} %collective-permute-done.ahead_ref, ...), custom_call_target="tpu_custom_call" | custom-call | tf_op jit(solution)/shard_map/last/pallas_call | solution.py:751
Async XLA Ops:
  5.5 23.8 %all-to-all-start = ((f32[16,104,128]{2,1,0:T(8,128)}), f32[16,104,128]{2,1,0:T(8,128)S(1)}, u32[]{:S(2)}, u32[]{:S(2)}) async-start(f32[16,104,128]{2,1,0:T(8,128)} %get-tuple-element.12.after_ref), calls=%async_computation | async-start | bytes 1703936 | tf_op jit(solution)/shard_map/all_to_all | solution.py:711
  15.8 13.5 %copy-start.5 = (s32[1,128]{1,0:T(1,128)S(1)}, s32[1,128]{1,0:T(1,128)}, u32[]{:S(2)}) copy-start(s32[1,128]{1,0:T(1,128)} %get-tuple-element.10.table_ref) | copy-start | bytes 1540
  25.6 33.7 %copy-start = (f32[2,8,1,128,128]{4,3,2,1,0:T(8,128)S(1)}, f32[2,8,1,128,128]{4,3,2,1,0:T(8,128)}, u32[]{:S(2)}) copy-start(f32[2,8,1,128,128]{4,3,2,1,0:T(8,128)} %param.10) | copy-start | bytes 3145732
  25.6 33.7 %copy-start.1 = (f32[8,1,128,128]{3,2,1,0:T(8,128)S(1)}, f32[8,1,128,128]{3,2,1,0:T(8,128)}, u32[]{:S(2)}) copy-start(f32[8,1,128,128]{3,2,1,0:T(8,128)} %param.11) | copy-start | bytes 1572868
  25.6 33.7 %copy-start.2 = (f32[45,8,128]{2,1,0:T(8,128)S(1)}, f32[45,8,128]{2,1,0:T(8,128)}, u32[]{:S(2)}) copy-start(f32[45,8,128]{2,1,0:T(8,128)} %constant.19.clone.tiles_far.tiles_ref) | copy-start | bytes 552964
  25.6 33.7 %copy-start.3 = (bf16[384,256]{1,0:T(8,128)(2,1)S(1)}, bf16[384,256]{1,0:T(8,128)(2,1)}, u32[]{:S(2)}) copy-start(bf16[384,256]{1,0:T(8,128)(2,1)} %constant.33.widen_ref) | copy-start | bytes 589828
  25.6 33.7 %copy-start.4 = (f32[256,128]{1,0:T(8,128)S(1)}, f32[256,128]{1,0:T(8,128)}, u32[]{:S(2)}) copy-start(f32[256,128]{1,0:T(8,128)} %get-tuple-element.11.lines_ref) | copy-start | bytes 393220
  30.7 28.6 %all-to-all-start.1 = ((f32[32,2,128]{2,1,0:T(2,128)}), f32[32,2,128]{2,1,0:T(2,128)S(1)}, u32[]{:S(2)}, u32[]{:S(2)}) async-start(f32[32,2,128]{2,1,0:T(2,128)} %bitcast.3), calls=%async_computation.1 | async-start | bytes 65536 | tf_op jit(solution)/shard_map/all_to_all | solution.py:748
  42.8 9.4 %collective-permute-start = (f32[72,128]{1,0:T(8,128)S(1)}, f32[72,128]{1,0:T(8,128)S(1)}, u32[]{:S(2)}, u32[]{:S(2)}) collective-permute-start(f32[72,128]{1,0:T(8,128)S(1)} %get-tuple-element.13), channel_id=1, source_target_pairs={{0,496},{1,497},{2,498},{3,499},{4,500},{5,501},{6,502},{7,503},{8... | collective-permute-start | bytes 110600 | tf_op jit(solution)/shard_map/ppermute | solution.py:749
  50.2 9.1 %collective-permute-start.1 = (f32[72,128]{1,0:T(8,128)S(1)}, f32[72,128]{1,0:T(8,128)S(1)}, u32[]{:S(2)}, u32[]{:S(2)}) collective-permute-start(f32[72,128]{1,0:T(8,128)S(1)} %get-tuple-element.14), channel_id=1, source_target_pairs={{0,16},{1,17},{2,18},{3,19},{4,20},{5,21},{6,22},{7,23},{8,24},{9,... | collective-permute-start | bytes 110600 | tf_op jit(solution)/shard_map/ppermute | solution.py:750
